TPU v7x, 32 devices: a whole 2x2x4 slice. The times are simulated.
32 devices in a mesh: dp: 4 (over y, x), row: 2 (over core), col: 4 (over z).
Axes of the slice: x: 2, y: 2, z: 4, core: 2. Of those that a mesh axis runs over, the one named last changes fastest.
Arguments:
- grad_parts: bfloat16 [4, 4, 4096, 10240], P('dp', None, 'row', 'col'), may hold values from -16 to 16, as said below
- params: float32 [4, 4096, 10240], P('dp', 'row', 'col'), may hold values from -1.2 to 1.2
- row_moment: float32 [4, 4096], P('dp', 'row'), may hold values from 0.03 to 3, as said below
- col_moment: float32 [4, 10240], P('dp', 'col'), may hold values from 0.02 to 0.4
Outputs:
- new_params: float32 [4, 4096, 10240], P('dp', 'row', 'col')
- update: bfloat16 [4, 4096, 10240], P('dp', 'row', 'col')
- new_row_moment: float32 [4, 4096], P('dp', 'row')
- new_col_moment: float32 [4, 10240], P('dp', 'col')
Inputs may be any that keep to these rules, and one draw needn't show every extreme that they name: `grad_parts`: each replica's partial gradient of the projections. `row_moment`: positive second moments of the rows.
All inputs are finite; a program needn't handle non-finite values.
Results may differ from a plain program's by a relative error of at most 0.011.
Values may be sent and summed in bfloat16 or wider, within the bound.
No kernel may reach another device: no remote copies, remote signals or barrier semaphores. Data moves between devices by JAX's collectives and lax.ppermute only.
A program may use at most 256 MiB of HBM per device.

v0:
```python
import jax
import jax.numpy as jnp
from jax import lax
from jax.sharding import PartitionSpec as P

D = 4096
FF = 10240


EPSILON = 1e-30
DECAY = 0.8415106807538888
LEARN_RATE = 0.01


def on_device(grad_parts, params, row_moment, col_moment):
    partial_value = grad_parts[0]
    gradient = lax.psum_scatter(partial_value, "dp", scatter_dimension=0, tiled=True).astype(
        jnp.float32
    )
    squares = gradient * gradient + EPSILON
    row_local = jnp.sum(squares, axis=2)
    col_local = jnp.sum(squares, axis=1)
    power_local = jnp.sum(params * params, axis=(1, 2))
    row_sums = lax.psum(row_local, "col")
    col_sums = lax.psum(col_local, "row")
    param_power = lax.psum(power_local, ("row", "col"))
    new_row = DECAY * row_moment + (1.0 - DECAY) * row_sums / FF
    row_mean = lax.psum(jnp.sum(new_row, axis=1), "row") / D
    new_col = DECAY * col_moment + (1.0 - DECAY) * col_sums / D
    factor = new_row[:, :, None] * new_col[:, None, :] / row_mean[:, None, None]
    scaled = gradient * lax.rsqrt(factor)
    update_power = lax.psum(jnp.sum(scaled * scaled, axis=(1, 2)), ("row", "col"))
    update_rms = jnp.sqrt(update_power / (D * FF))
    direction = scaled / jnp.maximum(1.0, update_rms)[:, None, None]
    param_scale = jnp.sqrt(param_power / (D * FF))
    full_update = param_scale[:, None, None] * direction
    new_params = params - LEARN_RATE * full_update
    return (new_params, full_update.astype(jnp.bfloat16), new_row, new_col)


def solution(mesh):
    placed = (P("dp", None, "row", "col"), P("dp", "row", "col"), P("dp", "row"), P("dp", "col"))
    return jax.shard_map(
        on_device,
        mesh=mesh,
        in_specs=placed,
        out_specs=(P("dp", "row", "col"), P("dp", "row", "col"), P("dp", "row"), P("dp", "col")),
        check_vma=False,
    )
```

profile of v0, /device:TPU:0, one launch (start us, length us, event | category | flops | bytes accessed | tf_op | source)
XLA Modules:
  0.0 453.1 jit_solution(3864527756851730941)
XLA Ops:
  7.2 0.0 reduce-scatter.4.cloned.1.call-start
  7.2 0.7 reduce-scatter.4.cloned.1.call-update
  7.9 0.0 copy-start.2
  7.9 0.0 copy-start.1
  7.9 13.0 %multiply_reduce_fusion.1 = f32[]{:T(128)} fusion(f32[1,2048,2560]{2,1,0:T(8,128)} %param.5), kind=kLoop, calls=%fused_computation.8 | loop fusion | flops 10485759 | bytes 20971524 | tf_op jit(solution)/shard_map/reduce_sum | solution.py:23
  20.9 349.3 %reduce-scatter.4.cloned.1.call-done = bf16[1,2048,2560]{2,1,0:T(8,128)(2,1)} async-done(((bf16[4,2048,2560]{2,1,0:T(8,128)(2,1)}), bf16[1,2048,2560]{2,1,0:T(8,128)(2,1)}) %reduce-scatter.4.cloned.1.call-update) | async-done | bytes 10485776
  370.2 8.4 %fusion.1 = (f32[2560]{0:T(1024)S(1)}, f32[2048]{0:T(1024)S(1)}) fusion(bf16[1,2048,2560]{2,1,0:T(8,128)(2,1)} %reduce-scatter.4.cloned.1.call-done), kind=kLoop, calls=%fused_computation.3 | loop fusion | flops 26209792 | bytes 10504192 | tf_op jit(solution)/shard_map/reduce_sum | solution.py:22
  378.6 11.9 %psum.36 = f32[1,2048]{1,0:T(1,128)S(1)} all-reduce(f32[1,2048]{1,0:T(1,128)S(1)} %bitcast.13), channel_id=1, replica_groups=mesh['dp'=4,'row'=2,'col'=4] {'col'}, use_global_device_ids=true, to_apply=%region_4.0 | all-reduce | flops 2048 | bytes 16384 | tf_op jit(solution)/shard_map/psum | solution.py:24
  390.5 0.0 copy-done.2
  390.5 0.6 fusion.5
  391.1 0.0 copy-start
  391.1 4.4 all-reduce.2
  396.2 0.0 copy-done.1
  396.2 0.6 fusion.4
  396.9 9.2 %multiply_reduce_fusion = f32[]{:T(128)} fusion(f32[]{:T(128)} %bitcast.7, f32[2560]{0:T(1024)S(1)} %get-tuple-element.10, f32[2048]{0:T(1024)S(1)} %bitcast.11, bf16[1,2048,2560]{2,1,0:T(8,128)(2,1)} %reduce-scatter.4.cloned.1.call-done), kind=kLoop, calls=%fused_computation.7 | loop fusion | flops 31457280 | bytes 10504200 | tf_op jit(solution)/shard_map/reduce_sum | solution.py:32
  406.1 14.3 %all-reduce.1 = (f32[1]{0:T(128)}, f32[1]{0:T(128)}) all-reduce(f32[1]{0:T(128)} %bitcast.8, f32[1]{0:T(128)} %bitcast), channel_id=1, replica_groups=mesh['dp'=4,'row'=2,'col'=4] {'row','col'}, use_global_device_ids=true, to_apply=%region_10.0 | all-reduce | flops 2 | bytes 16 | tf_op jit(solution)/shard_map/psum | solution.py:32
  421.8 24.5 %fusion.3 = (bf16[1,2048,2560]{2,1,0:T(8,128)(2,1)}, f32[1,2048,2560]{2,1,0:T(8,128)}) fusion(f32[]{:T(128)} %bitcast.9, f32[]{:T(128)} %bitcast.1, f32[]{:T(128)} %bitcast.7, f32[2560]{0:T(1024)S(1)} %get-tuple-element.10, f32[2048]{0:T(1024)S(1)} %bitcast.12, bf16[1,2048,2560]{2,1,0:T(8,128)(2,1)} %reduce-scatter.4.cloned.1.call-done, f32[1,2048,2560]{2,1,0:T(8,128)} %param.5), kind=kLoop, calls=%fused_computation.9 | loop fusion | flops 47185920 | bytes 62933004 | tf_op jit(solution)/shard_map/convert_element_type | solution.py:38
  446.3 0.0 copy-done
  (1 shorter events, 0.0 us)
Async XLA Ops:
  7.2 363.0 %reduce-scatter.4.cloned.1.call-start = ((), (), s32[]{:S(2)}) async-start(), calls=%async_computation.1 | async-start | bytes 52428800
  7.9 382.6 %copy-start.2 = (f32[1,2048]{1,0:T(1,128)S(1)}, f32[1,2048]{1,0:T(1,128)}, u32[]{:S(2)}) copy-start(f32[1,2048]{1,0:T(1,128)} %param.6) | copy-start | bytes 24580
  7.9 388.3 %copy-start.1 = (f32[1,2560]{1,0:T(1,128)S(1)}, f32[1,2560]{1,0:T(1,128)}, u32[]{:S(2)}) copy-start(f32[1,2560]{1,0:T(1,128)} %param.7) | copy-start | bytes 30724
  391.1 55.2 %copy-start = (f32[1,2048]{1,0:T(1,128)}, f32[1,2048]{1,0:T(1,128)S(1)}, u32[]{:S(2)}) copy-start(f32[1,2048]{1,0:T(1,128)S(1)} %get-tuple-element.13) | copy-start | bytes 24580
Sparse Core Ops, SparseCore 0:
  11.1 359.0 reduce-scatter.3
where the time goes:
time: 453 us
  waiting for transfers between devices  350 us (77%)
  other arithmetic  56.4 us (12%)
  blocking collectives  30.6 us (7%)
  between operations  16.1 us (4%)
    unnamed x2, waiting for transfers between devices  350 us
    convert_element_type x1, other arithmetic, on_device(): return (new_params, full_update.astype(jnp.bfloat16), new_row, new_col)  24.5 us
    psum x1, blocking collectives, on_device(): lax.psum(jnp.sum(scaled * scaled, axis=(1, 2)), ('row', 'col'))  14.3 us
    reduce_sum x1, other arithmetic, on_device(): power_local = jnp.sum(params * params, axis=(1, 2))  13 us
    psum x1, blocking collectives, on_device(): row_sums = lax.psum(row_local, 'col')  11.9 us
    reduce_sum x1, other arithmetic, on_device(): jnp.sum(scaled * scaled, axis=(1, 2))  9.23 us
  transfers between devices with their start and end apart: 1, of which 1 were waited for; matrix products, arithmetic and copies ran while one was open for 3% of the time, Pallas kernels for 0%

commit v1 on v0

v1 whole, which is shorter than its diff:
```python
import jax
import jax.numpy as jnp
from jax import lax
from jax.experimental import pallas as pl
from jax.experimental.pallas import tpu as pltpu
from jax.sharding import PartitionSpec as P

D = 4096
FF = 10240
EPSILON = 1e-30
DECAY = 0.8415106807538888
LEARN_RATE = 0.01
LANES = 128
TILE = 128
GROUP = 16
MIB = 1 << 20

NEAR = (1, 2)
FAR = (2, 1)

whole_vmem = pl.BlockSpec(memory_space=pltpu.VMEM)
anywhere = pl.BlockSpec(memory_space=pl.ANY)


def pairs(n, k):
    return [(i, i ^ k) for i in range(n)]


def cost(flops, bytes_accessed):
    return pl.CostEstimate(flops=flops, bytes_accessed=bytes_accessed, transcendentals=0)


def params_of(limit):
    return pltpu.CompilerParams(vmem_limit_bytes=limit)


def pick(parts, me, wants, size):
    columns = parts.shape[2]

    def kernel(me_ref, *refs):
        n = len(refs) // 2
        for a, b in zip(refs[:n], refs[n:]):
            b[...] = a[...]

    def spec(flip, start):
        return pl.BlockSpec((None, TILE, columns), lambda t, m: (m[0] ^ flip, start // TILE + t, 0))

    return pl.pallas_call(
        kernel,
        grid_spec=pltpu.PrefetchScalarGridSpec(
            num_scalar_prefetch=1,
            grid=(size // TILE,),
            in_specs=[spec(f, s) for f, s in wants],
            out_specs=[pl.BlockSpec((TILE, columns), lambda t, m: (t, 0)) for _ in wants],
        ),
        out_shape=[jax.ShapeDtypeStruct((size, columns), parts.dtype) for _ in wants],
        compiler_params=params_of(8 * MIB),
        cost_estimate=cost(0, 4 * len(wants) * size * columns),
        name="pick",
    )(me, *[parts] * len(wants))


def merge(parts, me, got, at, offset, size):
    columns = parts.shape[2]
    half = parts.shape[1] // 2

    def kernel(me_ref, a0, a1, b0, b1, o0, o1):
        o0[...] = (a0[...].astype(jnp.float32) + b0[...].astype(jnp.float32)).astype(o0.dtype)
        o1[...] = (a1[...].astype(jnp.float32) + b1[...].astype(jnp.float32)).astype(o1.dtype)

    def own(h):
        return pl.BlockSpec((None, TILE, columns), lambda t, m: (m[0] ^ FAR[h], (h * half + at) // TILE + t, 0))

    came = pl.BlockSpec((TILE, columns), lambda t, m: ((at - offset) // TILE + t, 0))
    return pl.pallas_call(
        kernel,
        grid_spec=pltpu.PrefetchScalarGridSpec(
            num_scalar_prefetch=1,
            grid=(size // TILE,),
            in_specs=[own(0), own(1), came, came],
            out_specs=[pl.BlockSpec((TILE, columns), lambda t, m: (t, 0))] * 2,
        ),
        out_shape=[jax.ShapeDtypeStruct((size, columns), parts.dtype)] * 2,
        compiler_params=params_of(12 * MIB),
        cost_estimate=cost(2 * size * columns, 12 * size * columns),
        name="merge",
    )(me, parts, parts, *got)


def lane_sums(x):
    return jnp.sum(x.T, axis=0, keepdims=True)


def settle(parts, me, second, third, at, size, state, step):
    rows, columns = parts.shape[1:]
    half = rows // 2
    chunks = columns // LANES
    steps = size // step

    def kernel(me_ref, a0, a1, b0, b1, c0, c1, *refs):
        if state is not None:
            refs = refs[2:]
        g_ref, col_ref, row_ref, sums_ref, carry_ref = refs
        t = pl.program_id(0)

        @pl.when(t == 0)
        def _():
            if state is None:
                carry_ref[...] = jnp.zeros_like(carry_ref)
            else:
                carry_ref[...] = jnp.zeros_like(carry_ref)

        for h, (a, b, c) in enumerate(((a0, b0, c0), (a1, b1, c1))):

            def body(r, carry):
                here = pl.ds(pl.multiple_of(r * GROUP, GROUP), GROUP)
                across = jnp.zeros((GROUP, LANES), jnp.float32)
                down = []
                for k in range(chunks):
                    lanes = slice(k * LANES, (k + 1) * LANES)
                    total = a[here, lanes].astype(jnp.float32) + b[here, lanes].astype(jnp.float32)
                    total = total + c[here, lanes].astype(jnp.float32)
                    first = pl.multiple_of(h * half + at + t * step + r * GROUP, GROUP)
                    g_ref[pl.ds(first, GROUP), lanes] = total.astype(g_ref.dtype)
                    square = total * total
                    across = across + square
                    down.append(carry[k] + square[:8] + square[8:])
                sums_ref[h, pl.ds(pl.multiple_of(t * step + r * GROUP, GROUP), GROUP), :] = across
                return tuple(down)

            carry = tuple(carry_ref[:, k * LANES : (k + 1) * LANES] for k in range(chunks))
            carry = lax.fori_loop(0, step // GROUP, body, carry)
            for k in range(chunks):
                carry_ref[:, k * LANES : (k + 1) * LANES] = carry[k]

        @pl.when(t == steps - 1)
        def _():
            for h in range(2):
                for q in range(size // LANES):
                    lanes = slice(q * LANES, (q + 1) * LANES)
                    row_ref[h : h + 1, lanes] = lane_sums(sums_ref[h, lanes, :])
            col_ref[...] = jnp.sum(carry_ref[...], axis=0, keepdims=True)
            if state is not None:
                col_ref[...] = col_ref[...] + refs_in[1][...]

    refs_in = [None, None]

    def wrapped(me_ref, *refs):
        if state is not None:
            refs_in[0], refs_in[1] = refs[6], refs[7]
        kernel(me_ref, *refs)

    def own(h):
        return pl.BlockSpec((None, step, columns), lambda t, m: (m[0], (h * half + at) // step + t, 0))

    inside = pl.BlockSpec((step, columns), lambda t, m: (at // step + t, 0))
    piece = pl.BlockSpec((step, columns), lambda t, m: (t, 0))
    in_specs = [own(0), own(1), inside, inside, piece, piece]
    operands = [parts, parts, *second, *third]
    aliases = {}
    if state is not None:
        in_specs += [anywhere, whole_vmem]
        operands += state
        aliases = {7: 0}
    return pl.pallas_call(
        wrapped,
        grid_spec=pltpu.PrefetchScalarGridSpec(
            num_scalar_prefetch=1,
            grid=(steps,),
            in_specs=in_specs,
            out_specs=[whole_vmem, whole_vmem, whole_vmem],
            scratch_shapes=[pltpu.VMEM((2, size, LANES), jnp.float32), pltpu.VMEM((8, columns), jnp.float32)],
        ),
        out_shape=[
            pltpu.VMEM((rows, columns), parts.dtype),
            jax.ShapeDtypeStruct((1, columns), jnp.float32),
            jax.ShapeDtypeStruct((2, size), jnp.float32),
        ],
        input_output_aliases=aliases,
        compiler_params=params_of(16 * MIB),
        cost_estimate=cost(12 * size * columns, 12 * size * columns),
        name="settle",
    )(me, *operands)


def power_of(params):
    rows, columns = params.shape

    def kernel(p_ref, o_ref):
        @pl.when(pl.program_id(0) == 0)
        def _():
            o_ref[...] = jnp.zeros_like(o_ref)

        def body(r, total):
            here = pl.ds(pl.multiple_of(r * 8, 8), 8)
            for k in range(columns // LANES):
                p = p_ref[here, k * LANES : (k + 1) * LANES]
                total = total + p * p
            return total

        o_ref[...] += lax.fori_loop(0, TILE // 8, body, jnp.zeros((8, LANES), jnp.float32))

    return pl.pallas_call(
        kernel,
        grid=(rows // TILE,),
        in_specs=[pl.BlockSpec((TILE, columns), lambda t: (t, 0))],
        out_specs=pl.BlockSpec((8, LANES), lambda t: (0, 0)),
        out_shape=jax.ShapeDtypeStruct((8, LANES), jnp.float32),
        compiler_params=params_of(8 * MIB),
        cost_estimate=cost(2 * rows * columns, 4 * rows * columns),
        name="param_power",
    )(params)


def tree(values):
    while len(values) > 1:
        values = [a + b for a, b in zip(values[::2], values[1::2])]
    return values[0]


def weigh(gradient, col_sums, col_moment, row_sums, power):
    rows, columns = gradient.shape
    chunks = columns // LANES
    n = len(col_sums)

    def kernel(g_ref, *refs):
        sums, (moment_ref, row_ref, power_ref, new_ref, root_ref, out_ref, wide_ref, acc_ref) = refs[:n], refs[n:]
        total = tree([s[...] for s in sums]) + D * EPSILON
        new = DECAY * moment_ref[...] + (1.0 - DECAY) * total / D
        new_ref[...] = new
        root = lax.rsqrt(new)
        root_ref[...] = root
        wide_ref[...] = jnp.broadcast_to(root, wide_ref.shape)
        out_ref[:, :rows] = row_ref[...]
        out_ref[:, 2 * rows :] = jnp.sum(power_ref[...], axis=0, keepdims=True)
        roots = [wide_ref[:, k * LANES : (k + 1) * LANES] for k in range(chunks)]

        def body(r, carry):
            here = pl.ds(pl.multiple_of(r * GROUP, GROUP), GROUP)
            low = jnp.zeros((8, LANES), jnp.float32)
            high = jnp.zeros((8, LANES), jnp.float32)
            for k in range(chunks):
                g = g_ref[here, k * LANES : (k + 1) * LANES].astype(jnp.float32)
                a, b = g[:8] * roots[k], g[8:] * roots[k]
                low, high = low + a * a, high + b * b
            acc_ref[here, :] = jnp.concatenate([low, high], axis=0)
            return carry

        lax.fori_loop(0, rows // GROUP, body, 0)
        for q in range(rows // LANES):
            out_ref[:, rows + q * LANES : rows + (q + 1) * LANES] = lane_sums(acc_ref[q * LANES : (q + 1) * LANES, :])

    return pl.pallas_call(
        kernel,
        in_specs=[whole_vmem] * (n + 4),
        out_specs=[whole_vmem] * 3,
        out_shape=[
            jax.ShapeDtypeStruct((1, columns), jnp.float32),
            jax.ShapeDtypeStruct((1, columns), jnp.float32),
            jax.ShapeDtypeStruct((1, 2 * rows + LANES), jnp.float32),
        ],
        scratch_shapes=[pltpu.VMEM((8, columns), jnp.float32), pltpu.VMEM((rows, LANES), jnp.float32)],
        compiler_params=params_of(8 * MIB),
        cost_estimate=cost(4 * rows * columns, 2 * rows * columns),
        name="weigh",
    )(gradient, *col_sums, col_moment, row_sums, power)


def balance(messages, row_moment):
    rows = row_moment.shape[1]
    n = len(messages)

    def kernel(*refs):
        got, (moment_ref, new_ref, root_ref, out_ref) = refs[:n], refs[n:]
        total = tree([m[...] for m in got])
        new = DECAY * moment_ref[...] + (1.0 - DECAY) * (total[:, :rows] + FF * EPSILON) / FF
        new_ref[...] = new
        root = lax.rsqrt(new)
        root_ref[...] = root
        ratio = total[:, rows : 2 * rows] * (root * root)
        fold = lambda x: tree_lanes(x, rows)
        out_ref[...] = jnp.zeros_like(out_ref)
        out_ref[0:1, :] = fold(ratio)
        out_ref[1:2, :] = fold(new)
        out_ref[2:3, :] = total[:, 2 * rows :]

    return pl.pallas_call(
        kernel,
        in_specs=[whole_vmem] * (n + 1),
        out_specs=[whole_vmem] * 3,
        out_shape=[
            jax.ShapeDtypeStruct((1, rows), jnp.float32),
            jax.ShapeDtypeStruct((1, rows), jnp.float32),
            jax.ShapeDtypeStruct((8, LANES), jnp.float32),
        ],
        compiler_params=params_of(4 * MIB),
        name="balance",
    )(*messages, row_moment)


def tree_lanes(x, rows):
    total = x[:, :LANES]
    for q in range(1, rows // LANES):
        total = total + x[:, q * LANES : (q + 1) * LANES]
    return total


def finish(gradient, params, row_root, col_root, stats):
    rows, columns = gradient.shape
    n = len(stats)

    def kernel(g_ref, p_ref, row_ref, col_ref, *refs):
        got, (new_ref, update_ref, scale_ref) = refs[:n], refs[n:]
        t = pl.program_id(0)

        @pl.when(t == 0)
        def _():
            total = jnp.sum(tree([s[...] for s in got]), axis=1, keepdims=True)
            mean = total[1:2] / D
            rms = jnp.sqrt(mean * total[0:1] / (D * FF))
            scale = jnp.sqrt(total[2:3] / (D * FF))
            factor = scale * jnp.sqrt(mean) / jnp.maximum(1.0, rms)
            scale_ref[...] = jnp.broadcast_to(col_ref[...] * factor, scale_ref.shape)

        first = pl.multiple_of(t * TILE, TILE)
        lanes = row_ref[:, pl.ds(first, TILE)]
        wide = jnp.broadcast_to(lanes, (TILE, TILE)).T
        for r in range(TILE // GROUP):
            here = pl.ds(pl.multiple_of(first + r * GROUP, GROUP), GROUP)
            out = slice(r * GROUP, (r + 1) * GROUP)
            root = wide[out, :]
            for k in range(columns // LANES):
                at = slice(k * LANES, (k + 1) * LANES)
                g = g_ref[here, at].astype(jnp.float32)
                s = scale_ref[:, at]
                full = jnp.concatenate([g[:8] * s, g[8:] * s], axis=0) * root
                update_ref[out, at] = full.astype(update_ref.dtype)
                new_ref[out, at] = p_ref[here, at] - LEARN_RATE * full

    return pl.pallas_call(
        kernel,
        grid=(rows // TILE,),
        in_specs=[whole_vmem] * (4 + n),
        out_specs=[pl.BlockSpec((TILE, columns), lambda t: (t, 0))] * 2,
        out_shape=[jax.ShapeDtypeStruct((rows, columns), jnp.float32), jax.ShapeDtypeStruct((rows, columns), jnp.bfloat16)],
        scratch_shapes=[pltpu.VMEM((8, columns), jnp.float32)],
        compiler_params=params_of(8 * MIB),
        cost_estimate=cost(6 * rows * columns, 12 * rows * columns),
        name="finish",
    )(gradient, params, row_root, col_root, *stats)


def all_parts(value, axis, size):
    return [value] + [lax.ppermute(value, axis, pairs(size, k)) for k in range(1, size)]


def after(values, others):
    return lax.optimization_barrier((tuple(values), tuple(others)))[0]


def solution(mesh):
    across = mesh.shape["row"]
    along = mesh.shape["col"]

    def hop(values, lines):
        return [lax.ppermute(v, "dp", pairs(mesh.shape["dp"], n)) for v, n in zip(values, lines)]

    def on_device(grad_parts, params, row_moment, col_moment):
        parts = grad_parts[0]
        rows, columns = parts.shape[1:]
        half = rows // 2
        me = lax.axis_index("dp").astype(jnp.int32)[None]

        head = min(TILE, half)
        rest = half - head
        first_head = hop(pick(parts, me, [(3, 0), (3, half)], head), NEAR)
        pieces = []
        if rest:
            first_rest = hop(pick(parts, me, [(3, head), (3, half + head)], rest), NEAR)
            mine = (rest // TILE + 1) // 2 * TILE
            pieces = [(head, mine)] + ([(head + mine, rest - mine)] if rest > mine else [])
        second = hop(pick(parts, me, [(NEAR[0], 0), (NEAR[1], half)], half), NEAR)
        power = power_of(params[0])

        merged = []
        for at, size in pieces:
            got = after(first_rest, merged[-1]) if merged else first_rest
            merged.append(merge(parts, me, got, at, head, size))
        got = after(first_head, merged[-1]) if merged else first_head
        merged.append(merge(parts, me, got, 0, 0, head))
        pieces.append((0, head))
        third = [hop(m, FAR) for m in merged]

        state, row_pieces = None, {}
        for (at, size), came in zip(pieces, third):
            gradient, col_sums, row_piece = settle(parts, me, second, came, at, size, state, min(64, size))
            state = [gradient, col_sums]
            row_pieces[at] = row_piece
        row_sums = jnp.concatenate([row_pieces[at][h : h + 1] for h in range(2) for at in sorted(row_pieces)], axis=1)

        new_col, col_root, message = weigh(gradient, all_parts(col_sums, "row", across), col_moment, row_sums, power)
        new_row, row_root, stats = balance(all_parts(message, "col", along), row_moment)
        new_params, update = finish(gradient, params[0], row_root, col_root, all_parts(stats, "row", across))
        return new_params[None], update[None], new_row, new_col

    placed = (P("dp", None, "row", "col"), P("dp", "row", "col"), P("dp", "row"), P("dp", "col"))
    return jax.shard_map(
        on_device,
        mesh=mesh,
        in_specs=placed,
        out_specs=(P("dp", "row", "col"), P("dp", "row", "col"), P("dp", "row"), P("dp", "col")),
        check_vma=False,
    )
```

time: 453 us -> 394 us (0.87)
  Pallas kernels: 0 us -> 72.5 us
  waiting for transfers between devices: 350 us -> 278 us
  other arithmetic: 56.4 us -> 0.01 us
  blocking collectives: 30.6 us -> 0 us
  local copies, waits for them, and re-layouts: 0.02 us -> 22 us
  starting transfers between devices: 0.04 us -> 20.2 us
  between operations: 16.1 us -> 0.76 us
    unnamed x2 -> x0, waiting for transfers between devices: 350 us -> none
    ppermute x0 -> x17, waiting for transfers between devices: none -> 278 us  [the longest x12 272 us: hop(): lax.ppermute(v, 'dp', pairs(mesh.shape['dp'], n))]
    pallas_call x0 -> x13, Pallas kernels: none -> 72.5 us  [the longest x3 19.9 us: pick(): pl.pallas_call(kernel, grid_spec=pltpu.PrefetchScalarGridSpec(num_scalar_...]
    reduce_sum x4 -> x0, other arithmetic: 31.2 us -> none  [the longest x1 13 us: on_device(): power_local = jnp.sum(params * params, axis=(1, 2))]
    psum x3 -> x0, blocking collectives: 30.6 us -> none  [the longest x1 14.3 us: on_device(): lax.psum(jnp.sum(scaled * scaled, axis=(1, 2)), ('row', 'col'))]
    convert_element_type x1 -> x0, other arithmetic: 24.5 us -> none  [on_device(): return (new_params, full_update.astype(jnp.bfloat16), new_row, new_col)]
    unnamed x6 -> x23, local copies, waits for them, and re-layouts: 0.01 us -> 21.9 us
    ppermute x0 -> x17, starting transfers between devices: none -> 20.2 us  [the longest x12 15.8 us: hop(): lax.ppermute(v, 'dp', pairs(mesh.shape['dp'], n))]
  transfers between devices with their start and end apart: 1 -> 17, of which waited for: 1 -> 12; matrix products, arithmetic and copies ran while one was open for 3% -> 0% of each run, Pallas kernels for 0% -> 11%
where the time goes in v1:
time: 394 us
  waiting for transfers between devices  278 us (71%)
  Pallas kernels  72.5 us (18%)
  local copies, waits for them, and re-layouts  22 us (6%)
  starting transfers between devices  20.2 us (5%)
    ppermute x12, waiting for transfers between devices, hop(): lax.ppermute(v, 'dp', pairs(mesh.shape['dp'], n))  272 us
    unnamed x23, local copies, waits for them, and re-layouts  21.9 us
    pallas_call x3, Pallas kernels, pick(): pl.pallas_call(kernel, grid_spec=pltpu.PrefetchScalarGridSpec(num_scalar_...  19.9 us
    ppermute x12, starting transfers between devices, hop(): lax.ppermute(v, 'dp', pairs(mesh.shape['dp'], n))  15.8 us
    pallas_call x3, Pallas kernels, settle(): pl.pallas_call(wrapped, grid_spec=pltpu.PrefetchScalarGridSpec(num_scalar...  14.6 us
    pallas_call x3, Pallas kernels, merge(): pl.pallas_call(kernel, grid_spec=pltpu.PrefetchScalarGridSpec(num_scalar_...  13.7 us
    pallas_call x1, Pallas kernels, finish(): pl.pallas_call(kernel, grid=(rows // TILE,), in_specs=[whole_vmem] * (4 +...  13.4 us
  transfers between devices with their start and end apart: 17, of which 12 were waited for; matrix products, arithmetic and copies ran while one was open for 0% of the time, Pallas kernels for 11%

profile of v1, /device:TPU:0, one launch (start us, length us, event | category | flops | bytes accessed | tf_op | source)
XLA Modules:
  0.0 393.6 jit_solution(8242106272224782088)
XLA Ops:
  0.6 9.7 %pick.5 = (bf16[896,2560]{1,0:T(8,128)(2,1)}, bf16[896,2560]{1,0:T(8,128)(2,1)}) custom-call(s32[1]{0:T(128)} %bitcast.me_ref, bf16[4,2048,2560]{2,1,0:T(8,128)(2,1)} %bitcast.5, bf16[4,2048,2560]{2,1,0:T(8,128)(2,1)} %bitcast.6), custom_call_target="tpu_custom_call" | custom-call | bytes 18350080 | tf_op jit(solution)/shard_map/pick/pallas_call | solution.py:48
  10.3 2.9 collective-permute-start.4
  13.3 1.5 collective-permute-start.5
  14.8 10.1 %pick.3 = (bf16[1024,2560]{1,0:T(8,128)(2,1)}, bf16[1024,2560]{1,0:T(8,128)(2,1)}) custom-call(s32[1]{0:T(128)} %bitcast.me_ref, bf16[4,2048,2560]{2,1,0:T(8,128)(2,1)} %bitcast.7, bf16[4,2048,2560]{2,1,0:T(8,128)(2,1)} %bitcast.8), custom_call_target="tpu_custom_call" | custom-call | bytes 20971520 | tf_op jit(solution)/shard_map/pick/pallas_call | solution.py:48
  25.4 12.9 %copy-done = bf16[1,4,2048,2560]{3,2,1,0:T(8,128)(2,1)S(1)} copy-done((bf16[1,4,2048,2560]{3,2,1,0:T(8,128)(2,1)S(1)}, bf16[1,4,2048,2560]{3,2,1,0:T(8,128)(2,1)}, u32[]{:S(2)}) %copy-start) | copy-done | bytes 41943064
  38.4 2.1 collective-permute-start.2
  40.5 72.9 %collective-permute-done.4.b0 = bf16[896,2560]{1,0:T(8,128)(2,1)} collective-permute-done((bf16[896,2560]{1,0:T(8,128)(2,1)}, bf16[896,2560]{1,0:T(8,128)(2,1)}, u32[]{:S(2)}, u32[]{:S(2)}) %collective-permute-start.4) | collective-permute-done | bytes 4587552 | tf_op jit(solution)/shard_map/ppermute | solution.py:366
  113.4 2.1 collective-permute-done.5.b1
  115.5 6.7 %merge.3 = (bf16[512,2560]{1,0:T(8,128)(2,1)}, bf16[512,2560]{1,0:T(8,128)(2,1)}) custom-call(s32[1]{0:T(128)} %bitcast.me_ref, bf16[4,2048,2560]{2,1,0:T(8,128)(2,1)} %bitcast.9, bf16[4,2048,2560]{2,1,0:T(8,128)(2,1)} %bitcast.10, bf16[896,2560]{1,0:T(8,128)(2,1)} %collective-permute-done.4.b0, bf16[896,2560]{1,0:T(8,128)(2,1)} %collective-permute-done.5.b1), custom_call_target="tpu_custom_call" | custom-call | flops 2621440 | bytes 15728640 | tf_op jit(solution)/shard_map/merge/pallas_call | solution.py:75
  122.3 1.5 collective-permute-start.10
  124.3 115.4 %collective-permute-done.2.b0 = bf16[128,2560]{1,0:T(8,128)(2,1)S(1)} collective-permute-done((bf16[128,2560]{1,0:T(8,128)(2,1)S(1)}, bf16[128,2560]{1,0:T(8,128)(2,1)S(1)}, u32[]{:S(2)}, u32[]{:S(2)}) %collective-permute-start.2) | collective-permute-done | bytes 655392 | tf_op jit(solution)/shard_map/ppermute | solution.py:366
  239.7 2.1 collective-permute-start.3
  241.8 4.1 %merge.4 = (bf16[384,2560]{1,0:T(8,128)(2,1)S(1)}, bf16[384,2560]{1,0:T(8,128)(2,1)S(1)}) custom-call(s32[1]{0:T(128)} %bitcast.me_ref, bf16[4,2048,2560]{2,1,0:T(8,128)(2,1)} %bitcast.11, bf16[4,2048,2560]{2,1,0:T(8,128)(2,1)} %bitcast.12, bf16[896,2560]{1,0:T(8,128)(2,1)} %collective-permute-done.4.b0, bf16[896,2560]{1,0:T(8,128)(2,1)} %collective-permute-done.5.b1), custom_call_target="tpu_custom_call" | custom-call | flops 1966080 | bytes 11796480 | tf_op jit(solution)/shard_map/merge/pallas_call | solution.py:75
  245.9 50.6 %collective-permute-done.3.b1 = bf16[128,2560]{1,0:T(8,128)(2,1)S(1)} collective-permute-done((bf16[128,2560]{1,0:T(8,128)(2,1)S(1)}, bf16[128,2560]{1,0:T(8,128)(2,1)S(1)}, u32[]{:S(2)}, u32[]{:S(2)}) %collective-permute-start.3) | collective-permute-done | bytes 655392 | tf_op jit(solution)/shard_map/ppermute | solution.py:366
  296.5 1.5 collective-permute-start.8
  298.7 2.8 merge.5
  301.7 2.3 collective-permute-start.7
  304.8 1.2 slice-done.4
  306.0 6.0 %param_power.1.refs_4_ = f32[8,128]{1,0:T(8,128)S(1)} custom-call(f32[2048,2560]{1,0:T(8,128)S(1)} %bitcast.25), custom_call_target="tpu_custom_call" | custom-call | flops 10485760 | bytes 20971520 | tf_op jit(solution)/shard_map/param_power/pallas_call | solution.py:203
  312.0 7.0 %settle.3 = (bf16[2048,2560]{1,0:T(8,128)(2,1)S(1)}, f32[1,2560]{1,0:T(1,128)S(1)}, f32[2,512]{1,0:T(2,128)S(1)}) custom-call(s32[1]{0:T(128)} %bitcast.me_ref, bf16[4,2048,2560]{2,1,0:T(8,128)(2,1)} %bitcast.15, bf16[4,2048,2560]{2,1,0:T(8,128)(2,1)} %bitcast.16, bf16[1024,2560]{1,0:T(8,128)(2,1)S(1)} %collective-permute-done.refs_2_, ...), custom_call_target="tpu_custom_call" | custom-call | flops 15728640 | bytes 15728640 | tf_op jit(solution)/shard_map/settle/pallas_call | solution.py:165
  319.1 23.2 %collective-permute-done.8.refs_4_ = bf16[384,2560]{1,0:T(8,128)(2,1)S(1)} collective-permute-done((bf16[384,2560]{1,0:T(8,128)(2,1)S(1)}, bf16[384,2560]{1,0:T(8,128)(2,1)S(1)}, u32[]{:S(2)}, u32[]{:S(2)}) %collective-permute-start.8) | collective-permute-done | bytes 1966112 | tf_op jit(solution)/shard_map/ppermute | solution.py:366
  342.3 1.6 collective-permute-done.9.refs_5_
  343.9 5.4 %settle.4 = (bf16[2048,2560]{1,0:T(8,128)(2,1)S(1)}, f32[1,2560]{1,0:T(1,128)S(1)}, f32[2,384]{1,0:T(2,128)S(1)}) custom-call(s32[1]{0:T(128)} %bitcast.me_ref, bf16[4,2048,2560]{2,1,0:T(8,128)(2,1)} %bitcast.17, bf16[4,2048,2560]{2,1,0:T(8,128)(2,1)} %bitcast.18, ...), custom_call_target="tpu_custom_call", output_to_operand_aliasing={{0}: (7, {})} | custom-call | flops 11796480 | bytes 11796480 | tf_op jit(solution)/shard_map/settle/pallas_call | solution.py:165
  349.3 4.6 %collective-permute-done.6.refs_4_ = bf16[128,2560]{1,0:T(8,128)(2,1)S(1)} collective-permute-done((bf16[128,2560]{1,0:T(8,128)(2,1)}, bf16[128,2560]{1,0:T(8,128)(2,1)S(1)}, u32[]{:S(2)}, u32[]{:S(2)}) %collective-permute-start.6) | collective-permute-done | bytes 655392 | tf_op jit(solution)/shard_map/ppermute | solution.py:366
  353.9 1.3 collective-permute-done.7.refs_5_
  355.3 2.2 settle.5
  358.8 4.4 %weigh.1 = (f32[1,2560]{1,0:T(1,128)}, f32[1,2560]{1,0:T(1,128)S(1)}, f32[1,4224]{1,0:T(1,128)S(1)}) custom-call(bf16[2048,2560]{1,0:T(8,128)(2,1)S(1)} %get-tuple-element.57.g_ref, f32[1,2560]{1,0:T(1,128)S(1)} %get-tuple-element.58.refs_0_, f32[1,2560]{1,0:T(1,128)S(1)} %collective-permute-done.12.refs_1_, f32[1,2560]{1,0:T(1,128)S(1)} %copy-done.2, ...), custom_call_target="tpu_custom_call" | custom-call | flops 20971520 | bytes 10485760 | tf_op jit(solution)/shard_map/weigh/pallas_call | solution.py:253
  363.2 3.6 collective-permute-start.15
  368.7 2.7 collective-permute-done.14.refs_2_
  372.1 1.2 collective-permute-done.16.refs_1_
  373.2 7.0 %copy-done.1 = f32[1,2048,2560]{2,1,0:T(8,128)S(1)} copy-done((f32[1,2048,2560]{2,1,0:T(8,128)S(1)}, f32[1,2048,2560]{2,1,0:T(8,128)}, u32[]{:S(2)}) %copy-start.1) | copy-done | bytes 20971544
  380.2 13.4 %finish.1 = (f32[2048,2560]{1,0:T(8,128)}, bf16[2048,2560]{1,0:T(8,128)(2,1)}) custom-call(bf16[2048,2560]{1,0:T(8,128)(2,1)S(1)} %get-tuple-element.57.g_ref, f32[2048,2560]{1,0:T(8,128)S(1)} %bitcast.26, f32[1,2048]{1,0:T(1,128)S(1)} %get-tuple-element.63.row_ref, f32[1,2560]{1,0:T(1,128)S(1)} %get-tuple-element.64.col_ref, ...), custom_call_target="tpu_custom_call" | custom-call | flops 31457280 | bytes 62914560 | tf_op jit(solution)/shard_map/finish/pallas_call | solution.py:340
  (40 shorter events, 6.6 us)
Async XLA Ops:
  10.3 103.1 %collective-permute-start.4 = (bf16[896,2560]{1,0:T(8,128)(2,1)}, bf16[896,2560]{1,0:T(8,128)(2,1)}, u32[]{:S(2)}, u32[]{:S(2)}) collective-permute-start(bf16[896,2560]{1,0:T(8,128)(2,1)} %get-tuple-element.41), channel_id=1, source_target_pairs={{0,8},{8,0},{16,24},{24,16},{1,9},{9,1},{17,25},{25,17},{2,10},{10... | collective-permute-start | bytes 13762568 | tf_op jit(solution)/shard_map/ppermute | solution.py:366
  13.3 102.2 %collective-permute-start.5 = (bf16[896,2560]{1,0:T(8,128)(2,1)}, bf16[896,2560]{1,0:T(8,128)(2,1)}, u32[]{:S(2)}, u32[]{:S(2)}) collective-permute-start(bf16[896,2560]{1,0:T(8,128)(2,1)} %get-tuple-element.42), channel_id=1, source_target_pairs={{0,16},{8,24},{16,0},{24,8},{1,17},{9,25},{17,1},{25,9},{2,18},{10... | collective-permute-start | bytes 13762568 | tf_op jit(solution)/shard_map/ppermute | solution.py:366
  24.9 273.2 %collective-permute-start = (bf16[1024,2560]{1,0:T(8,128)(2,1)}, bf16[1024,2560]{1,0:T(8,128)(2,1)S(1)}, u32[]{:S(2)}, u32[]{:S(2)}) collective-permute-start(bf16[1024,2560]{1,0:T(8,128)(2,1)} %get-tuple-element.37), channel_id=1, source_target_pairs={{0,8},{8,0},{16,24},{24,16},{1,9},{9,1},{17,25},{25,17},{2,10},{10... | collective-permute-start | bytes 15728648 | tf_op jit(solution)/shard_map/ppermute | solution.py:366
  25.4 276.1 %collective-permute-start.1 = (bf16[1024,2560]{1,0:T(8,128)(2,1)}, bf16[1024,2560]{1,0:T(8,128)(2,1)S(1)}, u32[]{:S(2)}, u32[]{:S(2)}) collective-permute-start(bf16[1024,2560]{1,0:T(8,128)(2,1)} %get-tuple-element.38), channel_id=1, source_target_pairs={{0,16},{8,24},{16,0},{24,8},{1,17},{9,25},{17,1},{25,9},{2,18},{10... | collective-permute-start | bytes 15728648 | tf_op jit(solution)/shard_map/ppermute | solution.py:366
  25.4 12.9 %copy-start = (bf16[1,4,2048,2560]{3,2,1,0:T(8,128)(2,1)S(1)}, bf16[1,4,2048,2560]{3,2,1,0:T(8,128)(2,1)}, u32[]{:S(2)}) copy-start(bf16[1,4,2048,2560]{3,2,1,0:T(8,128)(2,1)} %param.4) | copy-start | bytes 125829120
  38.4 201.3 %collective-permute-start.2 = (bf16[128,2560]{1,0:T(8,128)(2,1)S(1)}, bf16[128,2560]{1,0:T(8,128)(2,1)S(1)}, u32[]{:S(2)}, u32[]{:S(2)}) collective-permute-start(bf16[128,2560]{1,0:T(8,128)(2,1)S(1)} %get-tuple-element.39), channel_id=1, source_target_pairs={{0,8},{8,0},{16,24},{24,16},{1,9},{9,1},{17,25},{25,17},{2,10},{10... | collective-permute-start | bytes 1966088 | tf_op jit(solution)/shard_map/ppermute | solution.py:366
  122.3 179.4 %collective-permute-start.10 = (bf16[512,2560]{1,0:T(8,128)(2,1)}, bf16[512,2560]{1,0:T(8,128)(2,1)S(1)}, u32[]{:S(2)}, u32[]{:S(2)}) collective-permute-start(bf16[512,2560]{1,0:T(8,128)(2,1)} %get-tuple-element.43), channel_id=1, source_target_pairs={{0,16},{8,24},{16,0},{24,8},{1,17},{9,25},{17,1},{25,9},{2,18},{10... | collective-permute-start | bytes 7864328 | tf_op jit(solution)/shard_map/ppermute | solution.py:366
  123.8 188.2 %collective-permute-start.11 = (bf16[512,2560]{1,0:T(8,128)(2,1)}, bf16[512,2560]{1,0:T(8,128)(2,1)S(1)}, u32[]{:S(2)}, u32[]{:S(2)}) collective-permute-start(bf16[512,2560]{1,0:T(8,128)(2,1)} %get-tuple-element.44), channel_id=1, source_target_pairs={{0,8},{8,0},{16,24},{24,16},{1,9},{9,1},{17,25},{25,17},{2,10},{10... | collective-permute-start | bytes 7864328 | tf_op jit(solution)/shard_map/ppermute | solution.py:366
  239.7 56.8 %collective-permute-start.3 = (bf16[128,2560]{1,0:T(8,128)(2,1)S(1)}, bf16[128,2560]{1,0:T(8,128)(2,1)S(1)}, u32[]{:S(2)}, u32[]{:S(2)}) collective-permute-start(bf16[128,2560]{1,0:T(8,128)(2,1)S(1)} %get-tuple-element.40), channel_id=1, source_target_pairs={{0,16},{8,24},{16,0},{24,8},{1,17},{9,25},{17,1},{25,9},{2,18},{10... | collective-permute-start | bytes 1966088 | tf_op jit(solution)/shard_map/ppermute | solution.py:366
  296.5 45.8 %collective-permute-start.8 = (bf16[384,2560]{1,0:T(8,128)(2,1)S(1)}, bf16[384,2560]{1,0:T(8,128)(2,1)S(1)}, u32[]{:S(2)}, u32[]{:S(2)}) collective-permute-start(bf16[384,2560]{1,0:T(8,128)(2,1)S(1)} %get-tuple-element.47), channel_id=1, source_target_pairs={{0,16},{8,24},{16,0},{24,8},{1,17},{9,25},{17,1},{25,9},{2,18},{10... | collective-permute-start | bytes 5898248 | tf_op jit(solution)/shard_map/ppermute | solution.py:366
  298.1 5.9 %slice-start = ((s8[20971520]{0:T(1024)(128)(4,1)}), s8[4194304]{0:T(1024)(128)(4,1)S(1)}, s32[]{:S(2)}) async-start(s8[20971520]{0:T(1024)(128)(4,1)} %bitcast.23), calls=%async_computation | async-start | bytes 8388608
  298.1 5.9 %slice-start.1 = ((s8[20971520]{0:T(1024)(128)(4,1)}), s8[4194304]{0:T(1024)(128)(4,1)S(1)}, s32[]{:S(2)}) async-start(s8[20971520]{0:T(1024)(128)(4,1)} %bitcast.23), calls=%async_computation.1 | async-start | bytes 8388608
  298.1 5.9 %slice-start.2 = ((s8[20971520]{0:T(1024)(128)(4,1)}), s8[4194304]{0:T(1024)(128)(4,1)S(1)}, s32[]{:S(2)}) async-start(s8[20971520]{0:T(1024)(128)(4,1)} %bitcast.23), calls=%async_computation.2 | async-start | bytes 8388608
  298.1 6.7 %slice-start.3 = ((s8[20971520]{0:T(1024)(128)(4,1)}), s8[4194304]{0:T(1024)(128)(4,1)S(1)}, s32[]{:S(2)}) async-start(s8[20971520]{0:T(1024)(128)(4,1)} %bitcast.23), calls=%async_computation.3 | async-start | bytes 8388608
  298.1 7.9 %slice-start.4 = ((s8[20971520]{0:T(1024)(128)(4,1)}), s8[4194304]{0:T(1024)(128)(4,1)S(1)}, s32[]{:S(2)}) async-start(s8[20971520]{0:T(1024)(128)(4,1)} %bitcast.23), calls=%async_computation.4 | async-start | bytes 8388608
  298.1 45.8 %collective-permute-start.9 = (bf16[384,2560]{1,0:T(8,128)(2,1)S(1)}, bf16[384,2560]{1,0:T(8,128)(2,1)S(1)}, u32[]{:S(2)}, u32[]{:S(2)}) collective-permute-start(bf16[384,2560]{1,0:T(8,128)(2,1)S(1)} %get-tuple-element.48), channel_id=1, source_target_pairs={{0,8},{8,0},{16,24},{24,16},{1,9},{9,1},{17,25},{25,17},{2,10},{10... | collective-permute-start | bytes 5898248 | tf_op jit(solution)/shard_map/ppermute | solution.py:366
  301.5 52.4 %collective-permute-start.6 = (bf16[128,2560]{1,0:T(8,128)(2,1)}, bf16[128,2560]{1,0:T(8,128)(2,1)S(1)}, u32[]{:S(2)}, u32[]{:S(2)}) collective-permute-start(bf16[128,2560]{1,0:T(8,128)(2,1)} %get-tuple-element.51), channel_id=1, source_target_pairs={{0,16},{8,24},{16,0},{24,8},{1,17},{9,25},{17,1},{25,9},{2,18},{10... | collective-permute-start | bytes 1966088 | tf_op jit(solution)/shard_map/ppermute | solution.py:366
  301.7 53.6 %collective-permute-start.7 = (bf16[128,2560]{1,0:T(8,128)(2,1)}, bf16[128,2560]{1,0:T(8,128)(2,1)S(1)}, u32[]{:S(2)}, u32[]{:S(2)}) collective-permute-start(bf16[128,2560]{1,0:T(8,128)(2,1)} %get-tuple-element.52), channel_id=1, source_target_pairs={{0,8},{8,0},{16,24},{24,16},{1,9},{9,1},{17,25},{25,17},{2,10},{10... | collective-permute-start | bytes 1966088 | tf_op jit(solution)/shard_map/ppermute | solution.py:366
  355.3 3.5 copy-start.2
  357.5 1.2 collective-permute-start.12
  358.8 12.7 %copy-start.3 = (f32[1,2048]{1,0:T(1,128)S(1)}, f32[1,2048]{1,0:T(1,128)}, u32[]{:S(2)}) copy-start(f32[1,2048]{1,0:T(1,128)} %refs_4_.1) | copy-start | bytes 24580
  363.2 5.5 %collective-permute-start.15 = (f32[1,4224]{1,0:T(1,128)S(1)}, f32[1,4224]{1,0:T(1,128)S(1)}, u32[]{:S(2)}, u32[]{:S(2)}) collective-permute-start(f32[1,4224]{1,0:T(1,128)S(1)} %get-tuple-element.62.refs_0_), channel_id=1, source_target_pairs={{0,3},{1,2},{2,1},{3,0},{4,7},{5,6},{6,5},{7,4},{8,11},{9,10},{10,... | collective-permute-start | bytes 50696 | tf_op jit(solution)/shard_map/ppermute | solution.py:354
  366.8 4.6 %collective-permute-start.14 = (f32[1,4224]{1,0:T(1,128)S(1)}, f32[1,4224]{1,0:T(1,128)S(1)}, u32[]{:S(2)}, u32[]{:S(2)}) collective-permute-start(f32[1,4224]{1,0:T(1,128)S(1)} %get-tuple-element.62.refs_0_), channel_id=1, source_target_pairs={{0,2},{1,3},{2,0},{3,1},{4,6},{5,7},{6,4},{7,5},{8,10},{9,11},{10,... | collective-permute-start | bytes 50696 | tf_op jit(solution)/shard_map/ppermute | solution.py:354
  366.8 4.6 %collective-permute-start.13 = (f32[1,4224]{1,0:T(1,128)S(1)}, f32[1,4224]{1,0:T(1,128)S(1)}, u32[]{:S(2)}, u32[]{:S(2)}) collective-permute-start(f32[1,4224]{1,0:T(1,128)S(1)} %get-tuple-element.62.refs_0_), channel_id=1, source_target_pairs={{0,1},{1,0},{2,3},{3,2},{4,5},{5,4},{6,7},{7,6},{8,9},{9,8},{10,11... | collective-permute-start | bytes 50696 | tf_op jit(solution)/shard_map/ppermute | solution.py:354
  372.1 1.2 collective-permute-start.16
  373.2 7.0 %copy-start.1 = (f32[1,2048,2560]{2,1,0:T(8,128)S(1)}, f32[1,2048,2560]{2,1,0:T(8,128)}, u32[]{:S(2)}) copy-start(f32[1,2048,2560]{2,1,0:T(8,128)} %param.5) | copy-start | bytes 62914564

commit v2 on v1

--- a/solution.py
+++ b/solution.py
@@ -13,6 +13,7 @@
 LANES = 128
 TILE = 128
 GROUP = 16
+SHARES = 4
 MIB = 1 << 20
 
 NEAR = (1, 2)
@@ -24,6 +25,10 @@
 
 def pairs(n, k):
     return [(i, i ^ k) for i in range(n)]
+
+
+def in_hbm(x):
+    return pltpu.with_memory_space_constraint(x, pltpu.HBM)
 
 
 def cost(flops, bytes_accessed):
@@ -81,7 +86,7 @@
             out_specs=[pl.BlockSpec((TILE, columns), lambda t, m: (t, 0))] * 2,
         ),
         out_shape=[jax.ShapeDtypeStruct((size, columns), parts.dtype)] * 2,
-        compiler_params=params_of(12 * MIB),
+        compiler_params=params_of(9 * MIB),
         cost_estimate=cost(2 * size * columns, 12 * size * columns),
         name="merge",
     )(me, parts, parts, *got)
@@ -98,17 +103,15 @@
     steps = size // step
 
     def kernel(me_ref, a0, a1, b0, b1, c0, c1, *refs):
+        before_ref = None
         if state is not None:
-            refs = refs[2:]
+            before_ref, refs = refs[1], refs[2:]
         g_ref, col_ref, row_ref, sums_ref, carry_ref = refs
         t = pl.program_id(0)
 
         @pl.when(t == 0)
         def _():
-            if state is None:
-                carry_ref[...] = jnp.zeros_like(carry_ref)
-            else:
-                carry_ref[...] = jnp.zeros_like(carry_ref)
+            carry_ref[...] = jnp.zeros_like(carry_ref)
 
         for h, (a, b, c) in enumerate(((a0, b0, c0), (a1, b1, c1))):
 
@@ -141,14 +144,7 @@
                     row_ref[h : h + 1, lanes] = lane_sums(sums_ref[h, lanes, :])
             col_ref[...] = jnp.sum(carry_ref[...], axis=0, keepdims=True)
             if state is not None:
-                col_ref[...] = col_ref[...] + refs_in[1][...]
-
-    refs_in = [None, None]
-
-    def wrapped(me_ref, *refs):
-        if state is not None:
-            refs_in[0], refs_in[1] = refs[6], refs[7]
-        kernel(me_ref, *refs)
+                col_ref[...] = col_ref[...] + before_ref[...]
 
     def own(h):
         return pl.BlockSpec((None, step, columns), lambda t, m: (m[0], (h * half + at) // step + t, 0))
@@ -163,7 +159,7 @@
         operands += state
         aliases = {7: 0}
     return pl.pallas_call(
-        wrapped,
+        kernel,
         grid_spec=pltpu.PrefetchScalarGridSpec(
             num_scalar_prefetch=1,
             grid=(steps,),
@@ -177,7 +173,7 @@
             jax.ShapeDtypeStruct((2, size), jnp.float32),
         ],
         input_output_aliases=aliases,
-        compiler_params=params_of(16 * MIB),
+        compiler_params=params_of(7 * MIB),
         cost_estimate=cost(12 * size * columns, 12 * size * columns),
         name="settle",
     )(me, *operands)
@@ -185,31 +181,43 @@
 
 def power_of(params):
     rows, columns = params.shape
-
-    def kernel(p_ref, o_ref):
-        @pl.when(pl.program_id(0) == 0)
-        def _():
-            o_ref[...] = jnp.zeros_like(o_ref)
-
-        def body(r, total):
-            here = pl.ds(pl.multiple_of(r * 8, 8), 8)
-            for k in range(columns // LANES):
-                p = p_ref[here, k * LANES : (k + 1) * LANES]
-                total = total + p * p
-            return total
-
-        o_ref[...] += lax.fori_loop(0, TILE // 8, body, jnp.zeros((8, LANES), jnp.float32))
-
-    return pl.pallas_call(
-        kernel,
-        grid=(rows // TILE,),
-        in_specs=[pl.BlockSpec((TILE, columns), lambda t: (t, 0))],
-        out_specs=pl.BlockSpec((8, LANES), lambda t: (0, 0)),
-        out_shape=jax.ShapeDtypeStruct((8, LANES), jnp.float32),
-        compiler_params=params_of(8 * MIB),
+    steps = rows // TILE
+    shares = min(SHARES, steps)
+    each = steps // shares
+
+    def kernel(p_ref, *refs):
+        *kept, o_ref, sems = refs
+        copies = []
+        for t in range(steps):
+            here, there = pl.ds(t * TILE, TILE), pl.ds(t % each * TILE, TILE)
+            copies.append(pltpu.make_async_copy(p_ref.at[here], kept[t // each].at[there], sems.at[t]))
+            copies[-1].start()
+        total = jnp.zeros((8, LANES), jnp.float32)
+        for t in range(steps):
+            copies[t].wait()
+
+            def body(r, total):
+                here = pl.ds(pl.multiple_of(t % each * TILE + r * 8, 8), 8)
+                for k in range(columns // LANES):
+                    p = kept[t // each][here, k * LANES : (k + 1) * LANES]
+                    total = total + p * p
+                return total
+
+            total = lax.fori_loop(0, TILE // 8, body, total)
+        o_ref[...] = total
+
+    *kept, power = pl.pallas_call(
+        kernel,
+        in_specs=[anywhere],
+        out_specs=[whole_vmem] * (shares + 1),
+        out_shape=[pltpu.VMEM((rows // shares, columns), jnp.float32)] * shares
+        + [jax.ShapeDtypeStruct((8, LANES), jnp.float32)],
+        scratch_shapes=[pltpu.SemaphoreType.DMA((steps,))],
+        compiler_params=params_of(MIB),
         cost_estimate=cost(2 * rows * columns, 4 * rows * columns),
         name="param_power",
-    )(params)
+    )(in_hbm(params))
+    return kept, power
 
 
 def tree(values):
@@ -308,50 +316,86 @@
 def finish(gradient, params, row_root, col_root, stats):
     rows, columns = gradient.shape
     n = len(stats)
-
-    def kernel(g_ref, p_ref, row_ref, col_ref, *refs):
-        got, (new_ref, update_ref, scale_ref) = refs[:n], refs[n:]
-        t = pl.program_id(0)
-
-        @pl.when(t == 0)
-        def _():
-            total = jnp.sum(tree([s[...] for s in got]), axis=1, keepdims=True)
-            mean = total[1:2] / D
-            rms = jnp.sqrt(mean * total[0:1] / (D * FF))
-            scale = jnp.sqrt(total[2:3] / (D * FF))
-            factor = scale * jnp.sqrt(mean) / jnp.maximum(1.0, rms)
-            scale_ref[...] = jnp.broadcast_to(col_ref[...] * factor, scale_ref.shape)
-
-        first = pl.multiple_of(t * TILE, TILE)
-        lanes = row_ref[:, pl.ds(first, TILE)]
-        wide = jnp.broadcast_to(lanes, (TILE, TILE)).T
-        for r in range(TILE // GROUP):
-            here = pl.ds(pl.multiple_of(first + r * GROUP, GROUP), GROUP)
-            out = slice(r * GROUP, (r + 1) * GROUP)
-            root = wide[out, :]
-            for k in range(columns // LANES):
-                at = slice(k * LANES, (k + 1) * LANES)
-                g = g_ref[here, at].astype(jnp.float32)
-                s = scale_ref[:, at]
-                full = jnp.concatenate([g[:8] * s, g[8:] * s], axis=0) * root
-                update_ref[out, at] = full.astype(update_ref.dtype)
-                new_ref[out, at] = p_ref[here, at] - LEARN_RATE * full
-
-    return pl.pallas_call(
-        kernel,
-        grid=(rows // TILE,),
-        in_specs=[whole_vmem] * (4 + n),
-        out_specs=[pl.BlockSpec((TILE, columns), lambda t: (t, 0))] * 2,
-        out_shape=[jax.ShapeDtypeStruct((rows, columns), jnp.float32), jax.ShapeDtypeStruct((rows, columns), jnp.bfloat16)],
-        scratch_shapes=[pltpu.VMEM((8, columns), jnp.float32)],
-        compiler_params=params_of(8 * MIB),
+    shares = len(params)
+    each = rows // shares // TILE
+    group = 2 * GROUP
+
+    def kernel(_, row_ref, col_ref, *refs):
+        got, refs = refs[shares : shares + n], refs[shares + n :]
+        g_ref, held, (new_ref, update_ref, scale_ref, sems) = refs[0], refs[1 : 1 + shares], refs[1 + shares :]
+        total = jnp.sum(tree([s[...] for s in got]), axis=1, keepdims=True)
+        mean = total[1:2] / D
+        rms = jnp.sqrt(mean * total[0:1] / (D * FF))
+        scale = jnp.sqrt(total[2:3] / (D * FF))
+        factor = scale * jnp.sqrt(mean) / jnp.maximum(1.0, rms)
+        scale_ref[...] = jnp.broadcast_to(col_ref[...] * factor, scale_ref.shape)
+
+        def copies(q, t):
+            here = pl.ds(pl.multiple_of((q * each + t) * TILE, TILE), TILE)
+            there = pl.ds(pl.multiple_of(t * TILE, TILE), TILE)
+            return (
+                pltpu.make_async_copy(held[q].at[there], new_ref.at[here], sems.at[0, q * each + t]),
+                pltpu.make_async_copy(g_ref.at[here], update_ref.at[here], sems.at[1, q * each + t]),
+            )
+
+        for q in range(shares):
+
+            def block(t, carry):
+                first = pl.multiple_of((q * each + t) * TILE, TILE)
+                wide = jnp.broadcast_to(row_ref[:, pl.ds(first, TILE)], (LANES, TILE)).T
+                for r in range(0, TILE, group):
+                    here = pl.ds(pl.multiple_of(first + r, group), group)
+                    there = pl.ds(pl.multiple_of(t * TILE + r, group), group)
+                    root = wide[r : r + group, :]
+                    for k in range(columns // LANES):
+                        at = slice(k * LANES, (k + 1) * LANES)
+                        g = g_ref[here, at].astype(jnp.float32)
+                        s = scale_ref[:, at]
+                        full = jnp.concatenate([g[i : i + 8] * s for i in range(0, group, 8)], axis=0) * root
+                        g_ref[here, at] = full.astype(g_ref.dtype)
+                        held[q][there, at] = held[q][there, at] - LEARN_RATE * full
+                for copy in copies(q, t):
+                    copy.start()
+                return carry
+
+            lax.fori_loop(0, each, block, 0)
+
+        for q in range(shares):
+
+            def drain(t, carry):
+                for copy in copies(q, t):
+                    copy.wait()
+                return carry
+
+            lax.fori_loop(0, each, drain, 0)
+
+    out = pl.pallas_call(
+        kernel,
+        in_specs=[anywhere, whole_vmem, whole_vmem] + [anywhere] * shares + [whole_vmem] * n,
+        out_specs=[whole_vmem] * (1 + shares) + [anywhere] * 2,
+        out_shape=[pltpu.VMEM(x.shape, x.dtype) for x in (gradient, *params)]
+        + [pltpu.HBM((rows, columns), jnp.float32), pltpu.HBM((rows, columns), jnp.bfloat16)],
+        input_output_aliases={0: 0, **{3 + q: 1 + q for q in range(shares)}},
+        scratch_shapes=[pltpu.VMEM((8, columns), jnp.float32), pltpu.SemaphoreType.DMA((2, rows // TILE))],
+        compiler_params=params_of(4 * MIB),
         cost_estimate=cost(6 * rows * columns, 12 * rows * columns),
         name="finish",
-    )(gradient, params, row_root, col_root, *stats)
+    )(gradient, row_root, col_root, *params, *stats)
+    return out[-2:]
 
 
 def all_parts(value, axis, size):
     return [value] + [lax.ppermute(value, axis, pairs(size, k)) for k in range(1, size)]
+
+
+def cut(half):
+    units = half // TILE
+    sizes = [1, 2, units - 3] if units > 3 else [1, units - 1] if units > 1 else [units]
+    edges, at = [], 0
+    for n in sizes:
+        edges.append((at, n * TILE))
+        at += n * TILE
+    return edges
 
 
 def after(values, others):
@@ -371,36 +415,40 @@
         half = rows // 2
         me = lax.axis_index("dp").astype(jnp.int32)[None]
 
-        head = min(TILE, half)
-        rest = half - head
-        first_head = hop(pick(parts, me, [(3, 0), (3, half)], head), NEAR)
-        pieces = []
-        if rest:
-            first_rest = hop(pick(parts, me, [(3, head), (3, half + head)], rest), NEAR)
-            mine = (rest // TILE + 1) // 2 * TILE
-            pieces = [(head, mine)] + ([(head + mine, rest - mine)] if rest > mine else [])
-        second = hop(pick(parts, me, [(NEAR[0], 0), (NEAR[1], half)], half), NEAR)
-        power = power_of(params[0])
-
-        merged = []
+        held = in_hbm(parts)
+        pieces = cut(half)
+        rounds = []
+
+        def send(values, lines):
+            if len(rounds) > 1:
+                values = after(values, rounds[-2])
+            rounds.append(hop(values, lines))
+            return rounds[-1]
+
+        first, turn = [], me
         for at, size in pieces:
-            got = after(first_rest, merged[-1]) if merged else first_rest
-            merged.append(merge(parts, me, got, at, head, size))
-        got = after(first_head, merged[-1]) if merged else first_head
-        merged.append(merge(parts, me, got, 0, 0, head))
-        pieces.append((0, head))
-        third = [hop(m, FAR) for m in merged]
+            picked = pick(held, turn, [(3, at), (3, half + at)], size)
+            (turn,) = after([me], picked)
+            first.append(send(picked, NEAR))
+        second = send(pick(held, turn, [(NEAR[0], 0), (NEAR[1], half)], half), NEAR)
+        pieces.reverse()
+        third, done = [], []
+        for (at, size), came in zip(pieces, reversed(first)):
+            done = merge(held, me, after(came, done), at, at, size)
+            third.append(send(done, FAR))
 
         state, row_pieces = None, {}
         for (at, size), came in zip(pieces, third):
-            gradient, col_sums, row_piece = settle(parts, me, second, came, at, size, state, min(64, size))
+            gradient, col_sums, row_piece = settle(held, me, second, came, at, size, state, min(64, size))
+            if state is None:
+                kept, power = power_of(after([params[0]], [col_sums])[0])
             state = [gradient, col_sums]
             row_pieces[at] = row_piece
         row_sums = jnp.concatenate([row_pieces[at][h : h + 1] for h in range(2) for at in sorted(row_pieces)], axis=1)
 
         new_col, col_root, message = weigh(gradient, all_parts(col_sums, "row", across), col_moment, row_sums, power)
         new_row, row_root, stats = balance(all_parts(message, "col", along), row_moment)
-        new_params, update = finish(gradient, params[0], row_root, col_root, all_parts(stats, "row", across))
+        new_params, update = finish(gradient, kept, row_root, col_root, all_parts(stats, "row", across))
         return new_params[None], update[None], new_row, new_col
 
     placed = (P("dp", None, "row", "col"), P("dp", "row", "col"), P("dp", "row"), P("dp", "col"))

time: 394 us -> 374 us (0.949)
  local copies, waits for them, and re-layouts: 22 us -> 4.79 us
  Pallas kernels: 72.5 us -> 60.9 us
  waiting for transfers between devices: 278 us -> 287 us
    unnamed x23 -> x21, local copies, waits for them, and re-layouts: 21.9 us -> 4.77 us
    ppermute x12 -> x14, waiting for transfers between devices: 272 us -> 281 us  [hop(): lax.ppermute(v, 'dp', pairs(mesh.shape['dp'], n))]
    pallas_call x3 -> x4, Pallas kernels: 19.9 us -> 13.7 us  [pick(): pl.pallas_call(kernel, grid_spec=pltpu.PrefetchScalarGridSpec(num_scalar_...]
    pallas_call x3, Pallas kernels: 13.7 us -> 8.59 us  [merge(): pl.pallas_call(kernel, grid_spec=pltpu.PrefetchScalarGridSpec(num_scalar_...]
    ppermute x12 -> x14, starting transfers between devices: 15.8 us -> 15.5 us  [hop(): lax.ppermute(v, 'dp', pairs(mesh.shape['dp'], n))]
  transfers between devices with their start and end apart: 17 -> 19, of which waited for: 12 -> 15; matrix products, arithmetic and copies ran while one was open for 0% -> 0% of each run, Pallas kernels for 11% -> 11%
where the time goes in v2:
time: 374 us; the launch traced here: 373 us
  waiting for transfers between devices  287 us (77%)
  Pallas kernels  60.9 us (16%)
  starting transfers between devices  20 us (5%)
  local copies, waits for them, and re-layouts  4.79 us (1%)
    ppermute x14, waiting for transfers between devices, hop(): lax.ppermute(v, 'dp', pairs(mesh.shape['dp'], n))  281 us
    ppermute x14, starting transfers between devices, hop(): lax.ppermute(v, 'dp', pairs(mesh.shape['dp'], n))  15.5 us
    pallas_call x3, Pallas kernels, settle(): pl.pallas_call(kernel, grid_spec=pltpu.PrefetchScalarGridSpec(num_scalar_...  15.1 us
    pallas_call x4, Pallas kernels, pick(): pl.pallas_call(kernel, grid_spec=pltpu.PrefetchScalarGridSpec(num_scalar_...  13.7 us
    pallas_call x1, Pallas kernels, finish(): pl.pallas_call(kernel, in_specs=[anywhere, whole_vmem, whole_vmem] + [any...  11 us
    pallas_call x3, Pallas kernels, merge(): pl.pallas_call(kernel, grid_spec=pltpu.PrefetchScalarGridSpec(num_scalar_...  8.59 us
    pallas_call x1, Pallas kernels, power_of(): pl.pallas_call(kernel, in_specs=[anywhere], out_specs=[whole_vmem] * (sha...  7.51 us
  transfers between devices with their start and end apart: 19, of which 15 were waited for; matrix products, arithmetic and copies ran while one was open for 0% of the time, Pallas kernels for 11%

profile of v2, /device:TPU:0, one launch (start us, length us, event | category | flops | bytes accessed | tf_op | source)
XLA Modules:
  0.0 373.4 jit_solution(16260222786835724710)
XLA Ops:
  2.0 3.0 collective-permute-start.4
  6.5 1.8 pick.5
  9.0 4.3 %pick.6 = (bf16[640,2560]{1,0:T(8,128)(2,1)S(1)}, bf16[640,2560]{1,0:T(8,128)(2,1)S(1)}) custom-call(s32[1]{0:T(128)} %bitcast.me_ref, bf16[4,2048,2560]{2,1,0:T(8,128)(2,1)} %bitcast.13, bf16[4,2048,2560]{2,1,0:T(8,128)(2,1)} %bitcast.14), custom_call_target="tpu_custom_call" | custom-call | bytes 13107200 | tf_op jit(solution)/shard_map/pick/pallas_call | solution.py:53
  13.3 7.3 %collective-permute-done.4.b0 = bf16[128,2560]{1,0:T(8,128)(2,1)S(1)} collective-permute-done((bf16[128,2560]{1,0:T(8,128)(2,1)S(1)}, bf16[128,2560]{1,0:T(8,128)(2,1)S(1)}, u32[]{:S(2)}, u32[]{:S(2)}) %collective-permute-start.4) | collective-permute-done | bytes 655392 | tf_op jit(solution)/shard_map/ppermute | solution.py:410
  20.6 2.1 collective-permute-done.5.b1
  22.7 2.0 collective-permute-start.7
  24.7 6.2 %pick.7 = (bf16[1024,2560]{1,0:T(8,128)(2,1)S(1)}, bf16[1024,2560]{1,0:T(8,128)(2,1)S(1)}) custom-call(s32[1]{0:T(128)} %bitcast.me_ref, bf16[4,2048,2560]{2,1,0:T(8,128)(2,1)} %bitcast.15, bf16[4,2048,2560]{2,1,0:T(8,128)(2,1)} %bitcast.16), custom_call_target="tpu_custom_call" | custom-call | bytes 20971520 | tf_op jit(solution)/shard_map/pick/pallas_call | solution.py:53
  30.9 17.7 %collective-permute-done.b0 = bf16[256,2560]{1,0:T(8,128)(2,1)S(1)} collective-permute-done((bf16[256,2560]{1,0:T(8,128)(2,1)S(1)}, bf16[256,2560]{1,0:T(8,128)(2,1)S(1)}, u32[]{:S(2)}, u32[]{:S(2)}) %collective-permute-start) | collective-permute-done | bytes 1310752 | tf_op jit(solution)/shard_map/ppermute | solution.py:410
  48.7 2.1 collective-permute-done.1.b1
  50.8 2.0 collective-permute-start.3
  52.8 66.1 %collective-permute-done.6.b0 = bf16[640,2560]{1,0:T(8,128)(2,1)S(1)} collective-permute-done((bf16[640,2560]{1,0:T(8,128)(2,1)S(1)}, bf16[640,2560]{1,0:T(8,128)(2,1)S(1)}, u32[]{:S(2)}, u32[]{:S(2)}) %collective-permute-start.6) | collective-permute-done | bytes 3276832 | tf_op jit(solution)/shard_map/ppermute | solution.py:410
  118.9 2.1 collective-permute-done.7.b1
  121.0 5.0 %merge.3 = (bf16[640,2560]{1,0:T(8,128)(2,1)S(1)}, bf16[640,2560]{1,0:T(8,128)(2,1)S(1)}) custom-call(s32[1]{0:T(128)} %bitcast.me_ref, bf16[4,2048,2560]{2,1,0:T(8,128)(2,1)} %bitcast.17, bf16[4,2048,2560]{2,1,0:T(8,128)(2,1)} %bitcast.18, bf16[640,2560]{1,0:T(8,128)(2,1)S(1)} %collective-permute-done.6.b0, bf16[640,2560]{1,0:T(8,128)(2,1)S(1)} %collective-permute-done.7.b1), custom_call_target="tpu_custom_call" | custom-call | flops 3276800 | bytes 19660800 | tf_op jit(solution)/shard_map/merge/pallas_call | solution.py:80
  126.0 1.6 collective-permute-start.8
  128.1 2.0 merge.4
  130.1 101.1 %collective-permute-done.2.b0 = bf16[1024,2560]{1,0:T(8,128)(2,1)S(1)} collective-permute-done((bf16[1024,2560]{1,0:T(8,128)(2,1)S(1)}, bf16[1024,2560]{1,0:T(8,128)(2,1)S(1)}, u32[]{:S(2)}, u32[]{:S(2)}) %collective-permute-start.2) | collective-permute-done | bytes 5242912 | tf_op jit(solution)/shard_map/ppermute | solution.py:410
  231.2 2.1 collective-permute-done.3.b1
  235.4 1.6 merge.5
  237.0 66.6 %collective-permute-done.8.c0 = bf16[640,2560]{1,0:T(8,128)(2,1)S(1)} collective-permute-done((bf16[640,2560]{1,0:T(8,128)(2,1)S(1)}, bf16[640,2560]{1,0:T(8,128)(2,1)S(1)}, u32[]{:S(2)}, u32[]{:S(2)}) %collective-permute-start.8) | collective-permute-done | bytes 3276832 | tf_op jit(solution)/shard_map/ppermute | solution.py:410
  303.6 1.5 collective-permute-start.10
  305.6 8.6 %settle.3 = (bf16[2048,2560]{1,0:T(8,128)(2,1)S(1)}, f32[1,2560]{1,0:T(1,128)S(1)}, f32[2,640]{1,0:T(2,128)S(1)}) custom-call(s32[1]{0:T(128)} %bitcast.me_ref, bf16[4,2048,2560]{2,1,0:T(8,128)(2,1)} %bitcast.23, bf16[4,2048,2560]{2,1,0:T(8,128)(2,1)} %bitcast.24, bf16[1024,2560]{1,0:T(8,128)(2,1)S(1)} %collective-permute-done.2.b0, ...), custom_call_target="tpu_custom_call" | custom-call | flops 19660800 | bytes 19660800 | tf_op jit(solution)/shard_map/settle/pallas_call | solution.py:161
  314.2 7.5 %param_power.1 = (f32[512,2560]{1,0:T(8,128)S(1)}, f32[512,2560]{1,0:T(8,128)S(1)}, f32[512,2560]{1,0:T(8,128)S(1)}, f32[512,2560]{1,0:T(8,128)S(1)}, f32[8,128]{1,0:T(8,128)S(1)}) custom-call(f32[2048,2560]{1,0:T(8,128)} %bitcast.29), custom_call_target="tpu_custom_call" | custom-call | flops 10485760 | bytes 20971520 | tf_op jit(solution)/shard_map/param_power/pallas_call | solution.py:209
  321.8 2.3 copy-done
  324.1 2.4 copy-done.1
  326.5 5.2 %collective-permute-done.12.c0 = bf16[256,2560]{1,0:T(8,128)(2,1)S(1)} collective-permute-done((bf16[256,2560]{1,0:T(8,128)(2,1)S(1)}, bf16[256,2560]{1,0:T(8,128)(2,1)S(1)}, u32[]{:S(2)}, u32[]{:S(2)}) %collective-permute-start.12) | collective-permute-done | bytes 1310752 | tf_op jit(solution)/shard_map/ppermute | solution.py:410
  331.7 4.1 %settle.4 = (bf16[2048,2560]{1,0:T(8,128)(2,1)S(1)}, f32[1,2560]{1,0:T(1,128)S(1)}, f32[2,256]{1,0:T(2,128)S(1)}) custom-call(s32[1]{0:T(128)} %bitcast.me_ref, bf16[4,2048,2560]{2,1,0:T(8,128)(2,1)} %bitcast.25, bf16[4,2048,2560]{2,1,0:T(8,128)(2,1)} %bitcast.26, bf16[1024,2560]{1,0:T(8,128)(2,1)S(1)} %collective-permute-done.2.b0, ...), custom_call_target="tpu_custom_call", output_to_operand_aliasing={{0}: (7, {})} | custom-call | flops 7864320 | bytes 7864320 | tf_op jit(solution)/shard_map/settle/pallas_call | solution.py:161
  335.8 8.4 %collective-permute-done.10.c0 = bf16[128,2560]{1,0:T(8,128)(2,1)S(1)} collective-permute-done((bf16[128,2560]{1,0:T(8,128)(2,1)S(1)}, bf16[128,2560]{1,0:T(8,128)(2,1)S(1)}, u32[]{:S(2)}, u32[]{:S(2)}) %collective-permute-start.10) | collective-permute-done | bytes 655392 | tf_op jit(solution)/shard_map/ppermute | solution.py:410
  344.2 2.3 settle.5
  347.9 4.4 %weigh.1 = (f32[1,2560]{1,0:T(1,128)}, f32[1,2560]{1,0:T(1,128)S(1)}, f32[1,4224]{1,0:T(1,128)S(1)}) custom-call(bf16[2048,2560]{1,0:T(8,128)(2,1)S(1)} %get-tuple-element.97.g_ref._, f32[1,2560]{1,0:T(1,128)S(1)} %get-tuple-element.98.refs_0_, f32[1,2560]{1,0:T(1,128)S(1)} %collective-permute-done.14.refs_1_, f32[1,2560]{1,0:T(1,128)S(1)} %copy-done.2, ...), custom_call_target="tpu_custom_call" | custom-call | flops 20971520 | bytes 10485760 | tf_op jit(solution)/shard_map/weigh/pallas_call | solution.py:261
  352.3 3.6 collective-permute-start.17
  357.8 2.7 collective-permute-done.16.refs_2_
  362.4 11.0 %finish.1 = (bf16[2048,2560]{1,0:T(8,128)(2,1)S(1)}, f32[512,2560]{1,0:T(8,128)S(1)}, f32[512,2560]{1,0:T(8,128)S(1)}, f32[512,2560]{1,0:T(8,128)S(1)}, f32[512,...) custom-call(bf16[2048,2560]{1,0:T(8,128)(2,1)S(1)} %get-tuple-elemen, ...), custom_call_target="tpu_custom_call", output_to_operand_aliasing={{0}: (0, {}), {1}: (3, {}), {2}: (4, {}), {3}: (5, {}), {4}... | custom-call | flops 31457280 | bytes 62914560 | tf_op jit(solution)/shard_map/finish/pallas_call | solution.py:372
  (44 shorter events, 11.8 us)
Async XLA Ops:
  2.0 18.6 %collective-permute-start.4 = (bf16[128,2560]{1,0:T(8,128)(2,1)S(1)}, bf16[128,2560]{1,0:T(8,128)(2,1)S(1)}, u32[]{:S(2)}, u32[]{:S(2)}) collective-permute-start(bf16[128,2560]{1,0:T(8,128)(2,1)S(1)} %get-tuple-element.60), channel_id=1, source_target_pairs={{0,8},{8,0},{16,24},{24,16},{1,9},{9,1},{17,25},{25,17},{2,10},{10... | collective-permute-start | bytes 1966088 | tf_op jit(solution)/shard_map/ppermute | solution.py:410
  5.0 17.7 %collective-permute-start.5 = (bf16[128,2560]{1,0:T(8,128)(2,1)S(1)}, bf16[128,2560]{1,0:T(8,128)(2,1)S(1)}, u32[]{:S(2)}, u32[]{:S(2)}) collective-permute-start(bf16[128,2560]{1,0:T(8,128)(2,1)S(1)} %get-tuple-element.61), channel_id=1, source_target_pairs={{0,16},{8,24},{16,0},{24,8},{1,17},{9,25},{17,1},{25,9},{2,18},{10... | collective-permute-start | bytes 1966088 | tf_op jit(solution)/shard_map/ppermute | solution.py:410
  8.3 40.3 %collective-permute-start = (bf16[256,2560]{1,0:T(8,128)(2,1)S(1)}, bf16[256,2560]{1,0:T(8,128)(2,1)S(1)}, u32[]{:S(2)}, u32[]{:S(2)}) collective-permute-start(bf16[256,2560]{1,0:T(8,128)(2,1)S(1)} %get-tuple-element.63), channel_id=1, source_target_pairs={{0,8},{8,0},{16,24},{24,16},{1,9},{9,1},{17,25},{25,17},{2,10},{10... | collective-permute-start | bytes 3932168 | tf_op jit(solution)/shard_map/ppermute | solution.py:410
  8.9 41.8 %collective-permute-start.1 = (bf16[256,2560]{1,0:T(8,128)(2,1)S(1)}, bf16[256,2560]{1,0:T(8,128)(2,1)S(1)}, u32[]{:S(2)}, u32[]{:S(2)}) collective-permute-start(bf16[256,2560]{1,0:T(8,128)(2,1)S(1)} %get-tuple-element.64), channel_id=1, source_target_pairs={{0,16},{8,24},{16,0},{24,8},{1,17},{9,25},{17,1},{25,9},{2,18},{10... | collective-permute-start | bytes 3932168 | tf_op jit(solution)/shard_map/ppermute | solution.py:410
  22.7 96.2 %collective-permute-start.6 = (bf16[640,2560]{1,0:T(8,128)(2,1)S(1)}, bf16[640,2560]{1,0:T(8,128)(2,1)S(1)}, u32[]{:S(2)}, u32[]{:S(2)}) collective-permute-start(bf16[640,2560]{1,0:T(8,128)(2,1)S(1)} %get-tuple-element.73), channel_id=1, source_target_pairs={{0,8},{8,0},{16,24},{24,16},{1,9},{9,1},{17,25},{25,17},{2,10},{10... | collective-permute-start | bytes 9830408 | tf_op jit(solution)/shard_map/ppermute | solution.py:410
  22.7 98.3 %collective-permute-start.7 = (bf16[640,2560]{1,0:T(8,128)(2,1)S(1)}, bf16[640,2560]{1,0:T(8,128)(2,1)S(1)}, u32[]{:S(2)}, u32[]{:S(2)}) collective-permute-start(bf16[640,2560]{1,0:T(8,128)(2,1)S(1)} %get-tuple-element.74), channel_id=1, source_target_pairs={{0,16},{8,24},{16,0},{24,8},{1,17},{9,25},{17,1},{25,9},{2,18},{10... | collective-permute-start | bytes 9830408 | tf_op jit(solution)/shard_map/ppermute | solution.py:410
  50.8 180.5 %collective-permute-start.2 = (bf16[1024,2560]{1,0:T(8,128)(2,1)S(1)}, bf16[1024,2560]{1,0:T(8,128)(2,1)S(1)}, u32[]{:S(2)}, u32[]{:S(2)}) collective-permute-start(bf16[1024,2560]{1,0:T(8,128)(2,1)S(1)} %get-tuple-element.71), channel_id=1, source_target_pairs={{0,8},{8,0},{16,24},{24,16},{1,9},{9,1},{17,25},{25,17},{2,10},{10... | collective-permute-start | bytes 15728648 | tf_op jit(solution)/shard_map/ppermute | solution.py:410
  50.8 182.5 %collective-permute-start.3 = (bf16[1024,2560]{1,0:T(8,128)(2,1)S(1)}, bf16[1024,2560]{1,0:T(8,128)(2,1)S(1)}, u32[]{:S(2)}, u32[]{:S(2)}) collective-permute-start(bf16[1024,2560]{1,0:T(8,128)(2,1)S(1)} %get-tuple-element.72), channel_id=1, source_target_pairs={{0,16},{8,24},{16,0},{24,8},{1,17},{9,25},{17,1},{25,9},{2,18},{10... | collective-permute-start | bytes 15728648 | tf_op jit(solution)/shard_map/ppermute | solution.py:410
  126.0 177.6 %collective-permute-start.8 = (bf16[640,2560]{1,0:T(8,128)(2,1)S(1)}, bf16[640,2560]{1,0:T(8,128)(2,1)S(1)}, u32[]{:S(2)}, u32[]{:S(2)}) collective-permute-start(bf16[640,2560]{1,0:T(8,128)(2,1)S(1)} %get-tuple-element.87), channel_id=1, source_target_pairs={{0,16},{8,24},{16,0},{24,8},{1,17},{9,25},{17,1},{25,9},{2,18},{10... | collective-permute-start | bytes 9830408 | tf_op jit(solution)/shard_map/ppermute | solution.py:410
  127.5 176.0 %collective-permute-start.9 = (bf16[640,2560]{1,0:T(8,128)(2,1)S(1)}, bf16[640,2560]{1,0:T(8,128)(2,1)S(1)}, u32[]{:S(2)}, u32[]{:S(2)}) collective-permute-start(bf16[640,2560]{1,0:T(8,128)(2,1)S(1)} %get-tuple-element.88), channel_id=1, source_target_pairs={{0,8},{8,0},{16,24},{24,16},{1,9},{9,1},{17,25},{25,17},{2,10},{10... | collective-permute-start | bytes 9830408 | tf_op jit(solution)/shard_map/ppermute | solution.py:410
  233.3 98.3 %collective-permute-start.12 = (bf16[256,2560]{1,0:T(8,128)(2,1)S(1)}, bf16[256,2560]{1,0:T(8,128)(2,1)S(1)}, u32[]{:S(2)}, u32[]{:S(2)}) collective-permute-start(bf16[256,2560]{1,0:T(8,128)(2,1)S(1)} %get-tuple-element.91), channel_id=1, source_target_pairs={{0,16},{8,24},{16,0},{24,8},{1,17},{9,25},{17,1},{25,9},{2,18},{10... | collective-permute-start | bytes 3932168 | tf_op jit(solution)/shard_map/ppermute | solution.py:410
  234.9 96.8 %collective-permute-start.13 = (bf16[256,2560]{1,0:T(8,128)(2,1)S(1)}, bf16[256,2560]{1,0:T(8,128)(2,1)S(1)}, u32[]{:S(2)}, u32[]{:S(2)}) collective-permute-start(bf16[256,2560]{1,0:T(8,128)(2,1)S(1)} %get-tuple-element.92), channel_id=1, source_target_pairs={{0,8},{8,0},{16,24},{24,16},{1,9},{9,1},{17,25},{25,17},{2,10},{10... | collective-permute-start | bytes 3932168 | tf_op jit(solution)/shard_map/ppermute | solution.py:410
  303.6 40.7 %collective-permute-start.10 = (bf16[128,2560]{1,0:T(8,128)(2,1)S(1)}, bf16[128,2560]{1,0:T(8,128)(2,1)S(1)}, u32[]{:S(2)}, u32[]{:S(2)}) collective-permute-start(bf16[128,2560]{1,0:T(8,128)(2,1)S(1)} %get-tuple-element.89), channel_id=1, source_target_pairs={{0,16},{8,24},{16,0},{24,8},{1,17},{9,25},{17,1},{25,9},{2,18},{10... | collective-permute-start | bytes 1966088 | tf_op jit(solution)/shard_map/ppermute | solution.py:410
  305.1 39.1 %collective-permute-start.11 = (bf16[128,2560]{1,0:T(8,128)(2,1)S(1)}, bf16[128,2560]{1,0:T(8,128)(2,1)S(1)}, u32[]{:S(2)}, u32[]{:S(2)}) collective-permute-start(bf16[128,2560]{1,0:T(8,128)(2,1)S(1)} %get-tuple-element.90), channel_id=1, source_target_pairs={{0,8},{8,0},{16,24},{24,16},{1,9},{9,1},{17,25},{25,17},{2,10},{10... | collective-permute-start | bytes 1966088 | tf_op jit(solution)/shard_map/ppermute | solution.py:410
  321.8 2.4 copy-start
  324.1 2.4 copy-start.1
  331.7 30.7 %slice-start = ((s8[5242880]{0:T(1024)(128)(4,1)}), s8[4194304]{0:T(1024)(128)(4,1)S(1)}, s32[]{:S(2)}) async-start(s8[5242880]{0:T(1024)(128)(4,1)} %bitcast.5), calls=%async_computation | async-start | bytes 8388608
  331.7 30.7 %slice-start.2 = ((s8[5242880]{0:T(1024)(128)(4,1)}), s8[1048576]{0:T(1024)(128)(4,1)S(1)}, s32[]{:S(2)}) async-start(s8[5242880]{0:T(1024)(128)(4,1)} %bitcast.7), calls=%async_computation.2 | async-start | bytes 2097152
  344.2 3.6 copy-start.2
  344.2 18.1 %slice-start.1 = ((s8[5242880]{0:T(1024)(128)(4,1)}), s8[1048576]{0:T(1024)(128)(4,1)S(1)}, s32[]{:S(2)}) async-start(s8[5242880]{0:T(1024)(128)(4,1)} %bitcast.5), calls=%async_computation.1 | async-start | bytes 2097152
  344.2 18.1 %slice-start.3 = ((s8[5242880]{0:T(1024)(128)(4,1)}), s8[4194304]{0:T(1024)(128)(4,1)S(1)}, s32[]{:S(2)}) async-start(s8[5242880]{0:T(1024)(128)(4,1)} %bitcast.7), calls=%async_computation.3 | async-start | bytes 8388608
  346.6 1.2 collective-permute-start.14
  347.9 12.7 %copy-start.3 = (f32[1,2048]{1,0:T(1,128)S(1)}, f32[1,2048]{1,0:T(1,128)}, u32[]{:S(2)}) copy-start(f32[1,2048]{1,0:T(1,128)} %refs_4_.1) | copy-start | bytes 24580
  352.3 5.5 %collective-permute-start.17 = (f32[1,4224]{1,0:T(1,128)S(1)}, f32[1,4224]{1,0:T(1,128)S(1)}, u32[]{:S(2)}, u32[]{:S(2)}) collective-permute-start(f32[1,4224]{1,0:T(1,128)S(1)} %get-tuple-element.104.refs_0_), channel_id=1, source_target_pairs={{0,3},{1,2},{2,1},{3,0},{4,7},{5,6},{6,5},{7,4},{8,11},{9,10},{10,... | collective-permute-start | bytes 50696 | tf_op jit(solution)/shard_map/ppermute | solution.py:388
  355.9 4.6 %collective-permute-start.16 = (f32[1,4224]{1,0:T(1,128)S(1)}, f32[1,4224]{1,0:T(1,128)S(1)}, u32[]{:S(2)}, u32[]{:S(2)}) collective-permute-start(f32[1,4224]{1,0:T(1,128)S(1)} %get-tuple-element.104.refs_0_), channel_id=1, source_target_pairs={{0,2},{1,3},{2,0},{3,1},{4,6},{5,7},{6,4},{7,5},{8,10},{9,11},{10,... | collective-permute-start | bytes 50696 | tf_op jit(solution)/shard_map/ppermute | solution.py:388
  355.9 4.6 %collective-permute-start.15 = (f32[1,4224]{1,0:T(1,128)S(1)}, f32[1,4224]{1,0:T(1,128)S(1)}, u32[]{:S(2)}, u32[]{:S(2)}) collective-permute-start(f32[1,4224]{1,0:T(1,128)S(1)} %get-tuple-element.104.refs_0_), channel_id=1, source_target_pairs={{0,1},{1,0},{2,3},{3,2},{4,5},{5,4},{6,7},{7,6},{8,9},{9,8},{10,11... | collective-permute-start | bytes 50696 | tf_op jit(solution)/shard_map/ppermute | solution.py:388
  361.2 1.2 collective-permute-start.18

commit v3 on v2

--- a/solution.py
+++ b/solution.py
@@ -65,31 +65,74 @@
     )(me, *[parts] * len(wants))
 
 
-def merge(parts, me, got, at, offset, size):
+def grab(parts, wants, size):
+    columns = parts.shape[2]
+    n = len(wants)
+
+    def kernel(parts_ref, *refs):
+        outs, sems = refs[:n], refs[n]
+        me = lax.axis_index("dp")
+        copies = []
+        for i, (flip, start) in enumerate(wants):
+            copies.append(pltpu.make_async_copy(parts_ref.at[me ^ flip, pl.ds(start, size)], outs[i], sems.at[i]))
+            copies[-1].start()
+        for copy in copies:
+            copy.wait()
+
+    return pl.pallas_call(
+        kernel,
+        in_specs=[anywhere],
+        out_specs=[whole_vmem] * n,
+        out_shape=[pltpu.VMEM((size, columns), parts.dtype)] * n,
+        scratch_shapes=[pltpu.SemaphoreType.DMA((n,))],
+        compiler_params=params_of(MIB),
+        name="grab",
+    )(parts)
+
+
+def merge(parts, me, got, at, offset, size, lead=()):
     columns = parts.shape[2]
     half = parts.shape[1] // 2
-
-    def kernel(me_ref, a0, a1, b0, b1, o0, o1):
-        o0[...] = (a0[...].astype(jnp.float32) + b0[...].astype(jnp.float32)).astype(o0.dtype)
-        o1[...] = (a1[...].astype(jnp.float32) + b1[...].astype(jnp.float32)).astype(o1.dtype)
+    skip = 1 if lead else 0
+
+    def add(o, a, b):
+        o[...] = (a[...].astype(jnp.float32) + b[...].astype(jnp.float32)).astype(o.dtype)
+
+    def kernel(me_ref, a0, a1, *refs):
+        (o0, o1), refs = refs[-2:], refs[:-2]
+        t = pl.program_id(0)
+
+        @pl.when(t >= skip)
+        def _():
+            add(o0, a0, refs[-2])
+            add(o1, a1, refs[-1])
+
+        if lead:
+
+            @pl.when(t == 0)
+            def _():
+                add(o0, a0, refs[0])
+                add(o1, a1, refs[1])
 
     def own(h):
         return pl.BlockSpec((None, TILE, columns), lambda t, m: (m[0] ^ FAR[h], (h * half + at) // TILE + t, 0))
 
-    came = pl.BlockSpec((TILE, columns), lambda t, m: ((at - offset) // TILE + t, 0))
+    first = at // TILE + skip - offset // TILE
+    came = pl.BlockSpec((TILE, columns), lambda t, m: (first + jnp.maximum(t - skip, 0), 0))
+    ahead = pl.BlockSpec((TILE, columns), lambda t, m: (0, 0))
     return pl.pallas_call(
         kernel,
         grid_spec=pltpu.PrefetchScalarGridSpec(
             num_scalar_prefetch=1,
             grid=(size // TILE,),
-            in_specs=[own(0), own(1), came, came],
+            in_specs=[own(0), own(1)] + [ahead] * len(lead) + [came, came],
             out_specs=[pl.BlockSpec((TILE, columns), lambda t, m: (t, 0))] * 2,
         ),
         out_shape=[jax.ShapeDtypeStruct((size, columns), parts.dtype)] * 2,
-        compiler_params=params_of(9 * MIB),
+        compiler_params=params_of(12 * MIB),
         cost_estimate=cost(2 * size * columns, 12 * size * columns),
         name="merge",
-    )(me, parts, parts, *got)
+    )(me, parts, parts, *lead, *got)
 
 
 def lane_sums(x):
@@ -141,7 +184,7 @@
             for h in range(2):
                 for q in range(size // LANES):
                     lanes = slice(q * LANES, (q + 1) * LANES)
-                    row_ref[h : h + 1, lanes] = lane_sums(sums_ref[h, lanes, :])
+                    row_ref[:, h * size + q * LANES : h * size + (q + 1) * LANES] = lane_sums(sums_ref[h, lanes, :])
             col_ref[...] = jnp.sum(carry_ref[...], axis=0, keepdims=True)
             if state is not None:
                 col_ref[...] = col_ref[...] + before_ref[...]
@@ -170,13 +213,140 @@
         out_shape=[
             pltpu.VMEM((rows, columns), parts.dtype),
             jax.ShapeDtypeStruct((1, columns), jnp.float32),
-            jax.ShapeDtypeStruct((2, size), jnp.float32),
+            jax.ShapeDtypeStruct((1, 2 * size), jnp.float32),
         ],
         input_output_aliases=aliases,
         compiler_params=params_of(7 * MIB),
         cost_estimate=cost(12 * size * columns, 12 * size * columns),
         name="settle",
     )(me, *operands)
+
+
+def presum(parts, me, second, at, size):
+    columns = parts.shape[2]
+    half = parts.shape[1] // 2
+    step = min(64, size)
+
+    def kernel(me_ref, a0, a1, b0, b1, o_ref):
+        t = pl.program_id(0)
+        for h, (a, b) in enumerate(((a0, b0), (a1, b1))):
+            here = pl.ds(pl.multiple_of(h * size + t * step, step), step)
+            o_ref[here, :] = a[...].astype(jnp.float32) + b[...].astype(jnp.float32)
+
+    def own(h):
+        return pl.BlockSpec((None, step, columns), lambda t, m: (m[0], (h * half + at) // step + t, 0))
+
+    inside = pl.BlockSpec((step, columns), lambda t, m: (at // step + t, 0))
+    return pl.pallas_call(
+        kernel,
+        grid_spec=pltpu.PrefetchScalarGridSpec(
+            num_scalar_prefetch=1,
+            grid=(size // step,),
+            in_specs=[own(0), own(1), inside, inside],
+            out_specs=whole_vmem,
+        ),
+        out_shape=pltpu.VMEM((2 * size, columns), jnp.float32),
+        compiler_params=params_of(6 * MIB),
+        cost_estimate=cost(2 * size * columns, 16 * size * columns),
+        name="presum",
+    )(me, parts, parts, *second)
+
+
+def close(base, third, at, gradient, col_sums):
+    rows, columns = gradient.shape
+    half = rows // 2
+    size = base.shape[0] // 2
+    chunks = columns // LANES
+
+    def kernel(base_ref, c0, c1, _, before_ref, g_ref, col_ref, row_ref, sums_ref):
+        carry = tuple(jnp.zeros((8, LANES), jnp.float32) for _ in range(chunks))
+        for h, c in enumerate((c0, c1)):
+
+            def body(r, carry):
+                here = pl.ds(pl.multiple_of(r * GROUP, GROUP), GROUP)
+                there = pl.ds(pl.multiple_of(h * size + r * GROUP, GROUP), GROUP)
+                kept = pl.ds(pl.multiple_of(h * half + at + r * GROUP, GROUP), GROUP)
+                across = jnp.zeros((GROUP, LANES), jnp.float32)
+                down = []
+                for k in range(chunks):
+                    lanes = slice(k * LANES, (k + 1) * LANES)
+                    total = base_ref[there, lanes] + c[here, lanes].astype(jnp.float32)
+                    g_ref[kept, lanes] = total.astype(g_ref.dtype)
+                    square = total * total
+                    across = across + square
+                    down.append(carry[k] + square[:8] + square[8:])
+                sums_ref[there, :] = across
+                return tuple(down)
+
+            carry = lax.fori_loop(0, size // GROUP, body, carry)
+        for k in range(chunks):
+            lanes = slice(k * LANES, (k + 1) * LANES)
+            col_ref[:, lanes] = before_ref[:, lanes] + jnp.sum(carry[k], axis=0, keepdims=True)
+        for q in range(2 * size // LANES):
+            lanes = slice(q * LANES, (q + 1) * LANES)
+            row_ref[:, lanes] = lane_sums(sums_ref[lanes, :])
+
+    return pl.pallas_call(
+        kernel,
+        in_specs=[whole_vmem] * 3 + [anywhere, whole_vmem],
+        out_specs=[whole_vmem] * 3,
+        out_shape=[
+            pltpu.VMEM((rows, columns), gradient.dtype),
+            jax.ShapeDtypeStruct((1, columns), jnp.float32),
+            jax.ShapeDtypeStruct((1, 2 * size), jnp.float32),
+        ],
+        input_output_aliases={3: 0},
+        scratch_shapes=[pltpu.VMEM((2 * size, LANES), jnp.float32)],
+        compiler_params=params_of(4 * MIB),
+        cost_estimate=cost(10 * size * columns, 12 * size * columns),
+        name="close",
+    )(base, *third, gradient, col_sums)
+
+
+def early(gradient, messages, row_moment, at, size):
+    rows, columns = gradient.shape
+    half = rows // 2
+    chunks = columns // LANES
+    n = len(messages)
+
+    def kernel(g_ref, moment_ref, *refs):
+        got, (new_ref, out_ref, root_ref, acc_ref) = refs[:n], refs[n:]
+        total = tree([m[...] for m in got])
+        for h in range(2):
+            here = slice(h * size, (h + 1) * size)
+            moment = moment_ref[:, h * half + at : h * half + at + size]
+            new_ref[:, here] = DECAY * moment + (1.0 - DECAY) * (total[:, here] + FF * EPSILON) / FF
+        root_ref[...] = lax.rsqrt(new_ref[...])
+        acc_ref[...] = jnp.zeros_like(acc_ref)
+        for h in range(2):
+
+            def body(t, carry):
+                lanes = root_ref[:, pl.ds(pl.multiple_of(h * size + t * TILE, TILE), TILE)]
+                wide = jnp.broadcast_to(lanes, (LANES, TILE)).T
+                for k in range(chunks):
+                    at_lanes = slice(k * LANES, (k + 1) * LANES)
+                    here = pl.ds(pl.multiple_of(h * half + at + t * TILE, TILE), TILE)
+                    g = g_ref[here, at_lanes].astype(jnp.float32) * wide
+                    square = g * g
+                    acc_ref[:, at_lanes] += sum(square[i : i + 8] for i in range(8, TILE, 8)) + square[:8]
+                return carry
+
+            lax.fori_loop(0, size // TILE, body, 0)
+        out_ref[...] = jnp.sum(acc_ref[...], axis=0, keepdims=True)
+
+    return pl.pallas_call(
+        kernel,
+        in_specs=[whole_vmem] * (n + 2),
+        out_specs=[whole_vmem] * 2,
+        out_shape=[
+            jax.ShapeDtypeStruct((1, 2 * size), jnp.float32),
+            jax.ShapeDtypeStruct((1, columns), jnp.float32),
+        ],
+        scratch_shapes=[pltpu.VMEM((1, 2 * size), jnp.float32), pltpu.VMEM((8, columns), jnp.float32)],
+        compiler_params=params_of(4 * MIB),
+        cost_estimate=cost(8 * size * columns, 4 * size * columns),
+        name="early",
+    )(gradient, row_moment, *messages)
 
 
 def power_of(params):
@@ -226,75 +396,91 @@
     return values[0]
 
 
-def weigh(gradient, col_sums, col_moment, row_sums, power):
+def weigh(gradient, col_sums, col_moment, row_pieces, early_sums, power, late):
     rows, columns = gradient.shape
+    half = rows // 2
     chunks = columns // LANES
     n = len(col_sums)
+    places = sorted(row_pieces)
+    group = 4 * GROUP
 
     def kernel(g_ref, *refs):
-        sums, (moment_ref, row_ref, power_ref, new_ref, root_ref, out_ref, wide_ref, acc_ref) = refs[:n], refs[n:]
+        sums, refs = refs[:n], refs[n:]
+        row_refs, refs = refs[: len(places)], refs[len(places) :]
+        moment_ref, early_ref, power_ref, new_ref, root_ref, out_ref, wide_ref, acc_ref = refs
         total = tree([s[...] for s in sums]) + D * EPSILON
         new = DECAY * moment_ref[...] + (1.0 - DECAY) * total / D
         new_ref[...] = new
         root = lax.rsqrt(new)
         root_ref[...] = root
         wide_ref[...] = jnp.broadcast_to(root, wide_ref.shape)
-        out_ref[:, :rows] = row_ref[...]
-        out_ref[:, 2 * rows :] = jnp.sum(power_ref[...], axis=0, keepdims=True)
-        roots = [wide_ref[:, k * LANES : (k + 1) * LANES] for k in range(chunks)]
-
-        def body(r, carry):
-            here = pl.ds(pl.multiple_of(r * GROUP, GROUP), GROUP)
-            low = jnp.zeros((8, LANES), jnp.float32)
-            high = jnp.zeros((8, LANES), jnp.float32)
-            for k in range(chunks):
-                g = g_ref[here, k * LANES : (k + 1) * LANES].astype(jnp.float32)
-                a, b = g[:8] * roots[k], g[8:] * roots[k]
-                low, high = low + a * a, high + b * b
-            acc_ref[here, :] = jnp.concatenate([low, high], axis=0)
-            return carry
-
-        lax.fori_loop(0, rows // GROUP, body, 0)
-        for q in range(rows // LANES):
-            out_ref[:, rows + q * LANES : rows + (q + 1) * LANES] = lane_sums(acc_ref[q * LANES : (q + 1) * LANES, :])
-
-    return pl.pallas_call(
-        kernel,
-        in_specs=[whole_vmem] * (n + 4),
+        for at, row_ref in zip(places, row_refs):
+            size = row_ref.shape[1] // 2
+            for h in range(2):
+                out_ref[:, h * late + at : h * late + at + size] = row_ref[:, h * size : (h + 1) * size]
+        out_ref[:, 4 * late : 4 * late + LANES] = tree_lanes(early_ref[...] * (root * root), columns)
+        out_ref[:, 4 * late + LANES :] = jnp.sum(power_ref[...], axis=0, keepdims=True)
+        for h in range(2):
+
+            def body(r, carry):
+                here = pl.ds(pl.multiple_of(h * half + r * group, group), group)
+                total = jnp.zeros((group, LANES), jnp.float32)
+                for k in range(chunks):
+                    lanes = slice(k * LANES, (k + 1) * LANES)
+                    g = g_ref[here, lanes].astype(jnp.float32)
+                    w = wide_ref[:, lanes]
+                    g = jnp.concatenate([g[i : i + 8] * w for i in range(0, group, 8)], axis=0)
+                    total = total + g * g
+                acc_ref[pl.ds(pl.multiple_of(h * late + r * group, group), group), :] = total
+                return carry
+
+            lax.fori_loop(0, late // group, body, 0)
+        for q in range(2 * late // LANES):
+            lanes = slice(2 * late + q * LANES, 2 * late + (q + 1) * LANES)
+            out_ref[:, lanes] = lane_sums(acc_ref[q * LANES : (q + 1) * LANES, :])
+
+    return pl.pallas_call(
+        kernel,
+        in_specs=[whole_vmem] * (n + len(places) + 4),
         out_specs=[whole_vmem] * 3,
         out_shape=[
             jax.ShapeDtypeStruct((1, columns), jnp.float32),
             jax.ShapeDtypeStruct((1, columns), jnp.float32),
-            jax.ShapeDtypeStruct((1, 2 * rows + LANES), jnp.float32),
+            jax.ShapeDtypeStruct((1, 4 * late + 2 * LANES), jnp.float32),
         ],
-        scratch_shapes=[pltpu.VMEM((8, columns), jnp.float32), pltpu.VMEM((rows, LANES), jnp.float32)],
-        compiler_params=params_of(8 * MIB),
-        cost_estimate=cost(4 * rows * columns, 2 * rows * columns),
+        scratch_shapes=[pltpu.VMEM((8, columns), jnp.float32), pltpu.VMEM((2 * late, LANES), jnp.float32)],
+        compiler_params=params_of(4 * MIB),
+        cost_estimate=cost(8 * late * columns, 4 * late * columns),
         name="weigh",
-    )(gradient, *col_sums, col_moment, row_sums, power)
-
-
-def balance(messages, row_moment):
+    )(gradient, *col_sums, *[row_pieces[at] for at in places], col_moment, early_sums, power)
+
+
+def balance(messages, row_moment, new_early, late):
     rows = row_moment.shape[1]
+    half = rows // 2
+    first = half - late
     n = len(messages)
 
     def kernel(*refs):
-        got, (moment_ref, new_ref, root_ref, out_ref) = refs[:n], refs[n:]
+        got, (moment_ref, early_ref, new_ref, root_ref, out_ref) = refs[:n], refs[n:]
         total = tree([m[...] for m in got])
-        new = DECAY * moment_ref[...] + (1.0 - DECAY) * (total[:, :rows] + FF * EPSILON) / FF
-        new_ref[...] = new
-        root = lax.rsqrt(new)
-        root_ref[...] = root
-        ratio = total[:, rows : 2 * rows] * (root * root)
-        fold = lambda x: tree_lanes(x, rows)
+        ratio = jnp.zeros((1, LANES), jnp.float32)
+        for h in range(2):
+            here = slice(h * half, h * half + late)
+            there = slice(h * late, (h + 1) * late)
+            new = DECAY * moment_ref[:, here] + (1.0 - DECAY) * (total[:, there] + FF * EPSILON) / FF
+            new_ref[:, here] = new
+            new_ref[:, h * half + late : (h + 1) * half] = early_ref[:, h * first : (h + 1) * first]
+            ratio = ratio + tree_lanes(total[:, (2 + h) * late : (3 + h) * late] / new, late)
+        root_ref[...] = lax.rsqrt(new_ref[...])
         out_ref[...] = jnp.zeros_like(out_ref)
-        out_ref[0:1, :] = fold(ratio)
-        out_ref[1:2, :] = fold(new)
-        out_ref[2:3, :] = total[:, 2 * rows :]
-
-    return pl.pallas_call(
-        kernel,
-        in_specs=[whole_vmem] * (n + 1),
+        out_ref[0:1, :] = ratio + total[:, 4 * late : 4 * late + LANES]
+        out_ref[1:2, :] = tree_lanes(new_ref[...], rows)
+        out_ref[2:3, :] = total[:, 4 * late + LANES :]
+
+    return pl.pallas_call(
+        kernel,
+        in_specs=[whole_vmem] * (n + 2),
         out_specs=[whole_vmem] * 3,
         out_shape=[
             jax.ShapeDtypeStruct((1, rows), jnp.float32),
@@ -303,7 +489,7 @@
         ],
         compiler_params=params_of(4 * MIB),
         name="balance",
-    )(*messages, row_moment)
+    )(*messages, row_moment, new_early)
 
 
 def tree_lanes(x, rows):
@@ -390,12 +576,12 @@
 
 def cut(half):
     units = half // TILE
-    sizes = [1, 2, units - 3] if units > 3 else [1, units - 1] if units > 1 else [units]
-    edges, at = [], 0
-    for n in sizes:
-        edges.append((at, n * TILE))
-        at += n * TILE
-    return edges
+    late = 2 if units > 3 else 1
+    first = (units - late + 1) // 2 if units > 3 else units - late
+    edges = [((units - first) * TILE, first * TILE)]
+    if units - first > late:
+        edges.append((late * TILE, (units - first - late) * TILE))
+    return edges + [(0, late * TILE)]
 
 
 def after(values, others):
@@ -417,6 +603,7 @@
 
         held = in_hbm(parts)
         pieces = cut(half)
+        late = pieces[-1][1]
         rounds = []
 
         def send(values, lines):
@@ -425,29 +612,40 @@
             rounds.append(hop(values, lines))
             return rounds[-1]
 
-        first, turn = [], me
+        picked = grab(held, [(3, 0), (3, half)], TILE)
+        (turn,) = after([me], picked)
+        head = send(picked, NEAR)
+        picked = pick(held, turn, [(3, TILE), (3, half + TILE)], half - TILE)
+        (turn,) = after([me], picked)
+        rest = send(picked, NEAR)
+        second = send(pick(held, turn, [(NEAR[0], 0), (NEAR[1], half)], half), NEAR)
+
+        third, done = [], []
         for at, size in pieces:
-            picked = pick(held, turn, [(3, at), (3, half + at)], size)
-            (turn,) = after([me], picked)
-            first.append(send(picked, NEAR))
-        second = send(pick(held, turn, [(NEAR[0], 0), (NEAR[1], half)], half), NEAR)
-        pieces.reverse()
-        third, done = [], []
-        for (at, size), came in zip(pieces, reversed(first)):
-            done = merge(held, me, after(came, done), at, at, size)
+            if at:
+                done = merge(held, me, after(rest, done), at, TILE, size)
+            elif size == TILE:
+                done = merge(held, me, after(head, done), 0, 0, size)
+            else:
+                done = merge(held, me, after(rest, done), 0, TILE, size, after(head, done))
             third.append(send(done, FAR))
 
         state, row_pieces = None, {}
-        for (at, size), came in zip(pieces, third):
-            gradient, col_sums, row_piece = settle(held, me, second, came, at, size, state, min(64, size))
-            if state is None:
-                kept, power = power_of(after([params[0]], [col_sums])[0])
-            state = [gradient, col_sums]
-            row_pieces[at] = row_piece
-        row_sums = jnp.concatenate([row_pieces[at][h : h + 1] for h in range(2) for at in sorted(row_pieces)], axis=1)
-
-        new_col, col_root, message = weigh(gradient, all_parts(col_sums, "row", across), col_moment, row_sums, power)
-        new_row, row_root, stats = balance(all_parts(message, "col", along), row_moment)
+        for i, ((at, size), came) in enumerate(zip(pieces[:-1], third)):
+            if i + 2 == len(pieces):
+                kept, power = power_of(after([params[0]], state[1:] if state else second)[0])
+                base = presum(held, me, second, 0, late)
+                came = after(came, [*kept, base])
+            *state, row_pieces[at] = settle(held, me, second, came, at, size, state, 64)
+        message = jnp.concatenate(
+            [row_pieces[at][:, h * size : (h + 1) * size] for h in range(2) for at, size in sorted(pieces[:-1])], axis=1
+        )
+        new_early, early_sums = early(state[0], all_parts(message, "col", along), row_moment, late, half - late)
+        gradient, col_sums, late_rows = close(base, third[-1], 0, *state)
+
+        col_parts = all_parts(col_sums, "row", across)
+        new_col, col_root, message = weigh(gradient, col_parts, col_moment, {0: late_rows}, early_sums, power, late)
+        new_row, row_root, stats = balance(all_parts(message, "col", along), row_moment, new_early, late)
         new_params, update = finish(gradient, kept, row_root, col_root, all_parts(stats, "row", across))
         return new_params[None], update[None], new_row, new_col
 

time: 374 us -> 370 us (0.989)
  waiting for transfers between devices: 287 us -> 276 us
    ppermute x14 -> x12, waiting for transfers between devices: 281 us -> 267 us  [hop(): lax.ppermute(v, 'dp', pairs(mesh.shape['dp'], n))]
    pallas_call x2 -> x6, Pallas kernels: 5.03 us -> 10.4 us  [the longest x1 2.96 us: early(): pl.pallas_call(kernel, in_specs=[whole_vmem] * (n + 2), out_specs=[whole_...]
    ppermute x5 -> x8, starting transfers between devices: 4.46 us -> 8.91 us  [all_parts(): lax.ppermute(value, axis, pairs(size, k))]
    pallas_call x3 -> x2, Pallas kernels: 15.1 us -> 10.8 us  [settle(): pl.pallas_call(kernel, grid_spec=pltpu.PrefetchScalarGridSpec(num_scalar_...]
    ppermute x5 -> x8, waiting for transfers between devices: 6.17 us -> 9.8 us  [all_parts(): lax.ppermute(value, axis, pairs(size, k))]
    ppermute x14 -> x12, starting transfers between devices: 15.5 us -> 13.5 us  [hop(): lax.ppermute(v, 'dp', pairs(mesh.shape['dp'], n))]
    pallas_call x4 -> x2, Pallas kernels: 13.7 us -> 12 us  [pick(): pl.pallas_call(kernel, grid_spec=pltpu.PrefetchScalarGridSpec(num_scalar_...]
  transfers between devices with their start and end apart: 19 -> 20, of which waited for: 15 -> 15; matrix products, arithmetic and copies ran while one was open for 0% -> 0% of each run, Pallas kernels for 11% -> 13%
where the time goes in v3:
time: 370 us; the launch traced here: 369 us
  waiting for transfers between devices  276 us (75%)
  Pallas kernels  62.5 us (17%)
  starting transfers between devices  22.4 us (6%)
  local copies, waits for them, and re-layouts  7.09 us (2%)
    ppermute x12, waiting for transfers between devices, hop(): lax.ppermute(v, 'dp', pairs(mesh.shape['dp'], n))  267 us
    ppermute x12, starting transfers between devices, hop(): lax.ppermute(v, 'dp', pairs(mesh.shape['dp'], n))  13.5 us
    pallas_call x2, Pallas kernels, pick(): pl.pallas_call(kernel, grid_spec=pltpu.PrefetchScalarGridSpec(num_scalar_...  12 us
    pallas_call x1, Pallas kernels, finish(): pl.pallas_call(kernel, in_specs=[anywhere, whole_vmem, whole_vmem] + [any...  11 us
    pallas_call x3, Pallas kernels, merge(): pl.pallas_call(kernel, grid_spec=pltpu.PrefetchScalarGridSpec(num_scalar_...  10.8 us
    pallas_call x2, Pallas kernels, settle(): pl.pallas_call(kernel, grid_spec=pltpu.PrefetchScalarGridSpec(num_scalar_...  10.8 us
    ppermute x8, waiting for transfers between devices, all_parts(): lax.ppermute(value, axis, pairs(size, k))  9.8 us
    ppermute x8, starting transfers between devices, all_parts(): lax.ppermute(value, axis, pairs(size, k))  8.91 us
  transfers between devices with their start and end apart: 20, of which 15 were waited for; matrix products, arithmetic and copies ran while one was open for 0% of the time, Pallas kernels for 13%

profile of v3, /device:TPU:0, one launch (start us, length us, event | category | flops | bytes accessed | tf_op | source)
XLA Modules:
  0.0 369.3 jit_solution(9100934050188913717)
XLA Ops:
  2.0 3.0 collective-permute-start
  5.0 1.5 collective-permute-start.1
  6.5 5.8 %pick.2 = (bf16[896,2560]{1,0:T(8,128)(2,1)S(1)}, bf16[896,2560]{1,0:T(8,128)(2,1)S(1)}) custom-call(s32[1]{0:T(128)} %bitcast.me_ref, bf16[4,2048,2560]{2,1,0:T(8,128)(2,1)} %bitcast.12, bf16[4,2048,2560]{2,1,0:T(8,128)(2,1)} %bitcast.13), custom_call_target="tpu_custom_call" | custom-call | bytes 18350080 | tf_op jit(solution)/shard_map/pick/pallas_call | solution.py:53
  12.9 6.2 %pick.3 = (bf16[1024,2560]{1,0:T(8,128)(2,1)S(1)}, bf16[1024,2560]{1,0:T(8,128)(2,1)S(1)}) custom-call(s32[1]{0:T(128)} %bitcast.me_ref, bf16[4,2048,2560]{2,1,0:T(8,128)(2,1)} %bitcast.14, bf16[4,2048,2560]{2,1,0:T(8,128)(2,1)} %bitcast.15), custom_call_target="tpu_custom_call" | custom-call | bytes 20971520 | tf_op jit(solution)/shard_map/pick/pallas_call | solution.py:53
  20.5 2.1 collective-permute-done.1.refs_1_
  22.7 2.0 collective-permute-start.3
  24.7 94.2 %collective-permute-done.4.refs_0_.refs_2_ = bf16[896,2560]{1,0:T(8,128)(2,1)S(1)} collective-permute-done((bf16[896,2560]{1,0:T(8,128)(2,1)S(1)}, bf16[896,2560]{1,0:T(8,128)(2,1)S(1)}, u32[]{:S(2)}, u32[]{:S(2)}) %collective-permute-start.4) | collective-permute-done | bytes 4587552 | tf_op jit(solution)/shard_map/ppermute | solution.py:596
  118.8 2.1 collective-permute-done.5.refs_1_.refs_3_
  120.9 3.3 merge.3
  124.2 1.6 collective-permute-start.6
  126.4 4.6 %merge.4 = (bf16[384,2560]{1,0:T(8,128)(2,1)}, bf16[384,2560]{1,0:T(8,128)(2,1)S(1)}) custom-call(s32[1]{0:T(128)} %bitcast.me_ref, bf16[4,2048,2560]{2,1,0:T(8,128)(2,1)} %bitcast.18, bf16[4,2048,2560]{2,1,0:T(8,128)(2,1)} %bitcast.19, bf16[896,2560]{1,0:T(8,128)(2,1)S(1)} %collective-permute-done.4.refs_0_.refs_2_, ...), custom_call_target="tpu_custom_call" | custom-call | flops 1966080 | bytes 11796480 | tf_op jit(solution)/shard_map/merge/pallas_call | solution.py:123
  130.9 100.2 %collective-permute-done.2.b0 = bf16[1024,2560]{1,0:T(8,128)(2,1)S(1)} collective-permute-done((bf16[1024,2560]{1,0:T(8,128)(2,1)S(1)}, bf16[1024,2560]{1,0:T(8,128)(2,1)S(1)}, u32[]{:S(2)}, u32[]{:S(2)}) %collective-permute-start.2) | collective-permute-done | bytes 5242912 | tf_op jit(solution)/shard_map/ppermute | solution.py:596
  231.2 2.1 collective-permute-done.3.b1
  233.3 1.5 collective-permute-start.10
  235.3 2.9 merge.5
  238.3 37.1 %collective-permute-done.6.c0 = bf16[384,2560]{1,0:T(8,128)(2,1)S(1)} collective-permute-done((bf16[384,2560]{1,0:T(8,128)(2,1)S(1)}, bf16[384,2560]{1,0:T(8,128)(2,1)S(1)}, u32[]{:S(2)}, u32[]{:S(2)}) %collective-permute-start.6) | collective-permute-done | bytes 1966112 | tf_op jit(solution)/shard_map/ppermute | solution.py:596
  275.4 1.5 collective-permute-start.8
  277.5 2.7 presum.1.base_ref
  280.2 5.4 %settle.2 = (bf16[2048,2560]{1,0:T(8,128)(2,1)S(1)}, f32[1,2560]{1,0:T(1,128)S(1)}, f32[1,768]{1,0:T(1,128)S(1)}) custom-call(s32[1]{0:T(128)} %bitcast.me_ref, bf16[4,2048,2560]{2,1,0:T(8,128)(2,1)} %bitcast.24, bf16[4,2048,2560]{2,1,0:T(8,128)(2,1)} %bitcast.25, bf16[1024,2560]{1,0:T(8,128)(2,1)S(1)} %collective-permute-done.2.b0, ...), custom_call_target="tpu_custom_call" | custom-call | flops 11796480 | bytes 11796480 | tf_op jit(solution)/shard_map/settle/pallas_call | solution.py:204
  285.6 7.5 %param_power.1 = (f32[512,2560]{1,0:T(8,128)S(1)}, f32[512,2560]{1,0:T(8,128)S(1)}, f32[512,2560]{1,0:T(8,128)S(1)}, f32[512,2560]{1,0:T(8,128)S(1)}, f32[8,128]{1,0:T(8,128)S(1)}) custom-call(f32[2048,2560]{1,0:T(8,128)} %bitcast.28), custom_call_target="tpu_custom_call" | custom-call | flops 10485760 | bytes 20971520 | tf_op jit(solution)/shard_map/param_power/pallas_call | solution.py:379
  293.1 2.3 copy-done
  295.5 2.4 copy-done.1
  297.8 2.3 copy-done.2
  300.2 17.4 %collective-permute-done.10.c0 = bf16[384,2560]{1,0:T(8,128)(2,1)S(1)} collective-permute-done((bf16[384,2560]{1,0:T(8,128)(2,1)}, bf16[384,2560]{1,0:T(8,128)(2,1)S(1)}, u32[]{:S(2)}, u32[]{:S(2)}) %collective-permute-start.10) | collective-permute-done | bytes 1966112 | tf_op jit(solution)/shard_map/ppermute | solution.py:596
  317.5 5.4 %settle.3 = (bf16[2048,2560]{1,0:T(8,128)(2,1)S(1)}, f32[1,2560]{1,0:T(1,128)S(1)}, f32[1,768]{1,0:T(1,128)S(1)}) custom-call(s32[1]{0:T(128)} %bitcast.me_ref, bf16[4,2048,2560]{2,1,0:T(8,128)(2,1)} %bitcast.26, bf16[4,2048,2560]{2,1,0:T(8,128)(2,1)} %bitcast.27, bf16[1024,2560]{1,0:T(8,128)(2,1)S(1)} %collective-permute-done.2.b0, ...), custom_call_target="tpu_custom_call", output_to_operand_aliasing={{0}: (7, {})} | custom-call | flops 11796480 | bytes 11796480 | tf_op jit(solution)/shard_map/settle/pallas_call | solution.py:204
  323.0 3.7 collective-permute-start.15
  328.5 2.7 collective-permute-done.14.refs_2_
  331.2 3.0 early.1
  334.2 10.0 %collective-permute-done.8.c0 = bf16[256,2560]{1,0:T(8,128)(2,1)S(1)} collective-permute-done((bf16[256,2560]{1,0:T(8,128)(2,1)}, bf16[256,2560]{1,0:T(8,128)(2,1)S(1)}, u32[]{:S(2)}, u32[]{:S(2)}) %collective-permute-start.8) | collective-permute-done | bytes 1310752 | tf_op jit(solution)/shard_map/ppermute | solution.py:596
  348.3 3.6 collective-permute-start.18
  353.7 2.7 collective-permute-done.17.refs_2_
  358.2 11.0 %finish.1 = (bf16[2048,2560]{1,0:T(8,128)(2,1)S(1)}, f32[512,2560]{1,0:T(8,128)S(1)}, f32[512,2560]{1,0:T(8,128)S(1)}, f32[512,2560]{1,0:T(8,128)S(1)}, f32[512,...) custom-call(bf16[2048,2560]{1,0:T(8,128)(2,1)S(1)} %get-tuple-elemen, ...), custom_call_target="tpu_custom_call", output_to_operand_aliasing={{0}: (0, {}), {1}: (3, {}), {2}: (4, {}), {3}: (5, {}), {4}... | custom-call | flops 31457280 | bytes 62914560 | tf_op jit(solution)/shard_map/finish/pallas_call | solution.py:558
  (51 shorter events, 14.6 us)
Async XLA Ops:
  2.0 18.6 %collective-permute-start = (bf16[128,2560]{1,0:T(8,128)(2,1)S(1)}, bf16[128,2560]{1,0:T(8,128)(2,1)S(1)}, u32[]{:S(2)}, u32[]{:S(2)}) collective-permute-start(bf16[128,2560]{1,0:T(8,128)(2,1)S(1)} %get-tuple-element.61), channel_id=1, source_target_pairs={{0,8},{8,0},{16,24},{24,16},{1,9},{9,1},{17,25},{25,17},{2,10},{10... | collective-permute-start | bytes 1966088 | tf_op jit(solution)/shard_map/ppermute | solution.py:596
  5.0 17.7 %collective-permute-start.1 = (bf16[128,2560]{1,0:T(8,128)(2,1)S(1)}, bf16[128,2560]{1,0:T(8,128)(2,1)S(1)}, u32[]{:S(2)}, u32[]{:S(2)}) collective-permute-start(bf16[128,2560]{1,0:T(8,128)(2,1)S(1)} %get-tuple-element.62), channel_id=1, source_target_pairs={{0,16},{8,24},{16,0},{24,8},{1,17},{9,25},{17,1},{25,9},{2,18},{10... | collective-permute-start | bytes 1966088 | tf_op jit(solution)/shard_map/ppermute | solution.py:596
  12.2 106.6 %collective-permute-start.4 = (bf16[896,2560]{1,0:T(8,128)(2,1)S(1)}, bf16[896,2560]{1,0:T(8,128)(2,1)S(1)}, u32[]{:S(2)}, u32[]{:S(2)}) collective-permute-start(bf16[896,2560]{1,0:T(8,128)(2,1)S(1)} %get-tuple-element.64), channel_id=1, source_target_pairs={{0,8},{8,0},{16,24},{24,16},{1,9},{9,1},{17,25},{25,17},{2,10},{10... | collective-permute-start | bytes 13762568 | tf_op jit(solution)/shard_map/ppermute | solution.py:596
  12.8 108.1 %collective-permute-start.5 = (bf16[896,2560]{1,0:T(8,128)(2,1)S(1)}, bf16[896,2560]{1,0:T(8,128)(2,1)S(1)}, u32[]{:S(2)}, u32[]{:S(2)}) collective-permute-start(bf16[896,2560]{1,0:T(8,128)(2,1)S(1)} %get-tuple-element.65), channel_id=1, source_target_pairs={{0,16},{8,24},{16,0},{24,8},{1,17},{9,25},{17,1},{25,9},{2,18},{10... | collective-permute-start | bytes 13762568 | tf_op jit(solution)/shard_map/ppermute | solution.py:596
  22.6 208.6 %collective-permute-start.2 = (bf16[1024,2560]{1,0:T(8,128)(2,1)S(1)}, bf16[1024,2560]{1,0:T(8,128)(2,1)S(1)}, u32[]{:S(2)}, u32[]{:S(2)}) collective-permute-start(bf16[1024,2560]{1,0:T(8,128)(2,1)S(1)} %get-tuple-element.69), channel_id=1, source_target_pairs={{0,8},{8,0},{16,24},{24,16},{1,9},{9,1},{17,25},{25,17},{2,10},{10... | collective-permute-start | bytes 15728648 | tf_op jit(solution)/shard_map/ppermute | solution.py:596
  22.7 210.6 %collective-permute-start.3 = (bf16[1024,2560]{1,0:T(8,128)(2,1)S(1)}, bf16[1024,2560]{1,0:T(8,128)(2,1)S(1)}, u32[]{:S(2)}, u32[]{:S(2)}) collective-permute-start(bf16[1024,2560]{1,0:T(8,128)(2,1)S(1)} %get-tuple-element.70), channel_id=1, source_target_pairs={{0,16},{8,24},{16,0},{24,8},{1,17},{9,25},{17,1},{25,9},{2,18},{10... | collective-permute-start | bytes 15728648 | tf_op jit(solution)/shard_map/ppermute | solution.py:596
  124.2 151.2 %collective-permute-start.6 = (bf16[384,2560]{1,0:T(8,128)(2,1)S(1)}, bf16[384,2560]{1,0:T(8,128)(2,1)S(1)}, u32[]{:S(2)}, u32[]{:S(2)}) collective-permute-start(bf16[384,2560]{1,0:T(8,128)(2,1)S(1)} %get-tuple-element.85), channel_id=1, source_target_pairs={{0,16},{8,24},{16,0},{24,8},{1,17},{9,25},{17,1},{25,9},{2,18},{10... | collective-permute-start | bytes 5898248 | tf_op jit(solution)/shard_map/ppermute | solution.py:596
  125.8 149.6 %collective-permute-start.7 = (bf16[384,2560]{1,0:T(8,128)(2,1)S(1)}, bf16[384,2560]{1,0:T(8,128)(2,1)S(1)}, u32[]{:S(2)}, u32[]{:S(2)}) collective-permute-start(bf16[384,2560]{1,0:T(8,128)(2,1)S(1)} %get-tuple-element.86), channel_id=1, source_target_pairs={{0,8},{8,0},{16,24},{24,16},{1,9},{9,1},{17,25},{25,17},{2,10},{10... | collective-permute-start | bytes 5898248 | tf_op jit(solution)/shard_map/ppermute | solution.py:596
  233.3 84.3 %collective-permute-start.10 = (bf16[384,2560]{1,0:T(8,128)(2,1)}, bf16[384,2560]{1,0:T(8,128)(2,1)S(1)}, u32[]{:S(2)}, u32[]{:S(2)}) collective-permute-start(bf16[384,2560]{1,0:T(8,128)(2,1)} %get-tuple-element.89), channel_id=1, source_target_pairs={{0,16},{8,24},{16,0},{24,8},{1,17},{9,25},{17,1},{25,9},{2,18},{10... | collective-permute-start | bytes 5898248 | tf_op jit(solution)/shard_map/ppermute | solution.py:596
  234.8 82.7 %collective-permute-start.11 = (bf16[384,2560]{1,0:T(8,128)(2,1)S(1)}, bf16[384,2560]{1,0:T(8,128)(2,1)S(1)}, u32[]{:S(2)}, u32[]{:S(2)}) collective-permute-start(bf16[384,2560]{1,0:T(8,128)(2,1)S(1)} %get-tuple-element.90), channel_id=1, source_target_pairs={{0,8},{8,0},{16,24},{24,16},{1,9},{9,1},{17,25},{25,17},{2,10},{10... | collective-permute-start | bytes 5898248 | tf_op jit(solution)/shard_map/ppermute | solution.py:596
  275.4 68.8 %collective-permute-start.8 = (bf16[256,2560]{1,0:T(8,128)(2,1)}, bf16[256,2560]{1,0:T(8,128)(2,1)S(1)}, u32[]{:S(2)}, u32[]{:S(2)}) collective-permute-start(bf16[256,2560]{1,0:T(8,128)(2,1)} %get-tuple-element.87), channel_id=1, source_target_pairs={{0,16},{8,24},{16,0},{24,8},{1,17},{9,25},{17,1},{25,9},{2,18},{10... | collective-permute-start | bytes 3932168 | tf_op jit(solution)/shard_map/ppermute | solution.py:596
  276.9 67.2 %collective-permute-start.9 = (bf16[256,2560]{1,0:T(8,128)(2,1)S(1)}, bf16[256,2560]{1,0:T(8,128)(2,1)S(1)}, u32[]{:S(2)}, u32[]{:S(2)}) collective-permute-start(bf16[256,2560]{1,0:T(8,128)(2,1)S(1)} %get-tuple-element.88), channel_id=1, source_target_pairs={{0,8},{8,0},{16,24},{24,16},{1,9},{9,1},{17,25},{25,17},{2,10},{10... | collective-permute-start | bytes 3932168 | tf_op jit(solution)/shard_map/ppermute | solution.py:596
  293.1 2.4 copy-start
  295.5 2.4 copy-start.1
  297.8 2.3 copy-start.2
  317.5 13.6 %copy-start.3 = (f32[1,2048]{1,0:T(1,128)S(1)}, f32[1,2048]{1,0:T(1,128)}, u32[]{:S(2)}) copy-start(f32[1,2048]{1,0:T(1,128)} %refs_4_.1) | copy-start | bytes 24580
  323.0 5.5 %collective-permute-start.15 = (f32[1,1536]{1,0:T(1,128)S(1)}, f32[1,1536]{1,0:T(1,128)S(1)}, u32[]{:S(2)}, u32[]{:S(2)}) collective-permute-start(f32[1,1536]{1,0:T(1,128)S(1)} %pad_maximum_fusion.refs_0_), channel_id=1, source_target_pairs={{0,3},{1,2},{2,1},{3,0},{4,7},{5,6},{6,5},{7,4},{8,11},{9,10},{10,... | collective-permute-start | bytes 18440 | tf_op jit(solution)/shard_map/ppermute | solution.py:574
  326.7 4.5 %collective-permute-start.14 = (f32[1,1536]{1,0:T(1,128)S(1)}, f32[1,1536]{1,0:T(1,128)S(1)}, u32[]{:S(2)}, u32[]{:S(2)}) collective-permute-start(f32[1,1536]{1,0:T(1,128)S(1)} %pad_maximum_fusion.refs_0_), channel_id=1, source_target_pairs={{0,2},{1,3},{2,0},{3,1},{4,6},{5,7},{6,4},{7,5},{8,10},{9,11},{10,... | collective-permute-start | bytes 18440 | tf_op jit(solution)/shard_map/ppermute | solution.py:574
  326.7 4.5 %collective-permute-start.13 = (f32[1,1536]{1,0:T(1,128)S(1)}, f32[1,1536]{1,0:T(1,128)S(1)}, u32[]{:S(2)}, u32[]{:S(2)}) collective-permute-start(f32[1,1536]{1,0:T(1,128)S(1)} %pad_maximum_fusion.refs_0_), channel_id=1, source_target_pairs={{0,1},{1,0},{2,3},{3,2},{4,5},{5,4},{6,7},{7,6},{8,9},{9,8},{10,11... | collective-permute-start | bytes 18440 | tf_op jit(solution)/shard_map/ppermute | solution.py:574
  331.2 27.0 %slice-start = ((s8[5242880]{0:T(1024)(128)(4,1)}), s8[4194304]{0:T(1024)(128)(4,1)S(1)}, s32[]{:S(2)}) async-start(s8[5242880]{0:T(1024)(128)(4,1)} %bitcast.5), calls=%async_computation | async-start | bytes 8388608
  331.2 27.0 %slice-start.2 = ((s8[5242880]{0:T(1024)(128)(4,1)}), s8[4194304]{0:T(1024)(128)(4,1)S(1)}, s32[]{:S(2)}) async-start(s8[5242880]{0:T(1024)(128)(4,1)} %bitcast.7), calls=%async_computation.2 | async-start | bytes 8388608
  331.2 27.0 %slice-start.4 = ((s8[5242880]{0:T(1024)(128)(4,1)}), s8[4194304]{0:T(1024)(128)(4,1)S(1)}, s32[]{:S(2)}) async-start(s8[5242880]{0:T(1024)(128)(4,1)} %bitcast.9), calls=%async_computation.4 | async-start | bytes 8388608
  344.2 2.8 copy-start.4
  344.2 14.0 %slice-start.1 = ((s8[5242880]{0:T(1024)(128)(4,1)}), s8[1048576]{0:T(1024)(128)(4,1)S(1)}, s32[]{:S(2)}) async-start(s8[5242880]{0:T(1024)(128)(4,1)} %bitcast.5), calls=%async_computation.1 | async-start | bytes 2097152
  344.2 14.0 %slice-start.3 = ((s8[5242880]{0:T(1024)(128)(4,1)}), s8[1048576]{0:T(1024)(128)(4,1)S(1)}, s32[]{:S(2)}) async-start(s8[5242880]{0:T(1024)(128)(4,1)} %bitcast.7), calls=%async_computation.3 | async-start | bytes 2097152
  344.2 14.0 %slice-start.5 = ((s8[5242880]{0:T(1024)(128)(4,1)}), s8[1048576]{0:T(1024)(128)(4,1)S(1)}, s32[]{:S(2)}) async-start(s8[5242880]{0:T(1024)(128)(4,1)} %bitcast.9), calls=%async_computation.5 | async-start | bytes 2097152
  345.7 1.2 collective-permute-start.12
  348.3 5.4 %collective-permute-start.18 = (f32[1,1280]{1,0:T(1,128)S(1)}, f32[1,1280]{1,0:T(1,128)S(1)}, u32[]{:S(2)}, u32[]{:S(2)}) collective-permute-start(f32[1,1280]{1,0:T(1,128)S(1)} %get-tuple-element.109.refs_0_), channel_id=1, source_target_pairs={{0,3},{1,2},{2,1},{3,0},{4,7},{5,6},{6,5},{7,4},{8,11},{9,10},{10,... | collective-permute-start | bytes 15368 | tf_op jit(solution)/shard_map/ppermute | solution.py:574
  351.9 4.5 %collective-permute-start.17 = (f32[1,1280]{1,0:T(1,128)S(1)}, f32[1,1280]{1,0:T(1,128)S(1)}, u32[]{:S(2)}, u32[]{:S(2)}) collective-permute-start(f32[1,1280]{1,0:T(1,128)S(1)} %get-tuple-element.109.refs_0_), channel_id=1, source_target_pairs={{0,2},{1,3},{2,0},{3,1},{4,6},{5,7},{6,4},{7,5},{8,10},{9,11},{10,... | collective-permute-start | bytes 15368 | tf_op jit(solution)/shard_map/ppermute | solution.py:574
  351.9 4.5 %collective-permute-start.16 = (f32[1,1280]{1,0:T(1,128)S(1)}, f32[1,1280]{1,0:T(1,128)S(1)}, u32[]{:S(2)}, u32[]{:S(2)}) collective-permute-start(f32[1,1280]{1,0:T(1,128)S(1)} %get-tuple-element.109.refs_0_), channel_id=1, source_target_pairs={{0,1},{1,0},{2,3},{3,2},{4,5},{5,4},{6,7},{7,6},{8,9},{9,8},{10,11... | collective-permute-start | bytes 15368 | tf_op jit(solution)/shard_map/ppermute | solution.py:574
  357.0 1.2 collective-permute-start.19

commit v4 on v3

--- a/solution.py
+++ b/solution.py
@@ -444,9 +444,9 @@
         in_specs=[whole_vmem] * (n + len(places) + 4),
         out_specs=[whole_vmem] * 3,
         out_shape=[
-            jax.ShapeDtypeStruct((1, columns), jnp.float32),
-            jax.ShapeDtypeStruct((1, columns), jnp.float32),
-            jax.ShapeDtypeStruct((1, 4 * late + 2 * LANES), jnp.float32),
+            pltpu.VMEM((1, columns), jnp.float32),
+            pltpu.VMEM((1, columns), jnp.float32),
+            pltpu.VMEM((1, 4 * late + 2 * LANES), jnp.float32),
         ],
         scratch_shapes=[pltpu.VMEM((8, columns), jnp.float32), pltpu.VMEM((2 * late, LANES), jnp.float32)],
         compiler_params=params_of(4 * MIB),
@@ -483,9 +483,9 @@
         in_specs=[whole_vmem] * (n + 2),
         out_specs=[whole_vmem] * 3,
         out_shape=[
-            jax.ShapeDtypeStruct((1, rows), jnp.float32),
-            jax.ShapeDtypeStruct((1, rows), jnp.float32),
-            jax.ShapeDtypeStruct((8, LANES), jnp.float32),
+            pltpu.VMEM((1, rows), jnp.float32),
+            pltpu.VMEM((1, rows), jnp.float32),
+            pltpu.VMEM((8, LANES), jnp.float32),
         ],
         compiler_params=params_of(4 * MIB),
         name="balance",
@@ -508,7 +508,7 @@
 
     def kernel(_, row_ref, col_ref, *refs):
         got, refs = refs[shares : shares + n], refs[shares + n :]
-        g_ref, held, (new_ref, update_ref, scale_ref, sems) = refs[0], refs[1 : 1 + shares], refs[1 + shares :]
+        g_ref, held, (new_ref, update_ref, scale_ref, sems, first_sems) = refs[0], refs[1 : 1 + shares], refs[1 + shares :]
         total = jnp.sum(tree([s[...] for s in got]), axis=1, keepdims=True)
         mean = total[1:2] / D
         rms = jnp.sqrt(mean * total[0:1] / (D * FF))
@@ -524,28 +524,50 @@
                 pltpu.make_async_copy(g_ref.at[here], update_ref.at[here], sems.at[1, q * each + t]),
             )
 
+        def opening(r):
+            here = pl.ds(r * group, group)
+            return (
+                pltpu.make_async_copy(held[0].at[here], new_ref.at[here], first_sems.at[0, r]),
+                pltpu.make_async_copy(g_ref.at[here], update_ref.at[here], first_sems.at[1, r]),
+            )
+
+        def rows_of(q, t, wide, r):
+            here = pl.ds(pl.multiple_of((q * each + t) * TILE + r * group, group), group)
+            there = pl.ds(pl.multiple_of(t * TILE + r * group, group), group)
+            root = wide[r * group : (r + 1) * group, :]
+            for k in range(columns // LANES):
+                at = slice(k * LANES, (k + 1) * LANES)
+                g = g_ref[here, at].astype(jnp.float32)
+                s = scale_ref[:, at]
+                full = jnp.concatenate([g[i : i + 8] * s for i in range(0, group, 8)], axis=0) * root
+                g_ref[here, at] = full.astype(g_ref.dtype)
+                held[q][there, at] = held[q][there, at] - LEARN_RATE * full
+
+        def widen(q, t):
+            lanes = row_ref[:, pl.ds(pl.multiple_of((q * each + t) * TILE, TILE), TILE)]
+            return jnp.broadcast_to(lanes, (LANES, TILE)).T
+
+        wide = widen(0, 0)
+        for r in range(TILE // group):
+            rows_of(0, 0, wide, r)
+            for copy in opening(r):
+                copy.start()
+
         for q in range(shares):
 
             def block(t, carry):
-                first = pl.multiple_of((q * each + t) * TILE, TILE)
-                wide = jnp.broadcast_to(row_ref[:, pl.ds(first, TILE)], (LANES, TILE)).T
-                for r in range(0, TILE, group):
-                    here = pl.ds(pl.multiple_of(first + r, group), group)
-                    there = pl.ds(pl.multiple_of(t * TILE + r, group), group)
-                    root = wide[r : r + group, :]
-                    for k in range(columns // LANES):
-                        at = slice(k * LANES, (k + 1) * LANES)
-                        g = g_ref[here, at].astype(jnp.float32)
-                        s = scale_ref[:, at]
-                        full = jnp.concatenate([g[i : i + 8] * s for i in range(0, group, 8)], axis=0) * root
-                        g_ref[here, at] = full.astype(g_ref.dtype)
-                        held[q][there, at] = held[q][there, at] - LEARN_RATE * full
+                wide = widen(q, t)
+                for r in range(TILE // group):
+                    rows_of(q, t, wide, r)
                 for copy in copies(q, t):
                     copy.start()
                 return carry
 
-            lax.fori_loop(0, each, block, 0)
-
+            lax.fori_loop(0 if q else 1, each, block, 0)
+
+        for r in range(TILE // group):
+            for copy in opening(r):
+                copy.wait()
         for q in range(shares):
 
             def drain(t, carry):
@@ -553,7 +575,7 @@
                     copy.wait()
                 return carry
 
-            lax.fori_loop(0, each, drain, 0)
+            lax.fori_loop(0 if q else 1, each, drain, 0)
 
     out = pl.pallas_call(
         kernel,
@@ -562,7 +584,11 @@
         out_shape=[pltpu.VMEM(x.shape, x.dtype) for x in (gradient, *params)]
         + [pltpu.HBM((rows, columns), jnp.float32), pltpu.HBM((rows, columns), jnp.bfloat16)],
         input_output_aliases={0: 0, **{3 + q: 1 + q for q in range(shares)}},
-        scratch_shapes=[pltpu.VMEM((8, columns), jnp.float32), pltpu.SemaphoreType.DMA((2, rows // TILE))],
+        scratch_shapes=[
+            pltpu.VMEM((8, columns), jnp.float32),
+            pltpu.SemaphoreType.DMA((2, rows // TILE)),
+            pltpu.SemaphoreType.DMA((2, TILE // group)),
+        ],
         compiler_params=params_of(4 * MIB),
         cost_estimate=cost(6 * rows * columns, 12 * rows * columns),
         name="finish",

time: 370 us -> 369 us (level)
    unnamed x22 -> x24, local copies, waits for them, and re-layouts: 7.09 us -> 8.29 us
  transfers between devices with their start and end apart: 20 -> 20, of which waited for: 15 -> 14; matrix products, arithmetic and copies ran while one was open for 0% -> 0% of each run, Pallas kernels for 13% -> 13%
where the time goes in v4:
time: 369 us; the launch traced here: 368 us
  waiting for transfers between devices  275 us (75%)
  Pallas kernels  61.4 us (17%)
  starting transfers between devices  22.5 us (6%)
  local copies, waits for them, and re-layouts  8.29 us (2%)
    ppermute x12, waiting for transfers between devices, hop(): lax.ppermute(v, 'dp', pairs(mesh.shape['dp'], n))  267 us
    ppermute x12, starting transfers between devices, hop(): lax.ppermute(v, 'dp', pairs(mesh.shape['dp'], n))  13.5 us
    pallas_call x2, Pallas kernels, pick(): pl.pallas_call(kernel, grid_spec=pltpu.PrefetchScalarGridSpec(num_scalar_...  12 us
    pallas_call x1, Pallas kernels, finish(): pl.pallas_call(kernel, in_specs=[anywhere, whole_vmem, whole_vmem] + [any...  10.8 us
    pallas_call x3, Pallas kernels, merge(): pl.pallas_call(kernel, grid_spec=pltpu.PrefetchScalarGridSpec(num_scalar_...  10.8 us
    pallas_call x2, Pallas kernels, settle(): pl.pallas_call(kernel, grid_spec=pltpu.PrefetchScalarGridSpec(num_scalar_...  10.8 us
    ppermute x8, starting transfers between devices, all_parts(): lax.ppermute(value, axis, pairs(size, k))  9.05 us
    ppermute x8, waiting for transfers between devices, all_parts(): lax.ppermute(value, axis, pairs(size, k))  8.64 us
  transfers between devices with their start and end apart: 20, of which 14 were waited for; matrix products, arithmetic and copies ran while one was open for 0% of the time, Pallas kernels for 13%

profile of v4, /device:TPU:0, one launch (start us, length us, event | category | flops | bytes accessed | tf_op | source)
XLA Modules:
  0.0 368.3 jit_solution(4204794361940306301)
XLA Ops:
  2.0 3.0 collective-permute-start
  5.0 1.5 collective-permute-start.1
  6.5 5.8 %pick.2 = (bf16[896,2560]{1,0:T(8,128)(2,1)S(1)}, bf16[896,2560]{1,0:T(8,128)(2,1)S(1)}) custom-call(s32[1]{0:T(128)} %bitcast.me_ref, bf16[4,2048,2560]{2,1,0:T(8,128)(2,1)} %bitcast.12, bf16[4,2048,2560]{2,1,0:T(8,128)(2,1)} %bitcast.13), custom_call_target="tpu_custom_call" | custom-call | bytes 18350080 | tf_op jit(solution)/shard_map/pick/pallas_call | solution.py:53
  12.9 6.2 %pick.3 = (bf16[1024,2560]{1,0:T(8,128)(2,1)S(1)}, bf16[1024,2560]{1,0:T(8,128)(2,1)S(1)}) custom-call(s32[1]{0:T(128)} %bitcast.me_ref, bf16[4,2048,2560]{2,1,0:T(8,128)(2,1)} %bitcast.14, bf16[4,2048,2560]{2,1,0:T(8,128)(2,1)} %bitcast.15), custom_call_target="tpu_custom_call" | custom-call | bytes 20971520 | tf_op jit(solution)/shard_map/pick/pallas_call | solution.py:53
  20.5 2.1 collective-permute-done.1.refs_1_
  22.7 2.0 collective-permute-start.3
  24.7 94.2 %collective-permute-done.4.refs_0_.refs_2_ = bf16[896,2560]{1,0:T(8,128)(2,1)S(1)} collective-permute-done((bf16[896,2560]{1,0:T(8,128)(2,1)S(1)}, bf16[896,2560]{1,0:T(8,128)(2,1)S(1)}, u32[]{:S(2)}, u32[]{:S(2)}) %collective-permute-start.4) | collective-permute-done | bytes 4587552 | tf_op jit(solution)/shard_map/ppermute | solution.py:622
  118.8 2.1 collective-permute-done.5.refs_1_.refs_3_
  120.9 3.3 merge.3
  124.2 1.6 collective-permute-start.6
  126.4 4.6 %merge.4 = (bf16[384,2560]{1,0:T(8,128)(2,1)}, bf16[384,2560]{1,0:T(8,128)(2,1)S(1)}) custom-call(s32[1]{0:T(128)} %bitcast.me_ref, bf16[4,2048,2560]{2,1,0:T(8,128)(2,1)} %bitcast.18, bf16[4,2048,2560]{2,1,0:T(8,128)(2,1)} %bitcast.19, bf16[896,2560]{1,0:T(8,128)(2,1)S(1)} %collective-permute-done.4.refs_0_.refs_2_, ...), custom_call_target="tpu_custom_call" | custom-call | flops 1966080 | bytes 11796480 | tf_op jit(solution)/shard_map/merge/pallas_call | solution.py:123
  130.9 100.2 %collective-permute-done.2.b0 = bf16[1024,2560]{1,0:T(8,128)(2,1)S(1)} collective-permute-done((bf16[1024,2560]{1,0:T(8,128)(2,1)S(1)}, bf16[1024,2560]{1,0:T(8,128)(2,1)S(1)}, u32[]{:S(2)}, u32[]{:S(2)}) %collective-permute-start.2) | collective-permute-done | bytes 5242912 | tf_op jit(solution)/shard_map/ppermute | solution.py:622
  231.2 2.1 collective-permute-done.3.b1
  233.3 1.5 collective-permute-start.10
  235.3 2.9 merge.5
  238.3 37.1 %collective-permute-done.6.c0 = bf16[384,2560]{1,0:T(8,128)(2,1)S(1)} collective-permute-done((bf16[384,2560]{1,0:T(8,128)(2,1)S(1)}, bf16[384,2560]{1,0:T(8,128)(2,1)S(1)}, u32[]{:S(2)}, u32[]{:S(2)}) %collective-permute-start.6) | collective-permute-done | bytes 1966112 | tf_op jit(solution)/shard_map/ppermute | solution.py:622
  275.4 1.5 collective-permute-start.8
  277.5 2.7 presum.1.base_ref
  280.2 5.4 %settle.2 = (bf16[2048,2560]{1,0:T(8,128)(2,1)S(1)}, f32[1,2560]{1,0:T(1,128)S(1)}, f32[1,768]{1,0:T(1,128)S(1)}) custom-call(s32[1]{0:T(128)} %bitcast.me_ref, bf16[4,2048,2560]{2,1,0:T(8,128)(2,1)} %bitcast.24, bf16[4,2048,2560]{2,1,0:T(8,128)(2,1)} %bitcast.25, bf16[1024,2560]{1,0:T(8,128)(2,1)S(1)} %collective-permute-done.2.b0, ...), custom_call_target="tpu_custom_call" | custom-call | flops 11796480 | bytes 11796480 | tf_op jit(solution)/shard_map/settle/pallas_call | solution.py:204
  285.6 7.5 %param_power.1 = (f32[512,2560]{1,0:T(8,128)S(1)}, f32[512,2560]{1,0:T(8,128)S(1)}, f32[512,2560]{1,0:T(8,128)S(1)}, f32[512,2560]{1,0:T(8,128)S(1)}, f32[8,128]{1,0:T(8,128)S(1)}) custom-call(f32[2048,2560]{1,0:T(8,128)} %bitcast.28), custom_call_target="tpu_custom_call" | custom-call | flops 10485760 | bytes 20971520 | tf_op jit(solution)/shard_map/param_power/pallas_call | solution.py:379
  293.1 2.3 copy-done
  295.5 2.4 copy-done.1
  297.8 2.3 copy-done.2
  300.2 17.4 %collective-permute-done.10.c0 = bf16[384,2560]{1,0:T(8,128)(2,1)S(1)} collective-permute-done((bf16[384,2560]{1,0:T(8,128)(2,1)}, bf16[384,2560]{1,0:T(8,128)(2,1)S(1)}, u32[]{:S(2)}, u32[]{:S(2)}) %collective-permute-start.10) | collective-permute-done | bytes 1966112 | tf_op jit(solution)/shard_map/ppermute | solution.py:622
  317.5 5.4 %settle.3 = (bf16[2048,2560]{1,0:T(8,128)(2,1)S(1)}, f32[1,2560]{1,0:T(1,128)S(1)}, f32[1,768]{1,0:T(1,128)S(1)}) custom-call(s32[1]{0:T(128)} %bitcast.me_ref, bf16[4,2048,2560]{2,1,0:T(8,128)(2,1)} %bitcast.26, bf16[4,2048,2560]{2,1,0:T(8,128)(2,1)} %bitcast.27, bf16[1024,2560]{1,0:T(8,128)(2,1)S(1)} %collective-permute-done.2.b0, ...), custom_call_target="tpu_custom_call", output_to_operand_aliasing={{0}: (7, {})} | custom-call | flops 11796480 | bytes 11796480 | tf_op jit(solution)/shard_map/settle/pallas_call | solution.py:204
  323.0 3.7 collective-permute-start.15
  328.5 2.7 collective-permute-done.14.refs_2_
  331.2 3.0 early.1
  334.2 10.0 %collective-permute-done.8.c0 = bf16[256,2560]{1,0:T(8,128)(2,1)S(1)} collective-permute-done((bf16[256,2560]{1,0:T(8,128)(2,1)}, bf16[256,2560]{1,0:T(8,128)(2,1)S(1)}, u32[]{:S(2)}, u32[]{:S(2)}) %collective-permute-start.8) | collective-permute-done | bytes 1310752 | tf_op jit(solution)/shard_map/ppermute | solution.py:622
  347.9 3.7 collective-permute-start.18
  353.4 2.7 collective-permute-done.17.refs_2_
  357.5 10.8 %finish.1 = (bf16[2048,2560]{1,0:T(8,128)(2,1)S(1)}, f32[512,2560]{1,0:T(8,128)S(1)}, f32[512,2560]{1,0:T(8,128)S(1)}, f32[512,2560]{1,0:T(8,128)S(1)}, f32[512,...) custom-call(bf16[2048,2560]{1,0:T(8,128)(2,1)S(1)} %get-tuple-elemen, ...), custom_call_target="tpu_custom_call", output_to_operand_aliasing={{0}: (0, {}), {1}: (3, {}), {2}: (4, {}), {3}: (5, {}), {4}... | custom-call | flops 31457280 | bytes 62914560 | tf_op jit(solution)/shard_map/finish/pallas_call | solution.py:580
  (53 shorter events, 13.7 us)
Async XLA Ops:
  2.0 18.6 %collective-permute-start = (bf16[128,2560]{1,0:T(8,128)(2,1)S(1)}, bf16[128,2560]{1,0:T(8,128)(2,1)S(1)}, u32[]{:S(2)}, u32[]{:S(2)}) collective-permute-start(bf16[128,2560]{1,0:T(8,128)(2,1)S(1)} %get-tuple-element.61), channel_id=1, source_target_pairs={{0,8},{8,0},{16,24},{24,16},{1,9},{9,1},{17,25},{25,17},{2,10},{10... | collective-permute-start | bytes 1966088 | tf_op jit(solution)/shard_map/ppermute | solution.py:622
  5.0 17.7 %collective-permute-start.1 = (bf16[128,2560]{1,0:T(8,128)(2,1)S(1)}, bf16[128,2560]{1,0:T(8,128)(2,1)S(1)}, u32[]{:S(2)}, u32[]{:S(2)}) collective-permute-start(bf16[128,2560]{1,0:T(8,128)(2,1)S(1)} %get-tuple-element.62), channel_id=1, source_target_pairs={{0,16},{8,24},{16,0},{24,8},{1,17},{9,25},{17,1},{25,9},{2,18},{10... | collective-permute-start | bytes 1966088 | tf_op jit(solution)/shard_map/ppermute | solution.py:622
  12.2 106.6 %collective-permute-start.4 = (bf16[896,2560]{1,0:T(8,128)(2,1)S(1)}, bf16[896,2560]{1,0:T(8,128)(2,1)S(1)}, u32[]{:S(2)}, u32[]{:S(2)}) collective-permute-start(bf16[896,2560]{1,0:T(8,128)(2,1)S(1)} %get-tuple-element.64), channel_id=1, source_target_pairs={{0,8},{8,0},{16,24},{24,16},{1,9},{9,1},{17,25},{25,17},{2,10},{10... | collective-permute-start | bytes 13762568 | tf_op jit(solution)/shard_map/ppermute | solution.py:622
  12.8 108.1 %collective-permute-start.5 = (bf16[896,2560]{1,0:T(8,128)(2,1)S(1)}, bf16[896,2560]{1,0:T(8,128)(2,1)S(1)}, u32[]{:S(2)}, u32[]{:S(2)}) collective-permute-start(bf16[896,2560]{1,0:T(8,128)(2,1)S(1)} %get-tuple-element.65), channel_id=1, source_target_pairs={{0,16},{8,24},{16,0},{24,8},{1,17},{9,25},{17,1},{25,9},{2,18},{10... | collective-permute-start | bytes 13762568 | tf_op jit(solution)/shard_map/ppermute | solution.py:622
  22.6 208.6 %collective-permute-start.2 = (bf16[1024,2560]{1,0:T(8,128)(2,1)S(1)}, bf16[1024,2560]{1,0:T(8,128)(2,1)S(1)}, u32[]{:S(2)}, u32[]{:S(2)}) collective-permute-start(bf16[1024,2560]{1,0:T(8,128)(2,1)S(1)} %get-tuple-element.69), channel_id=1, source_target_pairs={{0,8},{8,0},{16,24},{24,16},{1,9},{9,1},{17,25},{25,17},{2,10},{10... | collective-permute-start | bytes 15728648 | tf_op jit(solution)/shard_map/ppermute | solution.py:622
  22.7 210.6 %collective-permute-start.3 = (bf16[1024,2560]{1,0:T(8,128)(2,1)S(1)}, bf16[1024,2560]{1,0:T(8,128)(2,1)S(1)}, u32[]{:S(2)}, u32[]{:S(2)}) collective-permute-start(bf16[1024,2560]{1,0:T(8,128)(2,1)S(1)} %get-tuple-element.70), channel_id=1, source_target_pairs={{0,16},{8,24},{16,0},{24,8},{1,17},{9,25},{17,1},{25,9},{2,18},{10... | collective-permute-start | bytes 15728648 | tf_op jit(solution)/shard_map/ppermute | solution.py:622
  124.2 151.2 %collective-permute-start.6 = (bf16[384,2560]{1,0:T(8,128)(2,1)S(1)}, bf16[384,2560]{1,0:T(8,128)(2,1)S(1)}, u32[]{:S(2)}, u32[]{:S(2)}) collective-permute-start(bf16[384,2560]{1,0:T(8,128)(2,1)S(1)} %get-tuple-element.85), channel_id=1, source_target_pairs={{0,16},{8,24},{16,0},{24,8},{1,17},{9,25},{17,1},{25,9},{2,18},{10... | collective-permute-start | bytes 5898248 | tf_op jit(solution)/shard_map/ppermute | solution.py:622
  125.8 149.6 %collective-permute-start.7 = (bf16[384,2560]{1,0:T(8,128)(2,1)S(1)}, bf16[384,2560]{1,0:T(8,128)(2,1)S(1)}, u32[]{:S(2)}, u32[]{:S(2)}) collective-permute-start(bf16[384,2560]{1,0:T(8,128)(2,1)S(1)} %get-tuple-element.86), channel_id=1, source_target_pairs={{0,8},{8,0},{16,24},{24,16},{1,9},{9,1},{17,25},{25,17},{2,10},{10... | collective-permute-start | bytes 5898248 | tf_op jit(solution)/shard_map/ppermute | solution.py:622
  233.3 84.3 %collective-permute-start.10 = (bf16[384,2560]{1,0:T(8,128)(2,1)}, bf16[384,2560]{1,0:T(8,128)(2,1)S(1)}, u32[]{:S(2)}, u32[]{:S(2)}) collective-permute-start(bf16[384,2560]{1,0:T(8,128)(2,1)} %get-tuple-element.89), channel_id=1, source_target_pairs={{0,16},{8,24},{16,0},{24,8},{1,17},{9,25},{17,1},{25,9},{2,18},{10... | collective-permute-start | bytes 5898248 | tf_op jit(solution)/shard_map/ppermute | solution.py:622
  234.8 82.7 %collective-permute-start.11 = (bf16[384,2560]{1,0:T(8,128)(2,1)S(1)}, bf16[384,2560]{1,0:T(8,128)(2,1)S(1)}, u32[]{:S(2)}, u32[]{:S(2)}) collective-permute-start(bf16[384,2560]{1,0:T(8,128)(2,1)S(1)} %get-tuple-element.90), channel_id=1, source_target_pairs={{0,8},{8,0},{16,24},{24,16},{1,9},{9,1},{17,25},{25,17},{2,10},{10... | collective-permute-start | bytes 5898248 | tf_op jit(solution)/shard_map/ppermute | solution.py:622
  275.4 68.8 %collective-permute-start.8 = (bf16[256,2560]{1,0:T(8,128)(2,1)}, bf16[256,2560]{1,0:T(8,128)(2,1)S(1)}, u32[]{:S(2)}, u32[]{:S(2)}) collective-permute-start(bf16[256,2560]{1,0:T(8,128)(2,1)} %get-tuple-element.87), channel_id=1, source_target_pairs={{0,16},{8,24},{16,0},{24,8},{1,17},{9,25},{17,1},{25,9},{2,18},{10... | collective-permute-start | bytes 3932168 | tf_op jit(solution)/shard_map/ppermute | solution.py:622
  276.9 67.2 %collective-permute-start.9 = (bf16[256,2560]{1,0:T(8,128)(2,1)S(1)}, bf16[256,2560]{1,0:T(8,128)(2,1)S(1)}, u32[]{:S(2)}, u32[]{:S(2)}) collective-permute-start(bf16[256,2560]{1,0:T(8,128)(2,1)S(1)} %get-tuple-element.88), channel_id=1, source_target_pairs={{0,8},{8,0},{16,24},{24,16},{1,9},{9,1},{17,25},{25,17},{2,10},{10... | collective-permute-start | bytes 3932168 | tf_op jit(solution)/shard_map/ppermute | solution.py:622
  293.1 2.4 copy-start
  295.5 2.4 copy-start.1
  297.8 2.3 copy-start.2
  317.5 13.6 %copy-start.3 = (f32[1,2048]{1,0:T(1,128)S(1)}, f32[1,2048]{1,0:T(1,128)}, u32[]{:S(2)}) copy-start(f32[1,2048]{1,0:T(1,128)} %refs_4_.1) | copy-start | bytes 24580
  323.0 5.5 %collective-permute-start.15 = (f32[1,1536]{1,0:T(1,128)S(1)}, f32[1,1536]{1,0:T(1,128)S(1)}, u32[]{:S(2)}, u32[]{:S(2)}) collective-permute-start(f32[1,1536]{1,0:T(1,128)S(1)} %pad_maximum_fusion.refs_0_), channel_id=1, source_target_pairs={{0,3},{1,2},{2,1},{3,0},{4,7},{5,6},{6,5},{7,4},{8,11},{9,10},{10,... | collective-permute-start | bytes 18440 | tf_op jit(solution)/shard_map/ppermute | solution.py:600
  326.7 4.5 %collective-permute-start.14 = (f32[1,1536]{1,0:T(1,128)S(1)}, f32[1,1536]{1,0:T(1,128)S(1)}, u32[]{:S(2)}, u32[]{:S(2)}) collective-permute-start(f32[1,1536]{1,0:T(1,128)S(1)} %pad_maximum_fusion.refs_0_), channel_id=1, source_target_pairs={{0,2},{1,3},{2,0},{3,1},{4,6},{5,7},{6,4},{7,5},{8,10},{9,11},{10,... | collective-permute-start | bytes 18440 | tf_op jit(solution)/shard_map/ppermute | solution.py:600
  326.7 4.5 %collective-permute-start.13 = (f32[1,1536]{1,0:T(1,128)S(1)}, f32[1,1536]{1,0:T(1,128)S(1)}, u32[]{:S(2)}, u32[]{:S(2)}) collective-permute-start(f32[1,1536]{1,0:T(1,128)S(1)} %pad_maximum_fusion.refs_0_), channel_id=1, source_target_pairs={{0,1},{1,0},{2,3},{3,2},{4,5},{5,4},{6,7},{7,6},{8,9},{9,8},{10,11... | collective-permute-start | bytes 18440 | tf_op jit(solution)/shard_map/ppermute | solution.py:600
  331.2 26.2 %slice-start = ((s8[5242880]{0:T(1024)(128)(4,1)}), s8[4194304]{0:T(1024)(128)(4,1)S(1)}, s32[]{:S(2)}) async-start(s8[5242880]{0:T(1024)(128)(4,1)} %bitcast.5), calls=%async_computation | async-start | bytes 8388608
  331.2 26.2 %slice-start.2 = ((s8[5242880]{0:T(1024)(128)(4,1)}), s8[4194304]{0:T(1024)(128)(4,1)S(1)}, s32[]{:S(2)}) async-start(s8[5242880]{0:T(1024)(128)(4,1)} %bitcast.7), calls=%async_computation.2 | async-start | bytes 8388608
  331.2 26.2 %slice-start.4 = ((s8[5242880]{0:T(1024)(128)(4,1)}), s8[4194304]{0:T(1024)(128)(4,1)S(1)}, s32[]{:S(2)}) async-start(s8[5242880]{0:T(1024)(128)(4,1)} %bitcast.9), calls=%async_computation.4 | async-start | bytes 8388608
  344.2 2.8 copy-start.4
  344.2 13.2 %slice-start.1 = ((s8[5242880]{0:T(1024)(128)(4,1)}), s8[1048576]{0:T(1024)(128)(4,1)S(1)}, s32[]{:S(2)}) async-start(s8[5242880]{0:T(1024)(128)(4,1)} %bitcast.5), calls=%async_computation.1 | async-start | bytes 2097152
  344.2 13.3 %slice-start.3 = ((s8[5242880]{0:T(1024)(128)(4,1)}), s8[1048576]{0:T(1024)(128)(4,1)S(1)}, s32[]{:S(2)}) async-start(s8[5242880]{0:T(1024)(128)(4,1)} %bitcast.7), calls=%async_computation.3 | async-start | bytes 2097152
  344.2 13.3 %slice-start.5 = ((s8[5242880]{0:T(1024)(128)(4,1)}), s8[1048576]{0:T(1024)(128)(4,1)S(1)}, s32[]{:S(2)}) async-start(s8[5242880]{0:T(1024)(128)(4,1)} %bitcast.9), calls=%async_computation.5 | async-start | bytes 2097152
  345.7 1.2 collective-permute-start.12
  347.9 5.5 %collective-permute-start.18 = (f32[1,1280]{1,0:T(1,128)S(1)}, f32[1,1280]{1,0:T(1,128)S(1)}, u32[]{:S(2)}, u32[]{:S(2)}) collective-permute-start(f32[1,1280]{1,0:T(1,128)S(1)} %get-tuple-element.109.refs_0_), channel_id=1, source_target_pairs={{0,3},{1,2},{2,1},{3,0},{4,7},{5,6},{6,5},{7,4},{8,11},{9,10},{10,... | collective-permute-start | bytes 15368 | tf_op jit(solution)/shard_map/ppermute | solution.py:600
  351.6 4.5 %collective-permute-start.17 = (f32[1,1280]{1,0:T(1,128)S(1)}, f32[1,1280]{1,0:T(1,128)S(1)}, u32[]{:S(2)}, u32[]{:S(2)}) collective-permute-start(f32[1,1280]{1,0:T(1,128)S(1)} %get-tuple-element.109.refs_0_), channel_id=1, source_target_pairs={{0,2},{1,3},{2,0},{3,1},{4,6},{5,7},{6,4},{7,5},{8,10},{9,11},{10,... | collective-permute-start | bytes 15368 | tf_op jit(solution)/shard_map/ppermute | solution.py:600
  351.6 4.5 %collective-permute-start.16 = (f32[1,1280]{1,0:T(1,128)S(1)}, f32[1,1280]{1,0:T(1,128)S(1)}, u32[]{:S(2)}, u32[]{:S(2)}) collective-permute-start(f32[1,1280]{1,0:T(1,128)S(1)} %get-tuple-element.109.refs_0_), channel_id=1, source_target_pairs={{0,1},{1,0},{2,3},{3,2},{4,5},{5,4},{6,7},{7,6},{8,9},{9,8},{10,11... | collective-permute-start | bytes 15368 | tf_op jit(solution)/shard_map/ppermute | solution.py:600
  356.1 1.3 collective-permute-start.19

commit v5 on v4

--- a/solution.py
+++ b/solution.py
@@ -252,55 +252,53 @@
     )(me, parts, parts, *second)
 
 
-def close(base, third, at, gradient, col_sums):
+def close(base, came, h, gradient, col_sums):
     rows, columns = gradient.shape
     half = rows // 2
-    size = base.shape[0] // 2
+    size = came.shape[0]
     chunks = columns // LANES
 
-    def kernel(base_ref, c0, c1, _, before_ref, g_ref, col_ref, row_ref, sums_ref):
+    def kernel(base_ref, came_ref, _, before_ref, g_ref, col_ref, row_ref, sums_ref):
+        def body(r, carry):
+            here = pl.ds(pl.multiple_of(r * GROUP, GROUP), GROUP)
+            there = pl.ds(pl.multiple_of(h * size + r * GROUP, GROUP), GROUP)
+            kept = pl.ds(pl.multiple_of(h * half + r * GROUP, GROUP), GROUP)
+            across = jnp.zeros((GROUP, LANES), jnp.float32)
+            down = []
+            for k in range(chunks):
+                lanes = slice(k * LANES, (k + 1) * LANES)
+                total = base_ref[there, lanes] + came_ref[here, lanes].astype(jnp.float32)
+                g_ref[kept, lanes] = total.astype(g_ref.dtype)
+                square = total * total
+                across = across + square
+                down.append(carry[k] + square[:8] + square[8:])
+            sums_ref[here, :] = across
+            return tuple(down)
+
         carry = tuple(jnp.zeros((8, LANES), jnp.float32) for _ in range(chunks))
-        for h, c in enumerate((c0, c1)):
-
-            def body(r, carry):
-                here = pl.ds(pl.multiple_of(r * GROUP, GROUP), GROUP)
-                there = pl.ds(pl.multiple_of(h * size + r * GROUP, GROUP), GROUP)
-                kept = pl.ds(pl.multiple_of(h * half + at + r * GROUP, GROUP), GROUP)
-                across = jnp.zeros((GROUP, LANES), jnp.float32)
-                down = []
-                for k in range(chunks):
-                    lanes = slice(k * LANES, (k + 1) * LANES)
-                    total = base_ref[there, lanes] + c[here, lanes].astype(jnp.float32)
-                    g_ref[kept, lanes] = total.astype(g_ref.dtype)
-                    square = total * total
-                    across = across + square
-                    down.append(carry[k] + square[:8] + square[8:])
-                sums_ref[there, :] = across
-                return tuple(down)
-
-            carry = lax.fori_loop(0, size // GROUP, body, carry)
+        carry = lax.fori_loop(0, size // GROUP, body, carry)
         for k in range(chunks):
             lanes = slice(k * LANES, (k + 1) * LANES)
             col_ref[:, lanes] = before_ref[:, lanes] + jnp.sum(carry[k], axis=0, keepdims=True)
-        for q in range(2 * size // LANES):
+        for q in range(size // LANES):
             lanes = slice(q * LANES, (q + 1) * LANES)
             row_ref[:, lanes] = lane_sums(sums_ref[lanes, :])
 
     return pl.pallas_call(
         kernel,
-        in_specs=[whole_vmem] * 3 + [anywhere, whole_vmem],
+        in_specs=[whole_vmem] * 2 + [anywhere, whole_vmem],
         out_specs=[whole_vmem] * 3,
         out_shape=[
             pltpu.VMEM((rows, columns), gradient.dtype),
-            jax.ShapeDtypeStruct((1, columns), jnp.float32),
-            jax.ShapeDtypeStruct((1, 2 * size), jnp.float32),
+            pltpu.VMEM((1, columns), jnp.float32),
+            pltpu.VMEM((1, size), jnp.float32),
         ],
-        input_output_aliases={3: 0},
-        scratch_shapes=[pltpu.VMEM((2 * size, LANES), jnp.float32)],
+        input_output_aliases={2: 0},
+        scratch_shapes=[pltpu.VMEM((size, LANES), jnp.float32)],
         compiler_params=params_of(4 * MIB),
-        cost_estimate=cost(10 * size * columns, 12 * size * columns),
+        cost_estimate=cost(5 * size * columns, 6 * size * columns),
         name="close",
-    )(base, *third, gradient, col_sums)
+    )(base, came, gradient, col_sums)
 
 
 def early(gradient, messages, row_moment, at, size):
@@ -396,17 +394,16 @@
     return values[0]
 
 
-def weigh(gradient, col_sums, col_moment, row_pieces, early_sums, power, late):
+def weigh(gradient, col_sums, col_moment, row_sums, early_sums, power, late):
     rows, columns = gradient.shape
     half = rows // 2
     chunks = columns // LANES
     n = len(col_sums)
-    places = sorted(row_pieces)
     group = 4 * GROUP
 
     def kernel(g_ref, *refs):
         sums, refs = refs[:n], refs[n:]
-        row_refs, refs = refs[: len(places)], refs[len(places) :]
+        row_refs, refs = refs[:2], refs[2:]
         moment_ref, early_ref, power_ref, new_ref, root_ref, out_ref, wide_ref, acc_ref = refs
         total = tree([s[...] for s in sums]) + D * EPSILON
         new = DECAY * moment_ref[...] + (1.0 - DECAY) * total / D
@@ -414,10 +411,8 @@
         root = lax.rsqrt(new)
         root_ref[...] = root
         wide_ref[...] = jnp.broadcast_to(root, wide_ref.shape)
-        for at, row_ref in zip(places, row_refs):
-            size = row_ref.shape[1] // 2
-            for h in range(2):
-                out_ref[:, h * late + at : h * late + at + size] = row_ref[:, h * size : (h + 1) * size]
+        for h, row_ref in enumerate(row_refs):
+            out_ref[:, h * late : (h + 1) * late] = row_ref[...]
         out_ref[:, 4 * late : 4 * late + LANES] = tree_lanes(early_ref[...] * (root * root), columns)
         out_ref[:, 4 * late + LANES :] = jnp.sum(power_ref[...], axis=0, keepdims=True)
         for h in range(2):
@@ -441,7 +436,7 @@
 
     return pl.pallas_call(
         kernel,
-        in_specs=[whole_vmem] * (n + len(places) + 4),
+        in_specs=[whole_vmem] * (n + 6),
         out_specs=[whole_vmem] * 3,
         out_shape=[
             pltpu.VMEM((1, columns), jnp.float32),
@@ -452,7 +447,7 @@
         compiler_params=params_of(4 * MIB),
         cost_estimate=cost(8 * late * columns, 4 * late * columns),
         name="weigh",
-    )(gradient, *col_sums, *[row_pieces[at] for at in places], col_moment, early_sums, power)
+    )(gradient, *col_sums, *row_sums, col_moment, early_sums, power)
 
 
 def balance(messages, row_moment, new_early, late):
@@ -667,10 +662,11 @@
             [row_pieces[at][:, h * size : (h + 1) * size] for h in range(2) for at, size in sorted(pieces[:-1])], axis=1
         )
         new_early, early_sums = early(state[0], all_parts(message, "col", along), row_moment, late, half - late)
-        gradient, col_sums, late_rows = close(base, third[-1], 0, *state)
+        gradient, col_sums, last_rows = close(base, third[-1][1], 1, *state)
+        gradient, col_sums, first_rows = close(base, third[-1][0], 0, gradient, col_sums)
 
         col_parts = all_parts(col_sums, "row", across)
-        new_col, col_root, message = weigh(gradient, col_parts, col_moment, {0: late_rows}, early_sums, power, late)
+        new_col, col_root, message = weigh(gradient, col_parts, col_moment, [first_rows, last_rows], early_sums, power, late)
         new_row, row_root, stats = balance(all_parts(message, "col", along), row_moment, new_early, late)
         new_params, update = finish(gradient, kept, row_root, col_root, all_parts(stats, "row", across))
         return new_params[None], update[None], new_row, new_col

time: 369 us -> 368 us (level)
  transfers between devices with their start and end apart: 20 -> 20, of which waited for: 14 -> 15; matrix products, arithmetic and copies ran while one was open for 0% -> 0% of each run, Pallas kernels for 13% -> 13%
where the time goes in v5:
time: 368 us
  waiting for transfers between devices  275 us (75%)
  Pallas kernels  61.4 us (17%)
  starting transfers between devices  22.5 us (6%)
  local copies, waits for them, and re-layouts  8.29 us (2%)
    ppermute x12, waiting for transfers between devices, hop(): lax.ppermute(v, 'dp', pairs(mesh.shape['dp'], n))  266 us
    ppermute x12, starting transfers between devices, hop(): lax.ppermute(v, 'dp', pairs(mesh.shape['dp'], n))  13.5 us
    pallas_call x2, Pallas kernels, pick(): pl.pallas_call(kernel, grid_spec=pltpu.PrefetchScalarGridSpec(num_scalar_...  12 us
    pallas_call x1, Pallas kernels, finish(): pl.pallas_call(kernel, in_specs=[anywhere, whole_vmem, whole_vmem] + [any...  10.8 us
    pallas_call x3, Pallas kernels, merge(): pl.pallas_call(kernel, grid_spec=pltpu.PrefetchScalarGridSpec(num_scalar_...  10.8 us
    pallas_call x2, Pallas kernels, settle(): pl.pallas_call(kernel, grid_spec=pltpu.PrefetchScalarGridSpec(num_scalar_...  10.8 us
    ppermute x8, starting transfers between devices, all_parts(): lax.ppermute(value, axis, pairs(size, k))  9.05 us
    ppermute x8, waiting for transfers between devices, all_parts(): lax.ppermute(value, axis, pairs(size, k))  8.64 us
  transfers between devices with their start and end apart: 20, of which 15 were waited for; matrix products, arithmetic and copies ran while one was open for 0% of the time, Pallas kernels for 13%

profile of v5, /device:TPU:0, one launch (start us, length us, event | category | flops | bytes accessed | tf_op | source)
XLA Modules:
  0.0 367.6 jit_solution(13259006646439424811)
XLA Ops:
  2.0 3.0 collective-permute-start
  5.0 1.5 collective-permute-start.1
  6.5 5.8 %pick.2 = (bf16[896,2560]{1,0:T(8,128)(2,1)S(1)}, bf16[896,2560]{1,0:T(8,128)(2,1)S(1)}) custom-call(s32[1]{0:T(128)} %bitcast.me_ref, bf16[4,2048,2560]{2,1,0:T(8,128)(2,1)} %bitcast.12, bf16[4,2048,2560]{2,1,0:T(8,128)(2,1)} %bitcast.13), custom_call_target="tpu_custom_call" | custom-call | bytes 18350080 | tf_op jit(solution)/shard_map/pick/pallas_call | solution.py:53
  12.9 6.2 %pick.3 = (bf16[1024,2560]{1,0:T(8,128)(2,1)S(1)}, bf16[1024,2560]{1,0:T(8,128)(2,1)S(1)}) custom-call(s32[1]{0:T(128)} %bitcast.me_ref, bf16[4,2048,2560]{2,1,0:T(8,128)(2,1)} %bitcast.14, bf16[4,2048,2560]{2,1,0:T(8,128)(2,1)} %bitcast.15), custom_call_target="tpu_custom_call" | custom-call | bytes 20971520 | tf_op jit(solution)/shard_map/pick/pallas_call | solution.py:53
  20.5 2.1 collective-permute-done.1.refs_1_
  22.7 2.0 collective-permute-start.3
  24.7 94.2 %collective-permute-done.4.refs_0_.refs_2_ = bf16[896,2560]{1,0:T(8,128)(2,1)S(1)} collective-permute-done((bf16[896,2560]{1,0:T(8,128)(2,1)S(1)}, bf16[896,2560]{1,0:T(8,128)(2,1)S(1)}, u32[]{:S(2)}, u32[]{:S(2)}) %collective-permute-start.4) | collective-permute-done | bytes 4587552 | tf_op jit(solution)/shard_map/ppermute | solution.py:617
  118.8 2.1 collective-permute-done.5.refs_1_.refs_3_
  120.9 3.3 merge.3
  124.2 1.6 collective-permute-start.6
  126.4 4.6 %merge.4 = (bf16[384,2560]{1,0:T(8,128)(2,1)}, bf16[384,2560]{1,0:T(8,128)(2,1)S(1)}) custom-call(s32[1]{0:T(128)} %bitcast.me_ref, bf16[4,2048,2560]{2,1,0:T(8,128)(2,1)} %bitcast.18, bf16[4,2048,2560]{2,1,0:T(8,128)(2,1)} %bitcast.19, bf16[896,2560]{1,0:T(8,128)(2,1)S(1)} %collective-permute-done.4.refs_0_.refs_2_, ...), custom_call_target="tpu_custom_call" | custom-call | flops 1966080 | bytes 11796480 | tf_op jit(solution)/shard_map/merge/pallas_call | solution.py:123
  130.9 100.2 %collective-permute-done.2.b0 = bf16[1024,2560]{1,0:T(8,128)(2,1)S(1)} collective-permute-done((bf16[1024,2560]{1,0:T(8,128)(2,1)S(1)}, bf16[1024,2560]{1,0:T(8,128)(2,1)S(1)}, u32[]{:S(2)}, u32[]{:S(2)}) %collective-permute-start.2) | collective-permute-done | bytes 5242912 | tf_op jit(solution)/shard_map/ppermute | solution.py:617
  231.2 2.1 collective-permute-done.3.b1
  233.3 1.5 collective-permute-start.10
  235.3 2.9 merge.5
  238.3 37.1 %collective-permute-done.6.c0 = bf16[384,2560]{1,0:T(8,128)(2,1)S(1)} collective-permute-done((bf16[384,2560]{1,0:T(8,128)(2,1)S(1)}, bf16[384,2560]{1,0:T(8,128)(2,1)S(1)}, u32[]{:S(2)}, u32[]{:S(2)}) %collective-permute-start.6) | collective-permute-done | bytes 1966112 | tf_op jit(solution)/shard_map/ppermute | solution.py:617
  275.5 2.0 collective-permute-start.8
  277.5 2.7 presum.1.base_ref
  280.2 5.4 %settle.2 = (bf16[2048,2560]{1,0:T(8,128)(2,1)S(1)}, f32[1,2560]{1,0:T(1,128)S(1)}, f32[1,768]{1,0:T(1,128)S(1)}) custom-call(s32[1]{0:T(128)} %bitcast.me_ref, bf16[4,2048,2560]{2,1,0:T(8,128)(2,1)} %bitcast.24, bf16[4,2048,2560]{2,1,0:T(8,128)(2,1)} %bitcast.25, bf16[1024,2560]{1,0:T(8,128)(2,1)S(1)} %collective-permute-done.2.b0, ...), custom_call_target="tpu_custom_call" | custom-call | flops 11796480 | bytes 11796480 | tf_op jit(solution)/shard_map/settle/pallas_call | solution.py:204
  285.6 7.5 %param_power.1 = (f32[512,2560]{1,0:T(8,128)S(1)}, f32[512,2560]{1,0:T(8,128)S(1)}, f32[512,2560]{1,0:T(8,128)S(1)}, f32[512,2560]{1,0:T(8,128)S(1)}, f32[8,128]{1,0:T(8,128)S(1)}) custom-call(f32[2048,2560]{1,0:T(8,128)} %bitcast.28), custom_call_target="tpu_custom_call" | custom-call | flops 10485760 | bytes 20971520 | tf_op jit(solution)/shard_map/param_power/pallas_call | solution.py:377
  293.1 2.3 copy-done
  295.5 2.4 copy-done.1
  297.8 2.3 copy-done.2
  300.2 17.4 %collective-permute-done.10.c0 = bf16[384,2560]{1,0:T(8,128)(2,1)S(1)} collective-permute-done((bf16[384,2560]{1,0:T(8,128)(2,1)}, bf16[384,2560]{1,0:T(8,128)(2,1)S(1)}, u32[]{:S(2)}, u32[]{:S(2)}) %collective-permute-start.10) | collective-permute-done | bytes 1966112 | tf_op jit(solution)/shard_map/ppermute | solution.py:617
  317.5 5.4 %settle.3 = (bf16[2048,2560]{1,0:T(8,128)(2,1)S(1)}, f32[1,2560]{1,0:T(1,128)S(1)}, f32[1,768]{1,0:T(1,128)S(1)}) custom-call(s32[1]{0:T(128)} %bitcast.me_ref, bf16[4,2048,2560]{2,1,0:T(8,128)(2,1)} %bitcast.26, bf16[4,2048,2560]{2,1,0:T(8,128)(2,1)} %bitcast.27, bf16[1024,2560]{1,0:T(8,128)(2,1)S(1)} %collective-permute-done.2.b0, ...), custom_call_target="tpu_custom_call", output_to_operand_aliasing={{0}: (7, {})} | custom-call | flops 11796480 | bytes 11796480 | tf_op jit(solution)/shard_map/settle/pallas_call | solution.py:204
  323.0 3.7 collective-permute-start.15
  328.5 2.7 collective-permute-done.14.refs_2_
  331.2 3.0 early.1
  334.2 8.6 %collective-permute-done.9.came_ref = bf16[256,2560]{1,0:T(8,128)(2,1)S(1)} collective-permute-done((bf16[256,2560]{1,0:T(8,128)(2,1)}, bf16[256,2560]{1,0:T(8,128)(2,1)S(1)}, u32[]{:S(2)}, u32[]{:S(2)}) %collective-permute-start.9) | collective-permute-done | bytes 1310752 | tf_op jit(solution)/shard_map/ppermute | solution.py:617
  347.1 3.7 collective-permute-start.18
  352.6 2.7 collective-permute-done.17.refs_2_
  356.7 10.8 %finish.1 = (bf16[2048,2560]{1,0:T(8,128)(2,1)S(1)}, f32[512,2560]{1,0:T(8,128)S(1)}, f32[512,2560]{1,0:T(8,128)S(1)}, f32[512,2560]{1,0:T(8,128)S(1)}, f32[512,...) custom-call(bf16[2048,2560]{1,0:T(8,128)(2,1)S(1)} %get-tuple-elemen, ...), custom_call_target="tpu_custom_call", output_to_operand_aliasing={{0}: (0, {}), {1}: (3, {}), {2}: (4, {}), {3}: (5, {}), {4}... | custom-call | flops 31457280 | bytes 62914560 | tf_op jit(solution)/shard_map/finish/pallas_call | solution.py:575
  (53 shorter events, 13.9 us)
Async XLA Ops:
  2.0 18.6 %collective-permute-start = (bf16[128,2560]{1,0:T(8,128)(2,1)S(1)}, bf16[128,2560]{1,0:T(8,128)(2,1)S(1)}, u32[]{:S(2)}, u32[]{:S(2)}) collective-permute-start(bf16[128,2560]{1,0:T(8,128)(2,1)S(1)} %get-tuple-element.64), channel_id=1, source_target_pairs={{0,8},{8,0},{16,24},{24,16},{1,9},{9,1},{17,25},{25,17},{2,10},{10... | collective-permute-start | bytes 1966088 | tf_op jit(solution)/shard_map/ppermute | solution.py:617
  5.0 17.7 %collective-permute-start.1 = (bf16[128,2560]{1,0:T(8,128)(2,1)S(1)}, bf16[128,2560]{1,0:T(8,128)(2,1)S(1)}, u32[]{:S(2)}, u32[]{:S(2)}) collective-permute-start(bf16[128,2560]{1,0:T(8,128)(2,1)S(1)} %get-tuple-element.65), channel_id=1, source_target_pairs={{0,16},{8,24},{16,0},{24,8},{1,17},{9,25},{17,1},{25,9},{2,18},{10... | collective-permute-start | bytes 1966088 | tf_op jit(solution)/shard_map/ppermute | solution.py:617
  12.2 106.6 %collective-permute-start.4 = (bf16[896,2560]{1,0:T(8,128)(2,1)S(1)}, bf16[896,2560]{1,0:T(8,128)(2,1)S(1)}, u32[]{:S(2)}, u32[]{:S(2)}) collective-permute-start(bf16[896,2560]{1,0:T(8,128)(2,1)S(1)} %get-tuple-element.67), channel_id=1, source_target_pairs={{0,8},{8,0},{16,24},{24,16},{1,9},{9,1},{17,25},{25,17},{2,10},{10... | collective-permute-start | bytes 13762568 | tf_op jit(solution)/shard_map/ppermute | solution.py:617
  12.8 108.1 %collective-permute-start.5 = (bf16[896,2560]{1,0:T(8,128)(2,1)S(1)}, bf16[896,2560]{1,0:T(8,128)(2,1)S(1)}, u32[]{:S(2)}, u32[]{:S(2)}) collective-permute-start(bf16[896,2560]{1,0:T(8,128)(2,1)S(1)} %get-tuple-element.68), channel_id=1, source_target_pairs={{0,16},{8,24},{16,0},{24,8},{1,17},{9,25},{17,1},{25,9},{2,18},{10... | collective-permute-start | bytes 13762568 | tf_op jit(solution)/shard_map/ppermute | solution.py:617
  22.6 208.6 %collective-permute-start.2 = (bf16[1024,2560]{1,0:T(8,128)(2,1)S(1)}, bf16[1024,2560]{1,0:T(8,128)(2,1)S(1)}, u32[]{:S(2)}, u32[]{:S(2)}) collective-permute-start(bf16[1024,2560]{1,0:T(8,128)(2,1)S(1)} %get-tuple-element.72), channel_id=1, source_target_pairs={{0,8},{8,0},{16,24},{24,16},{1,9},{9,1},{17,25},{25,17},{2,10},{10... | collective-permute-start | bytes 15728648 | tf_op jit(solution)/shard_map/ppermute | solution.py:617
  22.7 210.6 %collective-permute-start.3 = (bf16[1024,2560]{1,0:T(8,128)(2,1)S(1)}, bf16[1024,2560]{1,0:T(8,128)(2,1)S(1)}, u32[]{:S(2)}, u32[]{:S(2)}) collective-permute-start(bf16[1024,2560]{1,0:T(8,128)(2,1)S(1)} %get-tuple-element.73), channel_id=1, source_target_pairs={{0,16},{8,24},{16,0},{24,8},{1,17},{9,25},{17,1},{25,9},{2,18},{10... | collective-permute-start | bytes 15728648 | tf_op jit(solution)/shard_map/ppermute | solution.py:617
  124.2 151.2 %collective-permute-start.6 = (bf16[384,2560]{1,0:T(8,128)(2,1)S(1)}, bf16[384,2560]{1,0:T(8,128)(2,1)S(1)}, u32[]{:S(2)}, u32[]{:S(2)}) collective-permute-start(bf16[384,2560]{1,0:T(8,128)(2,1)S(1)} %get-tuple-element.88), channel_id=1, source_target_pairs={{0,16},{8,24},{16,0},{24,8},{1,17},{9,25},{17,1},{25,9},{2,18},{10... | collective-permute-start | bytes 5898248 | tf_op jit(solution)/shard_map/ppermute | solution.py:617
  125.8 149.6 %collective-permute-start.7 = (bf16[384,2560]{1,0:T(8,128)(2,1)S(1)}, bf16[384,2560]{1,0:T(8,128)(2,1)S(1)}, u32[]{:S(2)}, u32[]{:S(2)}) collective-permute-start(bf16[384,2560]{1,0:T(8,128)(2,1)S(1)} %get-tuple-element.89), channel_id=1, source_target_pairs={{0,8},{8,0},{16,24},{24,16},{1,9},{9,1},{17,25},{25,17},{2,10},{10... | collective-permute-start | bytes 5898248 | tf_op jit(solution)/shard_map/ppermute | solution.py:617
  233.3 84.3 %collective-permute-start.10 = (bf16[384,2560]{1,0:T(8,128)(2,1)}, bf16[384,2560]{1,0:T(8,128)(2,1)S(1)}, u32[]{:S(2)}, u32[]{:S(2)}) collective-permute-start(bf16[384,2560]{1,0:T(8,128)(2,1)} %get-tuple-element.92), channel_id=1, source_target_pairs={{0,16},{8,24},{16,0},{24,8},{1,17},{9,25},{17,1},{25,9},{2,18},{10... | collective-permute-start | bytes 5898248 | tf_op jit(solution)/shard_map/ppermute | solution.py:617
  234.8 82.7 %collective-permute-start.11 = (bf16[384,2560]{1,0:T(8,128)(2,1)S(1)}, bf16[384,2560]{1,0:T(8,128)(2,1)S(1)}, u32[]{:S(2)}, u32[]{:S(2)}) collective-permute-start(bf16[384,2560]{1,0:T(8,128)(2,1)S(1)} %get-tuple-element.93), channel_id=1, source_target_pairs={{0,8},{8,0},{16,24},{24,16},{1,9},{9,1},{17,25},{25,17},{2,10},{10... | collective-permute-start | bytes 5898248 | tf_op jit(solution)/shard_map/ppermute | solution.py:617
  275.4 67.3 %collective-permute-start.9 = (bf16[256,2560]{1,0:T(8,128)(2,1)}, bf16[256,2560]{1,0:T(8,128)(2,1)S(1)}, u32[]{:S(2)}, u32[]{:S(2)}) collective-permute-start(bf16[256,2560]{1,0:T(8,128)(2,1)} %get-tuple-element.91), channel_id=1, source_target_pairs={{0,8},{8,0},{16,24},{24,16},{1,9},{9,1},{17,25},{25,17},{2,10},{10... | collective-permute-start | bytes 3932168 | tf_op jit(solution)/shard_map/ppermute | solution.py:617
  275.5 68.7 %collective-permute-start.8 = (bf16[256,2560]{1,0:T(8,128)(2,1)S(1)}, bf16[256,2560]{1,0:T(8,128)(2,1)S(1)}, u32[]{:S(2)}, u32[]{:S(2)}) collective-permute-start(bf16[256,2560]{1,0:T(8,128)(2,1)S(1)} %get-tuple-element.90), channel_id=1, source_target_pairs={{0,16},{8,24},{16,0},{24,8},{1,17},{9,25},{17,1},{25,9},{2,18},{10... | collective-permute-start | bytes 3932168 | tf_op jit(solution)/shard_map/ppermute | solution.py:617
  293.1 2.4 copy-start
  295.5 2.4 copy-start.1
  297.8 2.3 copy-start.2
  317.5 13.6 %copy-start.3 = (f32[1,2048]{1,0:T(1,128)S(1)}, f32[1,2048]{1,0:T(1,128)}, u32[]{:S(2)}) copy-start(f32[1,2048]{1,0:T(1,128)} %refs_4_.3) | copy-start | bytes 24580
  323.0 5.5 %collective-permute-start.15 = (f32[1,1536]{1,0:T(1,128)S(1)}, f32[1,1536]{1,0:T(1,128)S(1)}, u32[]{:S(2)}, u32[]{:S(2)}) collective-permute-start(f32[1,1536]{1,0:T(1,128)S(1)} %pad_maximum_fusion.refs_0_), channel_id=1, source_target_pairs={{0,3},{1,2},{2,1},{3,0},{4,7},{5,6},{6,5},{7,4},{8,11},{9,10},{10,... | collective-permute-start | bytes 18440 | tf_op jit(solution)/shard_map/ppermute | solution.py:595
  326.7 4.5 %collective-permute-start.14 = (f32[1,1536]{1,0:T(1,128)S(1)}, f32[1,1536]{1,0:T(1,128)S(1)}, u32[]{:S(2)}, u32[]{:S(2)}) collective-permute-start(f32[1,1536]{1,0:T(1,128)S(1)} %pad_maximum_fusion.refs_0_), channel_id=1, source_target_pairs={{0,2},{1,3},{2,0},{3,1},{4,6},{5,7},{6,4},{7,5},{8,10},{9,11},{10,... | collective-permute-start | bytes 18440 | tf_op jit(solution)/shard_map/ppermute | solution.py:595
  326.7 4.5 %collective-permute-start.13 = (f32[1,1536]{1,0:T(1,128)S(1)}, f32[1,1536]{1,0:T(1,128)S(1)}, u32[]{:S(2)}, u32[]{:S(2)}) collective-permute-start(f32[1,1536]{1,0:T(1,128)S(1)} %pad_maximum_fusion.refs_0_), channel_id=1, source_target_pairs={{0,1},{1,0},{2,3},{3,2},{4,5},{5,4},{6,7},{7,6},{8,9},{9,8},{10,11... | collective-permute-start | bytes 18440 | tf_op jit(solution)/shard_map/ppermute | solution.py:595
  342.7 13.9 %slice-start = ((s8[5242880]{0:T(1024)(128)(4,1)}), s8[4194304]{0:T(1024)(128)(4,1)S(1)}, s32[]{:S(2)}) async-start(s8[5242880]{0:T(1024)(128)(4,1)} %bitcast.5), calls=%async_computation | async-start | bytes 8388608
  342.7 13.9 %slice-start.2 = ((s8[5242880]{0:T(1024)(128)(4,1)}), s8[4194304]{0:T(1024)(128)(4,1)S(1)}, s32[]{:S(2)}) async-start(s8[5242880]{0:T(1024)(128)(4,1)} %bitcast.7), calls=%async_computation.2 | async-start | bytes 8388608
  342.7 13.9 %slice-start.4 = ((s8[5242880]{0:T(1024)(128)(4,1)}), s8[4194304]{0:T(1024)(128)(4,1)S(1)}, s32[]{:S(2)}) async-start(s8[5242880]{0:T(1024)(128)(4,1)} %bitcast.9), calls=%async_computation.4 | async-start | bytes 8388608
  344.2 2.0 copy-start.4
  344.2 12.5 %slice-start.1 = ((s8[5242880]{0:T(1024)(128)(4,1)}), s8[1048576]{0:T(1024)(128)(4,1)S(1)}, s32[]{:S(2)}) async-start(s8[5242880]{0:T(1024)(128)(4,1)} %bitcast.5), calls=%async_computation.1 | async-start | bytes 2097152
  344.2 12.5 %slice-start.3 = ((s8[5242880]{0:T(1024)(128)(4,1)}), s8[1048576]{0:T(1024)(128)(4,1)S(1)}, s32[]{:S(2)}) async-start(s8[5242880]{0:T(1024)(128)(4,1)} %bitcast.7), calls=%async_computation.3 | async-start | bytes 2097152
  344.2 12.5 %slice-start.5 = ((s8[5242880]{0:T(1024)(128)(4,1)}), s8[1048576]{0:T(1024)(128)(4,1)S(1)}, s32[]{:S(2)}) async-start(s8[5242880]{0:T(1024)(128)(4,1)} %bitcast.9), calls=%async_computation.5 | async-start | bytes 2097152
  344.9 1.2 collective-permute-start.12
  347.1 5.5 %collective-permute-start.18 = (f32[1,1280]{1,0:T(1,128)S(1)}, f32[1,1280]{1,0:T(1,128)S(1)}, u32[]{:S(2)}, u32[]{:S(2)}) collective-permute-start(f32[1,1280]{1,0:T(1,128)S(1)} %get-tuple-element.115.refs_0_), channel_id=1, source_target_pairs={{0,3},{1,2},{2,1},{3,0},{4,7},{5,6},{6,5},{7,4},{8,11},{9,10},{10,... | collective-permute-start | bytes 15368 | tf_op jit(solution)/shard_map/ppermute | solution.py:595
  350.8 4.5 %collective-permute-start.17 = (f32[1,1280]{1,0:T(1,128)S(1)}, f32[1,1280]{1,0:T(1,128)S(1)}, u32[]{:S(2)}, u32[]{:S(2)}) collective-permute-start(f32[1,1280]{1,0:T(1,128)S(1)} %get-tuple-element.115.refs_0_), channel_id=1, source_target_pairs={{0,2},{1,3},{2,0},{3,1},{4,6},{5,7},{6,4},{7,5},{8,10},{9,11},{10,... | collective-permute-start | bytes 15368 | tf_op jit(solution)/shard_map/ppermute | solution.py:595
  350.8 4.5 %collective-permute-start.16 = (f32[1,1280]{1,0:T(1,128)S(1)}, f32[1,1280]{1,0:T(1,128)S(1)}, u32[]{:S(2)}, u32[]{:S(2)}) collective-permute-start(f32[1,1280]{1,0:T(1,128)S(1)} %get-tuple-element.115.refs_0_), channel_id=1, source_target_pairs={{0,1},{1,0},{2,3},{3,2},{4,5},{5,4},{6,7},{7,6},{8,9},{9,8},{10,11... | collective-permute-start | bytes 15368 | tf_op jit(solution)/shard_map/ppermute | solution.py:595
  355.4 1.3 collective-permute-start.19
